TPU v7x, 32 devices: a whole 2x2x4 slice. The times are simulated.
32 devices in a mesh: pack: 2 (over core), cp: 4 (over z), hd: 4 (over y, x).
Axes of the slice: x: 2, y: 2, z: 4, core: 2. Of those that a mesh axis runs over, the one named last changes fastest.
Arguments:
- inputs: bfloat16 [16384, 1024], P(('pack', 'cp', 'hd')), may hold values from -6 to 6
- cotangent: bfloat16 [16384, 1024], P(('pack', 'cp', 'hd')), may hold values from -6 to 6
- w_qkv: bfloat16 [1024, 3072], P(('pack', 'cp', 'hd')), may hold values from -0.1875 to 0.1875
- w_out: bfloat16 [1024, 1024], P(('pack', 'cp', 'hd')), may hold values from -0.75 to 0.75
- w_gate: bfloat16 [1024, 4096], P(('pack', 'cp', 'hd')), may hold values from -0.1875 to 0.1875
- w_up: bfloat16 [1024, 4096], P(('pack', 'cp', 'hd')), may hold values from -0.1875 to 0.1875
- w_down: bfloat16 [4096, 1024], P(('pack', 'cp', 'hd')), may hold values from -0.09375 to 0.09375
- gain_attn: bfloat16 [1024], P(('pack', 'cp', 'hd')), may hold values from 0.099609375 to 1.8984375
- gain_ffn: bfloat16 [1024], P(('pack', 'cp', 'hd')), may hold values from 0.099609375 to 1.8984375
- q_gain: float32 [64], replicated, may hold values from 0.1 to 1.9
- k_gain: float32 [64], replicated, may hold values from 0.1 to 1.9
- head_bias: float32 [16, 2], replicated, may hold values from -4 to 4
- segment_ids: int32 [16384], P(('pack', 'cp')), may hold values from 0 to 3, as said below
- variate_ids: int32 [16384], P(('pack', 'cp')), may hold values from 0 to 3
- time_index: int32 [16384], P(('pack', 'cp')), may hold values from 0 to 1023
Outputs:
- layer_out: bfloat16 [16384, 1024], P(('pack', 'cp', 'hd'))
- grad_inputs: float32 [16384, 1024], P(('pack', 'cp', 'hd'))
- grad_qkv: float32 [1024, 3072], P(('pack', 'cp', 'hd'))
- grad_out: float32 [1024, 1024], P(('pack', 'cp', 'hd'))
- grad_gate: float32 [1024, 4096], P(('pack', 'cp', 'hd'))
- grad_up: float32 [1024, 4096], P(('pack', 'cp', 'hd'))
- grad_down: float32 [4096, 1024], P(('pack', 'cp', 'hd'))
- grad_gain_attn: float32 [1024], P(('pack', 'cp', 'hd'))
- grad_gain_ffn: float32 [1024], P(('pack', 'cp', 'hd'))
- grad_q_gain: float32 [64], replicated
- grad_k_gain: float32 [64], replicated
- grad_bias: float32 [16, 2], replicated
Inputs may be any that keep to these rules, and one draw needn't show every extreme that they name: `segment_ids`: within each of the 2 packs of 8192 tokens the ids start at 0 and never fall; a pack holds at most four documents.
All inputs are finite; a program needn't handle non-finite values.
Results may differ from a plain program's by a relative error of at most 0.015.
The roundings to bfloat16 on the way count: a program that leaves them out, or rounds other values in their place, can miss the bound.
Values may be sent and summed in bfloat16 or wider, within the bound.
A program may use at most 192 MiB of HBM per device.

v0:
```python
import math

import jax
import jax.numpy as jnp
from jax import lax
from jax.sharding import PartitionSpec as P

HEADS = 16
HDIM = 64
HALF = 512


eps_norm = 1e-06
theta_base = 10000.0
masked_score = -1e30


def extended_2(cells, sides, width):
    for axis, dim in sides:
        count = lax.axis_size(axis)
        ends = count - 1
        head = lax.slice_in_dim(cells, 0, width, axis=dim)
        tail = lax.slice_in_dim(cells, cells.shape[dim] - width, cells.shape[dim], axis=dim)
        cells = jnp.concatenate(
            [
                lax.ppermute(tail, axis, [(i, (i + 1) % count) for i in range(ends)]),
                cells,
                lax.ppermute(head, axis, [((i + 1) % count, i) for i in range(ends)]),
            ],
            axis=dim,
        )
    return cells


def shifted(value, axis, steps):
    count = lax.axis_size(axis)
    leading, last = (max(0, -steps), min(count, count - steps))
    return lax.ppermute(value, axis, [(source, source + steps) for source in range(leading, last)])


def rotate(values, cosine, rot_sine):
    half_dim = values.shape[-1] // 2
    front_half = values[..., :half_dim]
    back_half = values[..., half_dim:]
    return jnp.concatenate(
        [front_half * cosine - back_half * rot_sine, back_half * cosine + front_half * rot_sine],
        axis=-1,
    )


def rms_scale(values):
    return lax.rsqrt(jnp.mean(values * values, axis=-1, keepdims=True) + eps_norm)


def norm_back(values, inv_rms, gain_vec, grad_in):
    scaled = grad_in * gain_vec
    d_values = inv_rms * scaled - values * inv_rms**3 * jnp.mean(
        scaled * values, axis=-1, keepdims=True
    )
    return (d_values, grad_in * values * inv_rms)


def contract_rows(left_mat, right_mat):
    return lax.dot_general(
        left_mat, right_mat, (((0,), (0,)), ((), ())), preferred_element_type=jnp.float32
    )


def contract_cols(left_mat, right_mat):
    return lax.dot_general(
        left_mat, right_mat, (((1,), (1,)), ((), ())), preferred_element_type=jnp.float32
    )


def local(
    inputs,
    cotangent,
    w_qkv,
    w_out,
    w_gate,
    w_up,
    w_down,
    gain_attn,
    gain_ffn,
    q_gain,
    k_gain,
    head_bias,
    segment_ids,
    variate_ids,
    time_index,
):
    gathered = (
        lax.all_gather(w_qkv, ("pack", "cp", "hd"), axis=0, tiled=True),
        lax.all_gather(w_out, ("pack", "cp", "hd"), axis=0, tiled=True),
        lax.all_gather(w_gate, ("pack", "cp", "hd"), axis=0, tiled=True),
        lax.all_gather(w_up, ("pack", "cp", "hd"), axis=0, tiled=True),
        lax.all_gather(w_down, ("pack", "cp", "hd"), axis=0, tiled=True),
        lax.all_gather(gain_attn, ("pack", "cp", "hd"), axis=0, tiled=True),
        lax.all_gather(gain_ffn, ("pack", "cp", "hd"), axis=0, tiled=True),
    )
    full_qkv, full_out, full_gate, full_up, full_down, full_gattn, full_gffn = gathered
    tok_rows = inputs.shape[0]
    model_width = inputs.shape[1]
    hd_count = lax.axis_size("hd")
    local_width = model_width // hd_count
    local_heads = local_width // HDIM
    group_rows = tok_rows * hd_count
    qblock = min(512, group_rows)
    key_span = qblock + 2 * HALF
    score_scale = 1.0 / math.sqrt(HDIM)
    residual = inputs.astype(jnp.float32)
    rms_attn = rms_scale(residual)
    normed = (residual * rms_attn * full_gattn.astype(jnp.float32)).astype(jnp.bfloat16)
    projected = jnp.dot(normed, full_qkv, preferred_element_type=jnp.float32).astype(jnp.bfloat16)
    head_q, head_k, head_v = (
        lax.all_to_all(projected[:, :model_width], "hd", split_axis=1, concat_axis=0, tiled=True),
        lax.all_to_all(
            projected[:, model_width : 2 * model_width],
            "hd",
            split_axis=1,
            concat_axis=0,
            tiled=True,
        ),
        lax.all_to_all(
            projected[:, 2 * model_width :], "hd", split_axis=1, concat_axis=0, tiled=True
        ),
    )
    q_raw = head_q.astype(jnp.float32).reshape(group_rows, local_heads, HDIM)
    k_raw = head_k.astype(jnp.float32).reshape(group_rows, local_heads, HDIM)
    frequency = jnp.exp(
        -math.log(theta_base) * 2.0 * jnp.arange(HDIM // 2, dtype=jnp.float32) / HDIM
    )
    rot_angle = time_index.astype(jnp.float32)[:, None] * frequency[None, :]
    cosine = jnp.cos(rot_angle)[:, None, :]
    rot_sine = jnp.sin(rot_angle)[:, None, :]
    rms_query = rms_scale(q_raw)
    rms_key = rms_scale(k_raw)
    q_rot = rotate(q_raw * rms_query * q_gain, cosine, rot_sine).astype(jnp.bfloat16)
    k_rot = rotate(k_raw * rms_key * k_gain, cosine, rot_sine).astype(jnp.bfloat16)
    stacked = jnp.stack([k_rot.reshape(group_rows, local_width), head_v])
    extended = extended_2(stacked, (("cp", 1),), HALF)
    k_ext = extended[0].reshape(group_rows + 2 * HALF, local_heads, HDIM)
    v_ext = extended[1].reshape(group_rows + 2 * HALF, local_heads, HDIM)
    id_pair = jnp.stack([segment_ids + 1, variate_ids])
    id_ext = extended_2(id_pair, (("cp", 1),), HALF)
    head_index = lax.axis_index("hd")
    bias_local = lax.dynamic_slice_in_dim(head_bias, head_index * local_heads, local_heads, 0)
    offsets_grid = jnp.arange(qblock)[:, None] + HALF - jnp.arange(key_span)[None, :]
    within = jnp.abs(offsets_grid) <= HALF

    def block_scores(begin_row):
        q_blk = lax.dynamic_slice_in_dim(q_rot, begin_row, qblock, 0)
        k_blk = lax.dynamic_slice_in_dim(k_ext, begin_row, key_span, 0)
        v_blk = lax.dynamic_slice_in_dim(v_ext, begin_row, key_span, 0)
        seg_q = lax.dynamic_slice_in_dim(id_ext[0], begin_row + HALF, qblock, 0)
        seg_k = lax.dynamic_slice_in_dim(id_ext[0], begin_row, key_span, 0)
        var_q = lax.dynamic_slice_in_dim(id_ext[1], begin_row + HALF, qblock, 0)
        var_k = lax.dynamic_slice_in_dim(id_ext[1], begin_row, key_span, 0)
        same_var = var_q[:, None] == var_k[None, :]
        scores = (
            jnp.einsum("qhd,khd->hqk", q_blk, k_blk, preferred_element_type=jnp.float32)
            * score_scale
        )
        scores = scores + jnp.where(
            same_var[None], bias_local[:, 0][:, None, None], bias_local[:, 1][:, None, None]
        )
        allowed = (seg_q[:, None] == seg_k[None, :]) & within
        scores = jnp.where(allowed[None], scores, masked_score)
        return (scores, same_var, q_blk, k_blk, v_blk)

    def forward_block(begin_row):
        scores, same_var, q_blk, k_blk, v_blk = block_scores(begin_row)
        top_val = jnp.max(scores, axis=-1, keepdims=True)
        exp_scores = jnp.exp(scores - top_val)
        row_total = jnp.sum(exp_scores, axis=-1, keepdims=True)
        attn_probs = exp_scores / row_total
        mixed_blk = jnp.einsum(
            "hqk,khd->qhd",
            attn_probs.astype(jnp.bfloat16),
            v_blk,
            preferred_element_type=jnp.float32,
        )
        return (mixed_blk.reshape(qblock, local_width), (top_val + jnp.log(row_total))[..., 0])

    starts = jnp.arange(group_rows // qblock, dtype=jnp.int32) * qblock
    mixed_blocks, lse_blocks = lax.map(forward_block, starts)
    heads_out = mixed_blocks.reshape(group_rows, local_width).astype(jnp.bfloat16)
    token_out = lax.all_to_all(heads_out, "hd", split_axis=0, concat_axis=1, tiled=True)
    hidden = residual + jnp.dot(token_out, full_out, preferred_element_type=jnp.float32)
    rms_ffn = rms_scale(hidden)
    normed_ffn = (hidden * rms_ffn * full_gffn.astype(jnp.float32)).astype(jnp.bfloat16)
    gate_pre = jnp.dot(normed_ffn, full_gate, preferred_element_type=jnp.float32)
    up_pre = jnp.dot(normed_ffn, full_up, preferred_element_type=jnp.float32)
    sigmoid_gate = jax.nn.sigmoid(gate_pre)
    silu_gate = gate_pre * sigmoid_gate
    product = (silu_gate * up_pre).astype(jnp.bfloat16)
    layer_out = (hidden + jnp.dot(product, full_down, preferred_element_type=jnp.float32)).astype(
        jnp.bfloat16
    )
    back_set = (
        lax.all_gather(w_qkv, ("pack", "cp", "hd"), axis=0, tiled=True),
        lax.all_gather(w_out, ("pack", "cp", "hd"), axis=0, tiled=True),
        lax.all_gather(w_gate, ("pack", "cp", "hd"), axis=0, tiled=True),
        lax.all_gather(w_up, ("pack", "cp", "hd"), axis=0, tiled=True),
        lax.all_gather(w_down, ("pack", "cp", "hd"), axis=0, tiled=True),
        lax.all_gather(gain_attn, ("pack", "cp", "hd"), axis=0, tiled=True),
        lax.all_gather(gain_ffn, ("pack", "cp", "hd"), axis=0, tiled=True),
    )
    back_qkv, back_out, back_gate, back_up, back_down, back_gattn, back_gffn = back_set
    grad_down = contract_rows(product, cotangent)
    d_product = contract_cols(cotangent, back_down)
    d_gate = (d_product * up_pre * sigmoid_gate * (1.0 + gate_pre * (1.0 - sigmoid_gate))).astype(
        jnp.bfloat16
    )
    d_up = (d_product * silu_gate).astype(jnp.bfloat16)
    grad_gate = contract_rows(normed_ffn, d_gate)
    grad_up = contract_rows(normed_ffn, d_up)
    d_normed_ffn = contract_cols(d_gate, back_gate) + contract_cols(d_up, back_up)
    d_hidden_norm, gffn_terms = norm_back(
        hidden, rms_ffn, back_gffn.astype(jnp.float32), d_normed_ffn
    )
    d_hidden = cotangent.astype(jnp.float32) + d_hidden_norm
    d_attn = d_hidden.astype(jnp.bfloat16)
    grad_out = contract_rows(token_out, d_attn)
    d_token_out = contract_cols(d_attn, back_out).astype(jnp.bfloat16)
    d_heads = lax.all_to_all(d_token_out, "hd", split_axis=1, concat_axis=0, tiled=True)
    d_heads3 = d_heads.reshape(group_rows, local_heads, HDIM)

    def backward_block(carried, block_inputs):
        dk_ext, dv_ext, bias_grad = carried
        begin_row, lse_row = block_inputs
        scores, same_var, q_blk, k_blk, v_blk = block_scores(begin_row)
        attn_probs = jnp.exp(scores - lse_row[..., None])
        do_blk = lax.dynamic_slice_in_dim(d_heads3, begin_row, qblock, 0)
        d_probs = jnp.einsum("qhd,khd->hqk", do_blk, v_blk, preferred_element_type=jnp.float32)
        delta_row = jnp.sum(attn_probs * d_probs, axis=-1, keepdims=True)
        d_scores = (attn_probs * (d_probs - delta_row)).astype(jnp.bfloat16)
        d_wide = d_scores.astype(jnp.float32)
        same_total = jnp.sum(jnp.where(same_var[None], d_wide, 0.0), axis=(1, 2))
        every_total = jnp.sum(d_wide, axis=(1, 2))
        bias_grad = bias_grad + jnp.stack([same_total, every_total - same_total], axis=1)
        dv_blk = jnp.einsum(
            "hqk,qhd->khd",
            attn_probs.astype(jnp.bfloat16),
            do_blk,
            preferred_element_type=jnp.float32,
        )
        dq_blk = (
            jnp.einsum("hqk,khd->qhd", d_scores, k_blk, preferred_element_type=jnp.float32)
            * score_scale
        )
        dk_blk = (
            jnp.einsum("hqk,qhd->khd", d_scores, q_blk, preferred_element_type=jnp.float32)
            * score_scale
        )
        dk_ext = lax.dynamic_update_slice_in_dim(
            dk_ext, lax.dynamic_slice_in_dim(dk_ext, begin_row, key_span, 0) + dk_blk, begin_row, 0
        )
        dv_ext = lax.dynamic_update_slice_in_dim(
            dv_ext, lax.dynamic_slice_in_dim(dv_ext, begin_row, key_span, 0) + dv_blk, begin_row, 0
        )
        return ((dk_ext, dv_ext, bias_grad), dq_blk)

    zero_ext = jnp.zeros((group_rows + 2 * HALF, local_heads, HDIM), jnp.float32)
    init_state = (zero_ext, zero_ext, jnp.zeros((local_heads, 2), jnp.float32))
    (dk_ext, dv_ext, bias_grad), dq_blocks = lax.scan(
        backward_block, init_state, (starts, lse_blocks)
    )
    dk_flat = dk_ext.reshape(group_rows + 2 * HALF, local_width)
    dv_flat = dv_ext.reshape(group_rows + 2 * HALF, local_width)
    rims_low = jnp.stack([dk_flat[:HALF], dv_flat[:HALF]])
    rims_high = jnp.stack([dk_flat[HALF + group_rows :], dv_flat[HALF + group_rows :]])
    from_above = shifted(rims_low.astype(jnp.bfloat16), "cp", -1).astype(rims_low.dtype)
    from_below = shifted(rims_high.astype(jnp.bfloat16), "cp", 1).astype(rims_high.dtype)
    tail_rows = group_rows - HALF
    dk_own = (
        dk_flat[HALF : HALF + group_rows]
        + jnp.pad(from_below[0], ((0, tail_rows), (0, 0)))
        + jnp.pad(from_above[0], ((tail_rows, 0), (0, 0)))
    )
    dv_own = (
        dv_flat[HALF : HALF + group_rows]
        + jnp.pad(from_below[1], ((0, tail_rows), (0, 0)))
        + jnp.pad(from_above[1], ((tail_rows, 0), (0, 0)))
    )
    dq_rot = dq_blocks.reshape(group_rows, local_heads, HDIM)
    dk_rot = dk_own.reshape(group_rows, local_heads, HDIM)
    dq_raw, qgain_terms = norm_back(q_raw, rms_query, q_gain, rotate(dq_rot, cosine, -rot_sine))
    dk_raw, kgain_terms = norm_back(k_raw, rms_key, k_gain, rotate(dk_rot, cosine, -rot_sine))
    grad_query = dq_raw.reshape(group_rows, local_width).astype(jnp.bfloat16)
    grad_key = dk_raw.reshape(group_rows, local_width).astype(jnp.bfloat16)
    back_q, back_k, back_v = (
        lax.all_to_all(grad_query, "hd", split_axis=0, concat_axis=1, tiled=True),
        lax.all_to_all(grad_key, "hd", split_axis=0, concat_axis=1, tiled=True),
        lax.all_to_all(dv_own.astype(jnp.bfloat16), "hd", split_axis=0, concat_axis=1, tiled=True),
    )
    d_projected = jnp.concatenate([back_q, back_k, back_v], axis=1)
    grad_qkv = contract_rows(normed, d_projected)
    d_normed = contract_cols(d_projected, back_qkv)
    d_resid_norm, gattn_terms = norm_back(
        residual, rms_attn, back_gattn.astype(jnp.float32), d_normed
    )
    grad_inputs = d_hidden + d_resid_norm
    summed = (
        lax.psum_scatter(grad_qkv, ("pack", "cp", "hd"), scatter_dimension=0, tiled=True),
        lax.psum_scatter(grad_out, ("pack", "cp", "hd"), scatter_dimension=0, tiled=True),
        lax.psum_scatter(grad_gate, ("pack", "cp", "hd"), scatter_dimension=0, tiled=True),
        lax.psum_scatter(grad_up, ("pack", "cp", "hd"), scatter_dimension=0, tiled=True),
        lax.psum_scatter(grad_down, ("pack", "cp", "hd"), scatter_dimension=0, tiled=True),
        lax.psum_scatter(
            jnp.sum(gattn_terms, axis=0), ("pack", "cp", "hd"), scatter_dimension=0, tiled=True
        ),
        lax.psum_scatter(
            jnp.sum(gffn_terms, axis=0), ("pack", "cp", "hd"), scatter_dimension=0, tiled=True
        ),
    )
    bias_full = lax.dynamic_update_slice_in_dim(
        jnp.zeros((HEADS, 2), jnp.float32), bias_grad, head_index * local_heads, 0
    )
    small_sums = lax.psum(
        (jnp.sum(qgain_terms, axis=(0, 1)), jnp.sum(kgain_terms, axis=(0, 1)), bias_full),
        ("pack", "cp", "hd"),
    )
    return (
        layer_out,
        grad_inputs,
        summed[0],
        summed[1],
        summed[2],
        summed[3],
        summed[4],
        summed[5],
        summed[6],
        small_sums[0],
        small_sums[1],
        small_sums[2],
    )


def solution(mesh):
    return jax.shard_map(
        local,
        mesh=mesh,
        in_specs=(
            P(("pack", "cp", "hd"), None),
            P(("pack", "cp", "hd"), None),
            P(("pack", "cp", "hd"), None),
            P(("pack", "cp", "hd"), None),
            P(("pack", "cp", "hd"), None),
            P(("pack", "cp", "hd"), None),
            P(("pack", "cp", "hd"), None),
            P(("pack", "cp", "hd")),
            P(("pack", "cp", "hd")),
            P(),
            P(),
            P(),
            P(("pack", "cp")),
            P(("pack", "cp")),
            P(("pack", "cp")),
        ),
        out_specs=(
            P(("pack", "cp", "hd"), None),
            P(("pack", "cp", "hd"), None),
            P(("pack", "cp", "hd"), None),
            P(("pack", "cp", "hd"), None),
            P(("pack", "cp", "hd"), None),
            P(("pack", "cp", "hd"), None),
            P(("pack", "cp", "hd"), None),
            P(("pack", "cp", "hd")),
            P(("pack", "cp", "hd")),
            P(),
            P(),
            P(),
        ),
        check_vma=False,
    )
```

profile of v0, /device:TPU:0, one launch (start us, length us, event | category | flops | bytes accessed | tf_op | source)
XLA Modules:
  0.0 2128.2 jit_solution(17712308021514468462)
XLA Ops:
  11.7 42.4 %all-reduce.9 = (bf16[1024]{0:T(1024)(128)(2,1)S(1)}, bf16[1024]{0:T(1024)(128)(2,1)}) all-reduce(bf16[1024]{0:T(1024)(128)(2,1)S(1)} %dynamic-update-slice, bf16[1024]{0:T(1024)(128)(2,1)S(1)} %dynamic-update-slice.1), channel_id=1, replica_groups=mesh['pack'=2,'cp'=4,'hd'=4] {'pack','cp','hd'}, use_global_device_ids=true, to_apply=%add.4 | all-reduce | flops 2048 | bytes 8192
  56.1 27.2 %all-gather.6.cloned.1.call-done = bf16[1024,3072]{1,0:T(8,128)(2,1)} async-done(((bf16[32,3072]{1,0:T(8,128)(2,1)}), bf16[1024,3072]{1,0:T(8,128)(2,1)}) %all-gather.6.cloned.1.call-update) | async-done | bytes 6291472 | tf_op jit(solution)/shard_map/all_gather | solution.py:93
  116.8 9.7 all-to-all-done.1
  167.4 16.4 collective-permute-done.1
  186.5 76.3 %while.34 = (s32[]{:T(128)}, bf16[4,512,256]{1,2,0:T(8,128)(2,1)}, f32[4,4,512]{2,1,0:T(4,128)S(1)}, s32[4]{0:T(128)S(1)}, bf16[3072,4,64]{0,2,1:T(8,128)(2,1)S(...) while((s32[]{:T(128)}, bf16[4,512,256]{1,2,0:T(8,128)(2,1)}, ...), condition=%wide.region_6.7_spmd.clone, body=%wide.region_3.6_spmd.clone.sunk | while | flops 841480192 | bytes 43682188 | solution.py:186
  266.8 13.3 all-to-all-done.3
  286.0 11.6 fusion.68
  297.6 10.3 all-gather.12.cloned.1.call-done
  307.9 11.5 fusion.69
  319.4 66.5 %all-gather.14.cloned.1.call-done = bf16[4096,1024]{1,0:T(8,128)(2,1)} async-done(((bf16[128,1024]{1,0:T(8,128)(2,1)}), bf16[4096,1024]{1,0:T(8,128)(2,1)}) %all-gather.14.cloned.1.call-update) | async-done | bytes 8388624 | tf_op jit(solution)/shard_map/all_gather | solution.py:97
  385.9 16.3 multiply_convert_fusion.1
  432.1 11.3 all-to-all-done.4
  451.0 293.8 %while.35 = (s32[]{:T(128)}, f32[3072,4,64]{0,2,1:T(8,128)}, f32[3072,4,64]{0,2,1:T(8,128)}, f32[4,2]{0,1:T(2,128)S(1)}, f32[4,512,4,64]{1,0,3,2:T(4,128)}, /*in...) while((s32[]{:T(128)}, f32[3072,4,64]{0,2,1:T(8,128)}, ...), condition=%wide.region_13.14_spmd.clone, body=%wide.region_9.13_spmd.clone.sunk | while | flops 2066479104 | bytes 165293776 | solution.py:266
  482.1 10.0 dynamic_update_slice.51
  498.5 10.0 dynamic_update_slice.52
  514.3 11.1 dynamic_update_slice.53
  556.2 9.8 dynamic_update_slice.51
  572.5 9.8 dynamic_update_slice.52
  587.9 11.1 dynamic_update_slice.53
  661.2 11.1 dynamic_update_slice.53
  733.4 11.1 dynamic_update_slice.53
  861.2 9.9 all-to-all-done.5
  871.0 9.9 fusion.51
  882.2 10.9 fusion.71
  893.2 11.1 fusion.72
  905.6 11.4 fusion.73
  918.7 10.8 add_convert_fusion
  938.8 41.9 %all-reduce.8 = (f32[1024]{0:T(1024)S(1)}, f32[1024]{0:T(1024)S(1)}, f32[64]{0:T(128)}, f32[64]{0:T(128)}, f32[16,2]{0,1:T(2,128)}) all-reduce(f32[1024]{0:T(1024)S(1)} %get-tuple-element.433, f32[1024]{0:T(1024)S(1)} %copy-done.56, f32[64]{0:T(128)S(1)} %reduce_sum.184, ...), channel_id=7, replica_groups=mesh['pack'=2,'cp'=4,'hd'=4] {'pack','cp','hd'}, use_global_device_ids=true, to_apply=%region_23.24.clone | all-reduce | flops 2208 | bytes 17664
  985.5 50.2 %reduce-scatter.6.cloned.1.call-done = f32[32,3072]{1,0:T(8,128)} async-done(((f32[1024,3072]{1,0:T(8,128)}), f32[32,3072]{1,0:T(8,128)}) %reduce-scatter.6.cloned.1.call-update) | async-done | bytes 393232 | tf_op jit(solution)/shard_map/reduce_scatter | solution.py:305
  1035.6 359.5 %reduce-scatter.10.cloned.1.call-done = f32[32,4096]{1,0:T(8,128)} async-done(((f32[1024,4096]{1,0:T(8,128)}), f32[32,4096]{1,0:T(8,128)}) %reduce-scatter.10.cloned.1.call-update) | async-done | bytes 524304 | tf_op jit(solution)/shard_map/reduce_scatter | solution.py:307
  1395.1 363.0 %reduce-scatter.12.cloned.1.call-done = f32[32,4096]{1,0:T(8,128)} async-done(((f32[1024,4096]{1,0:T(8,128)}), f32[32,4096]{1,0:T(8,128)}) %reduce-scatter.12.cloned.1.call-update) | async-done | bytes 524304 | tf_op jit(solution)/shard_map/reduce_scatter | solution.py:308
  1758.1 362.9 %reduce-scatter.14.cloned.1.call-done = f32[128,1024]{1,0:T(8,128)} async-done(((f32[4096,1024]{1,0:T(8,128)}), f32[128,1024]{1,0:T(8,128)}) %reduce-scatter.14.cloned.1.call-update) | async-done | bytes 524304 | tf_op jit(solution)/shard_map/reduce_scatter | solution.py:309
  (429 shorter events, 513.2 us)
Async XLA Ops:
  7.2 105.8 %copy-start = (f32[16,2]{0,1:T(2,128)S(1)}, f32[16,2]{0,1:T(2,128)}, u32[]{:S(2)}) copy-start(f32[16,2]{0,1:T(2,128)} %param.30) | copy-start | bytes 388
  7.2 76.1 %all-gather.6.cloned.1.call-start = ((), (), s32[]{:S(2)}) async-start(), calls=%async_computation.13 | async-start | bytes 6488064 | tf_op jit(solution)/shard_map/all_gather | solution.py:93
  7.9 258.9 %all-gather.8.cloned.1.call-start = ((), (), s32[]{:S(2)}) async-start(), calls=%async_computation.14 | async-start | bytes 2162688 | tf_op jit(solution)/shard_map/all_gather | solution.py:94
  8.7 277.4 %all-gather.10.cloned.1.call-start = ((), (), s32[]{:S(2)}) async-start(), calls=%async_computation.15 | async-start | bytes 8650752 | tf_op jit(solution)/shard_map/all_gather | solution.py:95
  9.4 298.5 %all-gather.12.cloned.1.call-start = ((), (), s32[]{:S(2)}) async-start(), calls=%async_computation.16 | async-start | bytes 8650752 | tf_op jit(solution)/shard_map/all_gather | solution.py:96
  54.0 29.2 %copy-start.45 = (f32[1024]{0:T(1024)}, f32[1024]{0:T(1024)S(1)}, u32[]{:S(2)}) copy-start(f32[1024]{0:T(1024)S(1)} %convert_element_type.142) | copy-start | bytes 12292
  56.1 27.2 %copy-start.48 = (f32[512]{0:T(512)}, f32[512]{0:T(512)S(1)}, u32[]{:S(2)}) copy-start(f32[512]{0:T(512)S(1)} %get-tuple-element.559) | copy-start | bytes 6148
  91.6 17.8 all-to-all-start.2
  95.2 290.7 %all-gather.14.cloned.1.call-start = ((), (), s32[]{:S(2)}) async-start(), calls=%async_computation.17 | async-start | bytes 8650752 | tf_op jit(solution)/shard_map/all_gather | solution.py:97
  95.3 71.0 %collective-permute-start.3 = (s32[2,512]{1,0:T(2,128)S(1)}, s32[2,512]{1,0:T(2,128)S(1)}, u32[]{:S(2)}, u32[]{:S(2)}) collective-permute-start(s32[2,512]{1,0:T(2,128)S(1)} %get-tuple-element.554), channel_id=1, source_target_pairs={{4,0},{8,4},{12,8},{5,1},{9,5},{13,9},{6,2},{10,6},{14,10},{7,3},{... | collective-permute-start | bytes 12296 | tf_op jit(solution)/shard_map/ppermute | solution.py:28
  96.6 69.7 %collective-permute-start.2 = (s32[2,512]{1,0:T(2,128)S(1)}, s32[2,512]{1,0:T(2,128)S(1)}, u32[]{:S(2)}, u32[]{:S(2)}) collective-permute-start(s32[2,512]{1,0:T(2,128)S(1)} %get-tuple-element.553), channel_id=1, source_target_pairs={{0,4},{4,8},{8,12},{1,5},{5,9},{9,13},{2,6},{6,10},{10,14},{3,7},{... | collective-permute-start | bytes 12296 | tf_op jit(solution)/shard_map/ppermute | solution.py:26
  109.5 17.0 all-to-all-start.1
  114.9 44.2 %copy-start.27 = (f32[2048,32]{0,1:T(8,128)}, f32[2048,32]{0,1:T(8,128)S(1)}, u32[]{:S(2)}) copy-start(f32[2048,32]{0,1:T(8,128)S(1)} %get-tuple-element.557) | copy-start | bytes 786436
  126.5 17.4 all-to-all-start
  160.1 23.7 %collective-permute-start.1 = (bf16[2,512,256]{1,2,0:T(8,128)(2,1)S(1)}, bf16[2,512,256]{1,2,0:T(8,128)(2,1)S(1)}, u32[]{:S(2)}, u32[]{:S(2)}) collective-permute-start(bf16[2,512,256]{1,2,0:T(8,128)(2,1)S(1)} %get-tuple-element.536), channel_id=1, source_target_pairs={{4,0},{8,4},{12,8},{5,1},{9,5},{13,9},{6,2},{10,6},{14,10},{7,3},{... | collective-permute-start | bytes 1572872 | tf_op jit(solution)/shard_map/ppermute | solution.py:28
  161.4 23.4 %collective-permute-start = (bf16[2,512,256]{1,2,0:T(8,128)(2,1)S(1)}, bf16[2,512,256]{1,2,0:T(8,128)(2,1)S(1)}, u32[]{:S(2)}, u32[]{:S(2)}) collective-permute-start(bf16[2,512,256]{1,2,0:T(8,128)(2,1)S(1)} %get-tuple-element.535), channel_id=1, source_target_pairs={{0,4},{4,8},{8,12},{1,5},{5,9},{9,13},{2,6},{6,10},{10,14},{3,7},{... | collective-permute-start | bytes 1572872 | tf_op jit(solution)/shard_map/ppermute | solution.py:26
  262.8 17.3 all-to-all-start.3
  422.9 20.6 all-to-all-start.4
  427.2 558.3 %reduce-scatter.8.cloned.1.call-start = ((), (), s32[]{:S(2)}) async-start(), calls=%async_computation.19 | async-start | bytes 4325376 | tf_op jit(solution)/shard_map/reduce_scatter | solution.py:306
  748.8 47.5 %collective-permute-start.5 = (bf16[2,512,256]{1,2,0:T(8,128)(2,1)}, bf16[2,512,256]{1,2,0:T(8,128)(2,1)}, u32[]{:S(2)}, u32[]{:S(2)}) collective-permute-start(bf16[2,512,256]{1,2,0:T(8,128)(2,1)} %pad_maximum_fusion.11), channel_id=1, source_target_pairs={{4,0},{8,4},{12,8},{5,1},{9,5},{13,9},{6,2},{10,6},{14,10},{7,3},{... | collective-permute-start | bytes 1572872 | tf_op jit(solution)/shard_map/ppermute | solution.py:38
  751.0 46.6 %collective-permute-start.4 = (bf16[2,512,256]{1,2,0:T(8,128)(2,1)}, bf16[2,512,256]{1,2,0:T(8,128)(2,1)}, u32[]{:S(2)}, u32[]{:S(2)}) collective-permute-start(bf16[2,512,256]{1,2,0:T(8,128)(2,1)} %pad_maximum_fusion.10), channel_id=1, source_target_pairs={{0,4},{4,8},{8,12},{1,5},{5,9},{9,13},{2,6},{6,10},{10,14},{3,7},{... | collective-permute-start | bytes 1572872 | tf_op jit(solution)/shard_map/ppermute | solution.py:38
  802.1 36.0 %all-to-all-start.7 = ((bf16[4,512,256]{2,1,0:T(8,128)(2,1)}), bf16[4,512,256]{2,1,0:T(8,128)(2,1)}, u32[]{:S(2)}, u32[]{:S(2)}) async-start(bf16[4,512,256]{2,1,0:T(8,128)(2,1)} %bitcast.29), calls=%async_computation.7 | async-start | bytes 2097152 | tf_op jit(solution)/shard_map/all_to_all | solution.py:295
  838.1 17.0 all-to-all-start.6
  855.1 16.0 all-to-all-start.5
  859.4 176.2 %reduce-scatter.6.cloned.1.call-start = ((), (), s32[]{:S(2)}) async-start(), calls=%async_computation.18 | async-start | bytes 12976128 | tf_op jit(solution)/shard_map/reduce_scatter | solution.py:305
  861.1 19.8 copy-start.35
  881.0 514.1 %reduce-scatter.10.cloned.1.call-start = ((), (), s32[]{:S(2)}) async-start(), calls=%async_computation.20 | async-start | bytes 17301504 | tf_op jit(solution)/shard_map/reduce_scatter | solution.py:307
  893.1 865.0 %reduce-scatter.12.cloned.1.call-start = ((), (), s32[]{:S(2)}) async-start(), calls=%async_computation.21 | async-start | bytes 17301504 | tf_op jit(solution)/shard_map/reduce_scatter | solution.py:308
  904.3 1216.6 %reduce-scatter.14.cloned.1.call-start = ((), (), s32[]{:S(2)}) async-start(), calls=%async_computation.22 | async-start | bytes 17301504 | tf_op jit(solution)/shard_map/reduce_scatter | solution.py:309
  929.8 52.1 %copy-start.11 = (f32[512,1024]{1,0:T(8,128)S(1)}, f32[512,1024]{1,0:T(8,128)}, u32[]{:S(2)}) copy-start(f32[512,1024]{1,0:T(8,128)} %copy-done.10) | copy-start | bytes 6291460
  929.8 52.1 %copy-start.47 = (f32[512]{0:T(512)S(1)}, f32[512]{0:T(512)}, u32[]{:S(2)}) copy-start(f32[512]{0:T(512)} %get-tuple-element.558) | copy-start | bytes 6148
  981.9 1139.1 %copy-start.1 = (f32[16,2]{0,1:T(2,128)S(1)}, f32[16,2]{0,1:T(2,128)}, u32[]{:S(2)}) copy-start(f32[16,2]{0,1:T(2,128)} %param.30) | copy-start | bytes 388
  (62 other events, 352.9 us)
Sparse Core Ops, SparseCore 0:
  10.9 72.3 all-gather.5
  86.2 54.9 all-gather.7
  144.1 78.7 all-gather.9
  225.6 82.2 all-gather.11
  310.6 75.2 all-gather.13
  432.2 143.6 reduce-scatter.7
  881.1 154.4 reduce-scatter.5
  1038.6 356.4 reduce-scatter.9
  1398.1 359.9 reduce-scatter.11
  1760.9 359.9 reduce-scatter.13
where the time goes:
time: 2140 us; the launch traced here: 2130 us
  waiting for transfers between devices  1320 us (62%)
  matrix products  272 us (13%)
  local copies, waits for them, and re-layouts  255 us (12%)
  other arithmetic  96.8 us (5%)
  blocking collectives  84.3 us (4%)
  starting transfers between devices  52.3 us (2%)
  loops' own time  37.6 us (2%)
    reduce_scatter x1, waiting for transfers between devices, local(): lax.psum_scatter(grad_up, ('pack', 'cp', 'hd'), scatter_dimension=0, tile...  363 us
    reduce_scatter x1, waiting for transfers between devices, local(): lax.psum_scatter(grad_down, ('pack', 'cp', 'hd'), scatter_dimension=0, ti...  363 us
    reduce_scatter x1, waiting for transfers between devices, local(): lax.psum_scatter(grad_gate, ('pack', 'cp', 'hd'), scatter_dimension=0, ti...  359 us
    unnamed x2, blocking collectives  84.3 us
    all_gather x1, waiting for transfers between devices, local(): lax.all_gather(w_down, ('pack', 'cp', 'hd'), axis=0, tiled=True)  66.5 us
    dot_general x8, matrix products, block_scores(): jnp.einsum('qhd,khd->hqk', q_blk, k_blk, preferred_element_type=jnp.float32)  59.4 us
    reduce_scatter x1, waiting for transfers between devices, local(): lax.psum_scatter(grad_qkv, ('pack', 'cp', 'hd'), scatter_dimension=0, til...  50.2 us
    dot_general x5, matrix products, contract_rows(): lax.dot_general(left_mat, right_mat, (((0,), (0,)), ((), ())), preferred_...  48.2 us
  transfers between devices with their start and end apart: 24, of which 15 were waited for; matrix products, arithmetic and copies ran while one was open for 27% of the time, Pallas kernels for 0%

commit v1 on v0

--- a/solution.py
+++ b/solution.py
@@ -1,8 +1,11 @@
+import functools
 import math
 
 import jax
 import jax.numpy as jnp
 from jax import lax
+from jax.experimental import pallas as pl
+from jax.experimental.pallas import tpu as pltpu
 from jax.sharding import PartitionSpec as P
 
 HEADS = 16
@@ -70,6 +73,207 @@
     return lax.dot_general(
         left_mat, right_mat, (((1,), (1,)), ((), ())), preferred_element_type=jnp.float32
     )
+
+
+MESH = pl.DeviceIdType.MESH
+
+
+def place():
+    return lax.axis_index("pack"), lax.axis_index("cp"), lax.axis_index("hd")
+
+
+def greet(peers):
+    barrier = pltpu.get_barrier_semaphore()
+    for peer in peers:
+        pl.semaphore_signal(barrier, inc=1, device_id=peer, device_id_type=MESH)
+    pl.semaphore_wait(barrier, len(peers))
+
+
+def group_peers(ring):
+    p, c, h = place()
+    peers = [(1 - p, c, h), (p, c, h + 1 - 2 * lax.rem(h, 2)), (p, c, lax.rem(h + 2, 4))]
+    peers += [(p, lax.rem(c + step, ring), h) for step in range(1, ring)]
+    return peers
+
+
+class Scatter:
+    def __init__(self, ring, count, pick, buffers, sems, out, write):
+        self.ring, self.count, self.pick = ring, count, pick
+        self.own, self.b0, self.b1, self.b2, self.b3 = buffers
+        self.load_sem, self.send_sem, self.recv_sem = sems
+        self.out, self.write = out, write
+        self.p, self.c, self.h = place()
+        self.hy, self.hx = self.h // 2, lax.rem(self.h, 2)
+        self.core = (1 - self.p, self.c, self.h)
+        self.xpeer = (self.p, self.c, self.hy * 2 + 1 - self.hx)
+        self.ypeer = (self.p, self.c, (1 - self.hy) * 2 + self.hx)
+
+    def remote(self, i, stage, src, dst, device):
+        return pltpu.make_async_remote_copy(
+            src_ref=src, dst_ref=dst, send_sem=self.send_sem.at[stage, i],
+            recv_sem=self.recv_sem.at[stage, i], device_id=device, device_id_type=MESH)
+
+    def copy0(self, i, src):
+        return self.remote(i, 0, src, self.b0.at[i], self.core)
+
+    def copy1(self, i, first_y):
+        if first_y:
+            return self.remote(i, 1, self.own.at[i, :, 1 - self.hy], self.b1.at[i], self.ypeer)
+        return self.remote(i, 1, self.own.at[i, :, :, 1 - self.hx], self.b1.at[i], self.xpeer)
+
+    def copy2(self, i, first_y):
+        if first_y:
+            return self.remote(i, 2, self.own.at[i, :, self.hy, 1 - self.hx], self.b2.at[i], self.xpeer)
+        return self.remote(i, 2, self.own.at[i, :, 1 - self.hy, self.hx], self.b2.at[i], self.ypeer)
+
+    def copy3(self, i, step):
+        peer = lax.rem(self.c + step, self.ring)
+        return self.remote(i, 3, self.own.at[i, peer, self.hy, self.hx], self.b3.at[i, step - 1], (self.p, peer, self.h))
+
+    def begin(self, i):
+        def go(mine, other):
+            pltpu.make_async_copy(mine, self.own.at[i], self.load_sem.at[i]).start()
+            self.copy0(i, other).start()
+        self.pick(i, self.p, go)
+
+    def stage1(self, i, first_y):
+        pltpu.make_async_copy(self.b0.at[i], self.own.at[i], self.load_sem.at[i]).wait()
+        self.copy0(i, self.own.at[i]).wait_recv()
+        def add(k, carry):
+            self.own[i, k] = self.own[i, k] + self.b0[i, k]
+            return carry
+        lax.fori_loop(0, self.ring, add, 0)
+        self.copy1(i, first_y).start()
+
+    def stage2(self, i, first_y):
+        self.copy1(i, first_y).wait_recv()
+        def add(k, carry):
+            for m in range(2):
+                at = (i, k, self.hy, m) if first_y else (i, k, m, self.hx)
+                self.own[at] = self.own[at] + self.b1[i, k, m]
+            return carry
+        lax.fori_loop(0, self.ring, add, 0)
+        self.copy2(i, first_y).start()
+
+    def stage3(self, i, first_y):
+        self.copy2(i, first_y).wait_recv()
+        def add(k, carry):
+            at = (i, k, self.hy, self.hx)
+            self.own[at] = self.own[at] + self.b2[i, k]
+            return carry
+        lax.fori_loop(0, self.ring, add, 0)
+        for step in range(1, self.ring):
+            self.copy3(i, step).start()
+
+    def finish(self, i):
+        pltpu.make_async_copy(self.b3.at[i], self.b3.at[i], self.recv_sem.at[3, i]).wait()
+        total = self.own[i, self.c, self.hy, self.hx].astype(jnp.float32)
+        for step in range(1, self.ring):
+            total = total + self.b3[i, step - 1].astype(jnp.float32)
+        self.write(i, total)
+
+    def drain(self, i, first_y):
+        self.copy0(i, self.own.at[i]).wait_send()
+        self.copy1(i, first_y).wait_send()
+        self.copy2(i, first_y).wait_send()
+        pltpu.make_async_copy(self.b3.at[i], self.b3.at[i], self.send_sem.at[3, i]).wait()
+
+    def step(self, t, ahead=3, lags=(0, 2, 4, 6)):
+        pairs = (self.count + 1) // 2
+        def both(pair, act):
+            for first_y in (True, False):
+                i = 2 * pair + (0 if first_y else 1)
+                guard = (pair >= 0) & (i < self.count) & (i >= 0)
+                pl.when(guard)(functools.partial(act, i, first_y))
+        both(t, lambda i, f: self.begin(i))
+        both(t - ahead - lags[0], self.stage1)
+        both(t - ahead - lags[1], self.stage2)
+        both(t - ahead - lags[2], self.stage3)
+        both(t - ahead - lags[3], lambda i, f: self.finish(i))
+
+    def steps(self, ahead=3, lags=(0, 2, 4, 6)):
+        return (self.count + 1) // 2 + ahead + lags[3]
+
+    def drain_all(self):
+        def one(t, carry):
+            for first_y in (True, False):
+                i = 2 * t + (0 if first_y else 1)
+                pl.when(i < self.count)(functools.partial(self.drain, i, first_y))
+            return carry
+        lax.fori_loop(0, (self.count + 1) // 2, one, 0)
+
+
+def scatter_scratch(ring, count, rows, cols):
+    bf = jnp.bfloat16
+    return [
+        pltpu.VMEM((count, ring, 2, 2, rows, cols), bf),
+        pltpu.VMEM((count, ring, 2, 2, rows, cols), bf),
+        pltpu.VMEM((count, ring, 2, rows, cols), bf),
+        pltpu.VMEM((count, ring, rows, cols), bf),
+        pltpu.VMEM((count, ring - 1, rows, cols), bf),
+        pltpu.SemaphoreType.DMA((count,)),
+        pltpu.SemaphoreType.DMA((4, count)),
+        pltpu.SemaphoreType.DMA((4, count)),
+    ]
+
+
+def scatter_kernel(ring, layout, count, *refs):
+    n = len(layout)
+    grads, out = refs[:n], refs[n]
+    own, b0, b1, b2, b3, load_sem, send_sem, recv_sem = refs[n + 1:]
+    greet(group_peers(ring))
+
+    def pick(i, p, go):
+        start = 0
+        for ref, (size, outer) in zip(grads, layout):
+            j = i - start
+            def run(ref=ref, j=j, outer=outer):
+                if outer:
+                    go(ref.at[j, p], ref.at[j, 1 - p])
+                else:
+                    go(ref.at[p, :, :, :, j], ref.at[1 - p, :, :, :, j])
+            pl.when((j >= 0) & (j < size))(run)
+            start += size
+
+    def write(i, total):
+        out[i] = total
+
+    work = Scatter(ring, count, pick, (own, b0, b1, b2, b3), (load_sem, send_sem, recv_sem), out, write)
+    def body(t, carry):
+        work.step(t)
+        return carry
+    lax.fori_loop(0, work.steps(), body, 0)
+    work.drain_all()
+
+
+def scatter(grads, layout, ring, collective_id):
+    rows, cols = grads[0].shape[-2:]
+    count = sum(size for size, _ in layout)
+    return pl.pallas_call(
+        functools.partial(scatter_kernel, ring, layout, count),
+        out_shape=jax.ShapeDtypeStruct((count, rows, cols), jnp.float32),
+        in_specs=[pl.BlockSpec(memory_space=pl.ANY)] * len(grads),
+        out_specs=pl.BlockSpec(memory_space=pltpu.VMEM),
+        scratch_shapes=scatter_scratch(ring, count, rows, cols),
+        compiler_params=pltpu.CompilerParams(collective_id=collective_id, has_side_effects=True, vmem_limit_bytes=60 * 2**20),
+        name="rsum",
+    )(*grads)
+
+
+def item_shape(rows):
+    full = max(rows, 16)
+    return full, rows * 512 // full
+
+
+def column_items(grad, ring):
+    depth = grad.shape[0] // (8 * ring)
+    rows, cols = item_shape(depth)
+    parts = jnp.moveaxis(grad.reshape(2, ring, 2, 2, depth, -1, 512), 5, 0)
+    return parts.reshape(-1, 2, ring, 2, 2, rows, cols)
+
+
+def back_columns(items, depth):
+    return jnp.moveaxis(items.reshape(-1, depth, 512), 0, 1).reshape(depth, -1)
 
 
 def local(
@@ -301,12 +505,27 @@
         residual, rms_attn, back_gattn.astype(jnp.float32), d_normed
     )
     grad_inputs = d_hidden + d_resid_norm
+    ring = lax.axis_size("cp")
+    low = jnp.bfloat16
+    depth = w_qkv.shape[0]
+    down_depth = w_down.shape[0]
+    down_items = column_items(
+        grad_down.astype(low).reshape(8 * ring, 4, depth, model_width).swapaxes(0, 1).reshape(4, 8 * ring * depth, model_width).swapaxes(0, 1).reshape(8 * ring * depth, 4 * model_width), ring)
+    parts = [column_items(grad.astype(low), ring) for grad in (grad_gate, grad_up)]
+    parts += [down_items]
+    parts += [column_items(grad.astype(low), ring) for grad in (grad_out, grad_qkv)]
+    items = scatter(parts, tuple((part.shape[0], True) for part in parts), ring, 0)
+    own_gate = back_columns(items[:8], depth)
+    own_up = back_columns(items[8:16], depth)
+    own_down = back_columns(items[16:24], depth).reshape(depth, 4, model_width).swapaxes(0, 1).reshape(down_depth, model_width)
+    own_out = back_columns(items[24:26], depth)
+    own_qkv = back_columns(items[26:], depth)
     summed = (
-        lax.psum_scatter(grad_qkv, ("pack", "cp", "hd"), scatter_dimension=0, tiled=True),
-        lax.psum_scatter(grad_out, ("pack", "cp", "hd"), scatter_dimension=0, tiled=True),
-        lax.psum_scatter(grad_gate, ("pack", "cp", "hd"), scatter_dimension=0, tiled=True),
-        lax.psum_scatter(grad_up, ("pack", "cp", "hd"), scatter_dimension=0, tiled=True),
-        lax.psum_scatter(grad_down, ("pack", "cp", "hd"), scatter_dimension=0, tiled=True),
+        own_qkv,
+        own_out,
+        own_gate,
+        own_up,
+        own_down,
         lax.psum_scatter(
             jnp.sum(gattn_terms, axis=0), ("pack", "cp", "hd"), scatter_dimension=0, tiled=True
         ),

time: 2140 us -> 1220 us (0.57)
  waiting for transfers between devices: 1320 us -> 125 us
  Pallas kernels: 0 us -> 159 us
  local copies, waits for them, and re-layouts: 255 us -> 384 us
    reduce_scatter x5 -> x0, waiting for transfers between devices: 1140 us -> none  [the longest x1 363 us: local(): lax.psum_scatter(grad_up, ('pack', 'cp', 'hd'), scatter_dimension=0, tile...]
    pallas_call x0 -> x1, Pallas kernels: none -> 159 us  [scatter(): pl.pallas_call(functools.partial(scatter_kernel, ring, layout, count), ou...]
    reshape x0 -> x11, local copies, waits for them, and re-layouts: none -> 60.9 us  [the longest x6 49.2 us: column_items(): parts = jnp.moveaxis(grad.reshape(2, ring, 2, 2, depth, -1, 512), 5, 0)]
    another operation x0 -> x3, local copies, waits for them, and re-layouts: none -> 24.6 us  [the longest x2 22.5 us: column_items(): parts = jnp.moveaxis(grad.reshape(2, ring, 2, 2, depth, -1, 512), 5, 0)]
    unnamed x114 -> x128, local copies, waits for them, and re-layouts: 10.6 us -> 35.1 us
  transfers between devices with their start and end apart: 24 -> 19, of which waited for: 15 -> 8; matrix products, arithmetic and copies ran while one was open for 27% -> 29% of each run, Pallas kernels for 0% -> 0%
where the time goes in v1:
time: 1220 us; the launch traced here: 1200 us
  local copies, waits for them, and re-layouts  384 us (31%)
  matrix products  256 us (21%)
  Pallas kernels  159 us (13%)
  waiting for transfers between devices  125 us (10%)
  other arithmetic  93.9 us (8%)
  blocking collectives  81.5 us (7%)
  starting transfers between devices  51.3 us (4%)
  loops' own time  37.5 us (3%)
  between operations  15.2 us (1%)
    pallas_call x1, Pallas kernels, scatter(): pl.pallas_call(functools.partial(scatter_kernel, ring, layout, count), ou...  159 us
    unnamed x2, blocking collectives  81.5 us
    dot_general x8, matrix products, block_scores(): jnp.einsum('qhd,khd->hqk', q_blk, k_blk, preferred_element_type=jnp.float32)  59.7 us
    all_gather x1, waiting for transfers between devices, local(): lax.all_gather(w_down, ('pack', 'cp', 'hd'), axis=0, tiled=True)  57.6 us
    reshape x6, local copies, waits for them, and re-layouts, column_items(): parts = jnp.moveaxis(grad.reshape(2, ring, 2, 2, depth, -1, 512), 5, 0)  49.2 us
    dynamic_update_slice x8, local copies, waits for them, and re-layouts, local(): lax.scan(backward_block, init_state, (starts, lse_blocks))  46.5 us
    dot_general x5, matrix products, contract_cols(): lax.dot_general(left_mat, right_mat, (((1,), (1,)), ((), ())), preferred_...  41.8 us
    dynamic_update_slice x4, local copies, waits for them, and re-layouts, backward_block(): lax.dynamic_update_slice_in_dim(dv_ext, lax.dynamic_slice_in_dim(dv_ext,...  38.6 us
  transfers between devices with their start and end apart: 19, of which 8 were waited for; matrix products, arithmetic and copies ran while one was open for 29% of the time, Pallas kernels for 0%

profile of v1, /device:TPU:0, one launch (start us, length us, event | category | flops | bytes accessed | tf_op | source)
XLA Modules:
  0.0 1202.7 jit_solution(13507586760755820273)
XLA Ops:
  11.7 42.4 %all-reduce.9 = (bf16[1024]{0:T(1024)(128)(2,1)S(1)}, bf16[1024]{0:T(1024)(128)(2,1)}) all-reduce(bf16[1024]{0:T(1024)(128)(2,1)S(1)} %dynamic-update-slice, bf16[1024]{0:T(1024)(128)(2,1)S(1)} %dynamic-update-slice.1), channel_id=1, replica_groups=mesh['pack'=2,'cp'=4,'hd'=4] {'pack','cp','hd'}, use_global_device_ids=true, to_apply=%add.4 | all-reduce | flops 2048 | bytes 8192
  56.2 27.1 %all-gather.6.cloned.1.call-done = bf16[1024,3072]{1,0:T(8,128)(2,1)} async-done(((bf16[32,3072]{1,0:T(8,128)(2,1)}), bf16[1024,3072]{1,0:T(8,128)(2,1)}) %all-gather.6.cloned.1.call-update) | async-done | bytes 6291472 | tf_op jit(solution)/shard_map/all_gather | solution.py:297
  116.7 9.7 all-to-all-done.1
  167.6 15.5 %collective-permute-done.1 = bf16[2,512,256]{1,2,0:T(8,128)(2,1)S(1)} collective-permute-done((bf16[2,512,256]{1,2,0:T(8,128)(2,1)S(1)}, bf16[2,512,256]{1,2,0:T(8,128)(2,1)S(1)}, u32[]{:S(2)}, u32[]{:S(2)}) %collective-permute-start.1) | collective-permute-done | bytes 524320 | tf_op jit(solution)/shard_map/ppermute | solution.py:31
  185.6 76.6 %while.34 = (s32[]{:T(128)}, bf16[4,512,256]{1,2,0:T(8,128)(2,1)}, f32[4,4,512]{2,1,0:T(4,128)S(1)}, s32[4]{0:T(128)S(1)}, bf16[3072,4,64]{0,2,1:T(8,128)(2,1)S(...) while((s32[]{:T(128)}, bf16[4,512,256]{1,2,0:T(8,128)(2,1)}, ...), condition=%wide.region_6.7_spmd.clone, body=%wide.region_3.6_spmd.clone.sunk | while | flops 841480192 | bytes 43682188 | solution.py:390
  306.8 10.1 fusion.66
  316.9 11.6 fusion.67
  328.5 57.6 %all-gather.14.cloned.1.call-done = bf16[4096,1024]{1,0:T(8,128)(2,1)} async-done(((bf16[128,1024]{1,0:T(8,128)(2,1)}), bf16[4096,1024]{1,0:T(8,128)(2,1)}) %all-gather.14.cloned.1.call-update) | async-done | bytes 8388624 | tf_op jit(solution)/shard_map/all_gather | solution.py:301
  386.1 16.1 %multiply_convert_fusion.1 = (bf16[512,4096]{1,0:T(8,128)(2,1)}, bf16[512,4096]{1,0:T(8,128)(2,1)}, bf16[512,4096]{1,0:T(8,128)(2,1)}) fusion(f32[512,4096]{1,0:T(8,128)} %fusion.66, f32[512,4096]{1,0:T(8,128)} %fusion.67, bf16[512,1024]{1,0:T(8,128)(2,1)S(1)} %copy-done.31, bf16[4096,1024]{1,0:T(8,128)(2,1)} %all-gather.14.cloned.1.call-done), kind=kOutput, calls=%fused_computation.66 | convolution fusion | flops 4326424576 | bytes 38797312 | tf_op jit(solution)/shard_map/dot_general | solution.py:73
  425.7 10.8 add_convert_fusion
  451.8 293.9 %while.35 = (s32[]{:T(128)}, f32[3072,4,64]{0,2,1:T(8,128)}, f32[3072,4,64]{0,2,1:T(8,128)}, f32[4,2]{0,1:T(2,128)S(1)}, f32[4,512,4,64]{1,0,3,2:T(4,128)}, /*in...) while((s32[]{:T(128)}, f32[3072,4,64]{0,2,1:T(8,128)}, ...), condition=%wide.region_13.14_spmd.clone, body=%wide.region_9.13_spmd.clone.sunk | while | flops 2066479104 | bytes 165293776 | solution.py:470
  483.0 10.0 dynamic_update_slice.51
  499.5 10.0 dynamic_update_slice.52
  515.1 11.1 dynamic_update_slice.53
  557.1 9.8 dynamic_update_slice.51
  573.4 9.8 dynamic_update_slice.52
  588.9 11.1 dynamic_update_slice.53
  630.8 9.6 dynamic_update_slice.51
  646.9 9.7 dynamic_update_slice.52
  662.2 11.1 dynamic_update_slice.53
  734.4 11.1 dynamic_update_slice.53
  831.3 9.4 convolution_convert_fusion.1
  840.8 12.3 %copy.322 = bf16[128,8,8,512]{3,2,1,0:T(8,128)(2,1)} copy(bf16[128,8,8,512]{3,1,2,0:T(8,128)(2,1)} %bitcast.252) | data formatting | bytes 16777216
  853.1 9.6 copy.333
  862.7 12.5 %copy.323 = bf16[128,8,8,512]{3,2,1,0:T(8,128)(2,1)} copy(bf16[128,8,8,512]{3,1,2,0:T(8,128)(2,1)} %bitcast.253) | data formatting | bytes 16777216
  875.2 9.6 copy.332
  893.4 12.1 %copy.280 = bf16[1024,4,1024]{2,1,0:T(4,128)(2,1)} copy(bf16[1024,4,1024]{2,0,1:T(8,128)(2,1)} %bitcast.243) | data formatting | bytes 16777216 | tf_op jit(solution)/shard_map/transpose | solution.py:513
  905.5 12.7 %reshape_reshape.6 = bf16[2,4,2,2,32,8,512]{6,5,4,3,2,1,0:T(8,128)(2,1)} reshape(bf16[1024,4,1024]{2,1,0:T(4,128)(2,1)} %copy.280) | data formatting | bytes 16777216 | tf_op jit(solution)/shard_map/reshape;reshape | solution.py:271
  918.3 9.8 copy.331
  950.7 13.8 %reshape.546 = bf16[2,4,2,2,32,6,512]{6,5,4,3,2,1,0:T(8,128)(2,1)} reshape(bf16[1024,3072]{1,0:T(8,128)(2,1)} %convolution_convert_fusion.3) | data formatting | bytes 12582912 | tf_op jit(solution)/shard_map/reshape | solution.py:271
  972.8 158.6 %rsum.1 = f32[32,32,512]{2,1,0:T(8,128)} custom-call(bf16[8,2,4,2,2,32,512]{6,5,4,3,2,1,0:T(8,128)(2,1)} %bitcast.238, bf16[8,2,4,2,2,32,512]{6,5,4,3,2,1,0:T(8,128)(2,1)} %bitcast.239, bf16[8,2,4,2,2,32,512]{6,5,4,3,2,1,0:T(8,128)(2,1)} %bitcast.240, bf16[2,2,4,2,2,32,512]{6,5,4,3,2,1,0:T(8,128)(2,1)} %bitcast.249, bf16[6,2,4,2,2,32,512]{6,5,4,3,2,1,0:T(8,128)(2,1)} %bitcast.244), custom_call_target="tpu_custom_call" | custom-call | tf_op jit(solution)/shard_map/rsum/pallas_call | solution.py:252
  1151.9 39.1 %all-reduce.8 = (f32[1024]{0:T(1024)S(1)}, f32[1024]{0:T(1024)S(1)}, f32[64]{0:T(128)}, f32[64]{0:T(128)}, f32[16,2]{0,1:T(2,128)}) all-reduce(f32[1024]{0:T(1024)S(1)} %get-tuple-element.433, f32[1024]{0:T(1024)S(1)} %copy-done.57, f32[64]{0:T(128)S(1)} %reduce_sum.184, ...), channel_id=2, replica_groups=mesh['pack'=2,'cp'=4,'hd'=4] {'pack','cp','hd'}, use_global_device_ids=true, to_apply=%region_18.19.clone | all-reduce | flops 2208 | bytes 17664
  (447 shorter events, 546.1 us)
Async XLA Ops:
  7.2 105.8 %copy-start = (f32[16,2]{0,1:T(2,128)S(1)}, f32[16,2]{0,1:T(2,128)}, u32[]{:S(2)}) copy-start(f32[16,2]{0,1:T(2,128)} %param.30) | copy-start | bytes 388
  7.2 76.1 %all-gather.6.cloned.1.call-start = ((), (), s32[]{:S(2)}) async-start(), calls=%async_computation.8 | async-start | bytes 6488064 | tf_op jit(solution)/shard_map/all_gather | solution.py:297
  7.9 292.9 %all-gather.8.cloned.1.call-start = ((), (), s32[]{:S(2)}) async-start(), calls=%async_computation.9 | async-start | bytes 2162688 | tf_op jit(solution)/shard_map/all_gather | solution.py:298
  8.7 297.2 %all-gather.10.cloned.1.call-start = ((), (), s32[]{:S(2)}) async-start(), calls=%async_computation.10 | async-start | bytes 8650752 | tf_op jit(solution)/shard_map/all_gather | solution.py:299
  9.4 307.5 %all-gather.12.cloned.1.call-start = ((), (), s32[]{:S(2)}) async-start(), calls=%async_computation.11 | async-start | bytes 8650752 | tf_op jit(solution)/shard_map/all_gather | solution.py:300
  54.1 29.2 %copy-start.42 = (f32[1024]{0:T(1024)}, f32[1024]{0:T(1024)S(1)}, u32[]{:S(2)}) copy-start(f32[1024]{0:T(1024)S(1)} %convert_element_type.157) | copy-start | bytes 12292
  56.2 27.1 %copy-start.45 = (f32[512]{0:T(512)}, f32[512]{0:T(512)S(1)}, u32[]{:S(2)}) copy-start(f32[512]{0:T(512)S(1)} %get-tuple-element.562) | copy-start | bytes 6148
  90.3 12.0 copy-start.48
  91.6 17.8 %all-to-all-start.2 = ((bf16[512,4,256]{0,2,1:T(8,128)(2,1)}), bf16[512,4,256]{0,2,1:T(8,128)(2,1)S(1)}, u32[]{:S(2)}, u32[]{:S(2)}) async-start(bf16[512,4,256]{0,2,1:T(8,128)(2,1)} %bitcast.8), calls=%async_computation.2 | async-start | bytes 2097152 | tf_op jit(solution)/shard_map/all_to_all | solution.py:320
  95.1 291.0 %all-gather.14.cloned.1.call-start = ((), (), s32[]{:S(2)}) async-start(), calls=%async_computation.12 | async-start | bytes 8650752 | tf_op jit(solution)/shard_map/all_gather | solution.py:301
  95.8 70.0 %collective-permute-start.3 = (s32[2,512]{1,0:T(2,128)}, s32[2,512]{1,0:T(2,128)}, u32[]{:S(2)}, u32[]{:S(2)}) collective-permute-start(s32[2,512]{1,0:T(2,128)} %get-tuple-element.557), channel_id=1, source_target_pairs={{4,0},{8,4},{12,8},{5,1},{9,5},{13,9},{6,2},{10,6},{14,10},{7,3},{... | collective-permute-start | bytes 12296 | tf_op jit(solution)/shard_map/ppermute | solution.py:31
  97.1 68.7 %collective-permute-start.2 = (s32[2,512]{1,0:T(2,128)}, s32[2,512]{1,0:T(2,128)}, u32[]{:S(2)}, u32[]{:S(2)}) collective-permute-start(s32[2,512]{1,0:T(2,128)} %get-tuple-element.556), channel_id=1, source_target_pairs={{0,4},{4,8},{8,12},{1,5},{5,9},{9,13},{2,6},{6,10},{10,14},{3,7},{... | collective-permute-start | bytes 12296 | tf_op jit(solution)/shard_map/ppermute | solution.py:29
  109.4 17.0 %all-to-all-start.1 = ((bf16[512,4,256]{2,0,1:T(8,128)(2,1)}), bf16[512,4,256]{2,0,1:T(8,128)(2,1)S(1)}, u32[]{:S(2)}, u32[]{:S(2)}) async-start(bf16[512,4,256]{2,0,1:T(8,128)(2,1)} %bitcast.199), calls=%async_computation.1 | async-start | bytes 2097152 | tf_op jit(solution)/shard_map/all_to_all | solution.py:328
  114.9 43.7 %copy-start.26 = (f32[2048,32]{0,1:T(8,128)}, f32[2048,32]{0,1:T(8,128)S(1)}, u32[]{:S(2)}) copy-start(f32[2048,32]{0,1:T(8,128)S(1)} %get-tuple-element.560) | copy-start | bytes 786436
  116.7 15.5 %copy-start.15 = (bf16[512,4,256]{2,0,1:T(8,128)(2,1)}, bf16[512,4,256]{2,0,1:T(8,128)(2,1)S(1)}, u32[]{:S(2)}) copy-start(bf16[512,4,256]{2,0,1:T(8,128)(2,1)S(1)} %copy.260) | copy-start | bytes 3145732
  126.5 17.4 %all-to-all-start = ((bf16[512,4,256]{0,2,1:T(8,128)(2,1)}), bf16[512,4,256]{0,2,1:T(8,128)(2,1)}, u32[]{:S(2)}, u32[]{:S(2)}) async-start(bf16[512,4,256]{0,2,1:T(8,128)(2,1)} %bitcast.256), calls=%async_computation | async-start | bytes 2097152 | tf_op jit(solution)/shard_map/all_to_all | solution.py:321
  138.8 18.8 %copy-start.6 = (f32[2048,4,64]{0,2,1:T(8,128)}, f32[2048,4,64]{0,2,1:T(8,128)S(1)}, u32[]{:S(2)}) copy-start(f32[2048,4,64]{0,2,1:T(8,128)S(1)} %reshape.553) | copy-start | bytes 6291460
  159.7 23.5 %collective-permute-start.1 = (bf16[2,512,256]{1,2,0:T(8,128)(2,1)S(1)}, bf16[2,512,256]{1,2,0:T(8,128)(2,1)S(1)}, u32[]{:S(2)}, u32[]{:S(2)}) collective-permute-start(bf16[2,512,256]{1,2,0:T(8,128)(2,1)S(1)} %get-tuple-element.539), channel_id=1, source_target_pairs={{4,0},{8,4},{12,8},{5,1},{9,5},{13,9},{6,2},{10,6},{14,10},{7,3},{... | collective-permute-start | bytes 1572872 | tf_op jit(solution)/shard_map/ppermute | solution.py:31
  161.0 22.9 %collective-permute-start = (bf16[2,512,256]{1,2,0:T(8,128)(2,1)S(1)}, bf16[2,512,256]{1,2,0:T(8,128)(2,1)S(1)}, u32[]{:S(2)}, u32[]{:S(2)}) collective-permute-start(bf16[2,512,256]{1,2,0:T(8,128)(2,1)S(1)} %get-tuple-element.538), channel_id=1, source_target_pairs={{0,4},{4,8},{8,12},{1,5},{5,9},{9,13},{2,6},{6,10},{10,14},{3,7},{... | collective-permute-start | bytes 1572872 | tf_op jit(solution)/shard_map/ppermute | solution.py:29
  262.2 38.6 %all-to-all-start.3 = ((bf16[4,512,256]{1,2,0:T(8,128)(2,1)}), bf16[4,512,256]{1,2,0:T(8,128)(2,1)}, u32[]{:S(2)}, u32[]{:S(2)}) async-start(bf16[4,512,256]{1,2,0:T(8,128)(2,1)} %get-tuple-element.314), calls=%async_computation.3 | async-start | bytes 2097152 | tf_op jit(solution)/shard_map/all_to_all | solution.py:392
  316.9 69.2 %copy-start.31 = (bf16[512,1024]{1,0:T(8,128)(2,1)S(1)}, bf16[512,1024]{1,0:T(8,128)(2,1)}, u32[]{:S(2)}) copy-start(bf16[512,1024]{1,0:T(8,128)(2,1)} %param.20) | copy-start | bytes 3145732
  422.1 21.1 %all-to-all-start.4 = ((bf16[512,4,256]{2,0,1:T(8,128)(2,1)}), bf16[512,4,256]{2,0,1:T(8,128)(2,1)S(1)}, u32[]{:S(2)}, u32[]{:S(2)}) async-start(bf16[512,4,256]{2,0,1:T(8,128)(2,1)} %bitcast.258), calls=%async_computation.4 | async-start | bytes 2097152 | tf_op jit(solution)/shard_map/all_to_all | solution.py:430
  425.7 10.8 copy-start.32
  425.7 10.8 copy-start.61
  471.2 10.5 copy-start.3
  749.6 19.8 %collective-permute-start.5 = (bf16[2,512,256]{1,2,0:T(8,128)(2,1)}, bf16[2,512,256]{1,2,0:T(8,128)(2,1)S(1)}, u32[]{:S(2)}, u32[]{:S(2)}) collective-permute-start(bf16[2,512,256]{1,2,0:T(8,128)(2,1)} %pad_maximum_fusion.11), channel_id=1, source_target_pairs={{4,0},{8,4},{12,8},{5,1},{9,5},{13,9},{6,2},{10,6},{14,10},{7,3},{... | collective-permute-start | bytes 1572872 | tf_op jit(solution)/shard_map/ppermute | solution.py:41
  751.9 11.7 copy-start.5
  751.9 18.5 %collective-permute-start.4 = (bf16[2,512,256]{1,2,0:T(8,128)(2,1)}, bf16[2,512,256]{1,2,0:T(8,128)(2,1)S(1)}, u32[]{:S(2)}, u32[]{:S(2)}) collective-permute-start(bf16[2,512,256]{1,2,0:T(8,128)(2,1)} %pad_maximum_fusion.10), channel_id=1, source_target_pairs={{0,4},{4,8},{8,12},{1,5},{5,9},{9,13},{2,6},{6,10},{10,14},{3,7},{... | collective-permute-start | bytes 1572872 | tf_op jit(solution)/shard_map/ppermute | solution.py:41
  773.7 35.1 %all-to-all-start.7 = ((bf16[4,512,256]{2,1,0:T(8,128)(2,1)}), bf16[4,512,256]{2,1,0:T(8,128)(2,1)}, u32[]{:S(2)}, u32[]{:S(2)}) async-start(bf16[4,512,256]{2,1,0:T(8,128)(2,1)} %bitcast.29), calls=%async_computation.7 | async-start | bytes 2097152 | tf_op jit(solution)/shard_map/all_to_all | solution.py:499
  808.9 18.1 %all-to-all-start.6 = ((bf16[4,512,256]{1,2,0:T(8,128)(2,1)}), bf16[4,512,256]{1,2,0:T(8,128)(2,1)}, u32[]{:S(2)}, u32[]{:S(2)}) async-start(bf16[4,512,256]{1,2,0:T(8,128)(2,1)} %copy.274), calls=%async_computation.6 | async-start | bytes 2097152 | tf_op jit(solution)/shard_map/all_to_all | solution.py:498
  827.0 115.4 %all-to-all-start.5 = ((bf16[4,512,256]{1,2,0:T(8,128)(2,1)}), bf16[4,512,256]{1,2,0:T(8,128)(2,1)}, u32[]{:S(2)}, u32[]{:S(2)}) async-start(bf16[4,512,256]{1,2,0:T(8,128)(2,1)} %copy.269), calls=%async_computation.5 | async-start | bytes 2097152 | tf_op jit(solution)/shard_map/all_to_all | solution.py:497
  1145.7 46.5 %copy-start.44 = (f32[512]{0:T(512)S(1)}, f32[512]{0:T(512)}, u32[]{:S(2)}) copy-start(f32[512]{0:T(512)} %get-tuple-element.561) | copy-start | bytes 6148
  (62 other events, 250.8 us)
Sparse Core Ops, SparseCore 0:
  10.9 72.3 all-gather.5
  86.2 54.9 all-gather.7
  144.1 78.5 all-gather.9
  225.3 81.7 all-gather.11
  309.8 76.2 all-gather.13

commit v2 on v1

v2 whole, which is shorter than its diff:
```python
import functools
import math

import jax
import jax.numpy as jnp
from jax import lax
from jax.experimental import pallas as pl
from jax.experimental.pallas import tpu as pltpu
from jax.sharding import PartitionSpec as P

HEADS = 16
HDIM = 64
HALF = 512
QB = 256
SPAN = QB + 2 * HALF
FAR = -1e30
EPS = 1e-6
theta_base = 10000.0
MIB = 2**20
F32, BF = jnp.float32, jnp.bfloat16
MESH = pl.DeviceIdType.MESH
VM = pl.BlockSpec(memory_space=pltpu.VMEM)
ANY = pl.BlockSpec(memory_space=pl.ANY)
ALL = slice(None)


def item_shape(rows):
    full = max(rows, 16)
    return full, rows * 512 // full


def place():
    return lax.axis_index("pack"), lax.axis_index("cp"), lax.axis_index("hd")


def greet(peers):
    barrier = pltpu.get_barrier_semaphore()
    for peer in peers:
        pl.semaphore_signal(barrier, inc=1, device_id=peer, device_id_type=MESH)
    pl.semaphore_wait(barrier, len(peers))


def group_peers(ring):
    p, c, h = place()
    peers = [(1 - p, c, h), (p, c, h + 1 - 2 * lax.rem(h, 2)), (p, c, lax.rem(h + 2, 4))]
    peers += [(p, lax.rem(c + step, ring), h) for step in range(1, ring)]
    return peers


class Scatter:
    def __init__(self, ring, count, pick, buffers, sems, out, write):
        self.ring, self.count, self.pick = ring, count, pick
        self.load, self.own, self.b1, self.b2, self.b3 = buffers
        self.slots = self.load.shape[0]
        self.load_sem, self.send_sem, self.recv_sem = sems
        self.out, self.write = out, write
        self.p, self.c, self.h = place()
        self.hy, self.hx = self.h // 2, lax.rem(self.h, 2)
        self.core = (1 - self.p, self.c, self.h)
        self.xpeer = (self.p, self.c, self.hy * 2 + 1 - self.hx)
        self.ypeer = (self.p, self.c, (1 - self.hy) * 2 + self.hx)

    def remote(self, i, stage, src, dst, device):
        return pltpu.make_async_remote_copy(
            src_ref=src, dst_ref=dst, send_sem=self.send_sem.at[stage, i],
            recv_sem=self.recv_sem.at[stage, i], device_id=device, device_id_type=MESH)

    def copy0(self, i, src):
        return self.remote(i, 0, src, self.own.at[i], self.core)

    def copy1(self, i, first_y):
        if first_y:
            return self.remote(i, 1, self.own.at[i, :, 1 - self.hy], self.b1.at[i], self.ypeer)
        return self.remote(i, 1, self.own.at[i, :, :, 1 - self.hx], self.b1.at[i], self.xpeer)

    def copy2(self, i, first_y):
        if first_y:
            return self.remote(i, 2, self.own.at[i, :, self.hy, 1 - self.hx], self.b2.at[i], self.xpeer)
        return self.remote(i, 2, self.own.at[i, :, 1 - self.hy, self.hx], self.b2.at[i], self.ypeer)

    def copy3(self, i, step):
        peer = lax.rem(self.c + step, self.ring)
        return self.remote(i, 3, self.own.at[i, peer, self.hy, self.hx], self.b3.at[i, step - 1], (self.p, peer, self.h))

    def begin(self, i):
        def go(mine, other):
            slot = lax.rem(i, self.slots)
            pltpu.make_async_copy(mine, self.load.at[slot], self.load_sem.at[slot]).start()
            self.copy0(i, other).start()
        self.pick(i, self.p, go)

    def stage1(self, i, first_y):
        slot = lax.rem(i, self.slots)
        pltpu.make_async_copy(self.load.at[slot], self.load.at[slot], self.load_sem.at[slot]).wait()
        self.copy0(i, self.own.at[i]).wait_recv()
        def add(k, carry):
            self.own[i, k] = self.own[i, k] + self.load[slot, k]
            return carry
        lax.fori_loop(0, self.ring, add, 0)
        self.copy1(i, first_y).start()

    def stage2(self, i, first_y):
        self.copy1(i, first_y).wait_recv()
        def add(k, carry):
            for m in range(2):
                at = (i, k, self.hy, m) if first_y else (i, k, m, self.hx)
                self.own[at] = self.own[at] + self.b1[i, k, m]
            return carry
        lax.fori_loop(0, self.ring, add, 0)
        self.copy2(i, first_y).start()

    def stage3(self, i, first_y):
        self.copy2(i, first_y).wait_recv()
        def add(k, carry):
            at = (i, k, self.hy, self.hx)
            self.own[at] = self.own[at] + self.b2[i, k]
            return carry
        lax.fori_loop(0, self.ring, add, 0)
        for step in range(1, self.ring):
            self.copy3(i, step).start()

    def finish(self, i):
        pltpu.make_async_copy(self.b3.at[i], self.b3.at[i], self.recv_sem.at[3, i]).wait()
        total = self.own[i, self.c, self.hy, self.hx].astype(jnp.float32)
        for step in range(1, self.ring):
            total = total + self.b3[i, step - 1].astype(jnp.float32)
        self.write(i, total)

    def drain(self, i, first_y):
        self.copy0(i, self.own.at[i]).wait_send()
        self.copy1(i, first_y).wait_send()
        self.copy2(i, first_y).wait_send()
        pltpu.make_async_copy(self.b3.at[i], self.b3.at[i], self.send_sem.at[3, i]).wait()

    def step(self, t, ahead=3, lags=(0, 2, 4, 6)):
        pairs = (self.count + 1) // 2
        def both(pair, act):
            for first_y in (True, False):
                i = 2 * pair + (0 if first_y else 1)
                guard = (pair >= 0) & (i < self.count) & (i >= 0)
                pl.when(guard)(functools.partial(act, i, first_y))
        both(t, lambda i, f: self.begin(i))
        both(t - ahead - lags[0], self.stage1)
        both(t - ahead - lags[1], self.stage2)
        both(t - ahead - lags[2], self.stage3)
        both(t - ahead - lags[3], lambda i, f: self.finish(i))

    def steps(self, ahead=3, lags=(0, 2, 4, 6)):
        return (self.count + 1) // 2 + ahead + lags[3]

    def drain_all(self):
        def one(t, carry):
            for first_y in (True, False):
                i = 2 * t + (0 if first_y else 1)
                pl.when(i < self.count)(functools.partial(self.drain, i, first_y))
            return carry
        lax.fori_loop(0, (self.count + 1) // 2, one, 0)


def scatter_scratch(ring, count, rows, cols):
    bf = jnp.bfloat16
    return [
        pltpu.VMEM((8, ring, 2, 2, rows, cols), bf),
        pltpu.VMEM((count, ring, 2, 2, rows, cols), bf),
        pltpu.VMEM((count, ring, 2, rows, cols), bf),
        pltpu.VMEM((count, ring, rows, cols), bf),
        pltpu.VMEM((count, ring - 1, rows, cols), bf),
        pltpu.SemaphoreType.DMA((8,)),
        pltpu.SemaphoreType.DMA((4, count)),
        pltpu.SemaphoreType.DMA((4, count)),
    ]


def scatter_pick(grads, layout, cols):
    def pick(i, p, go):
        start = 0
        for ref, (size, outer) in zip(grads, layout):
            j = i - start
            def run(ref=ref, j=j, outer=outer):
                if outer:
                    go(ref.at[j, p], ref.at[j, 1 - p])
                else:
                    at = pl.ds(pl.multiple_of(lax.rem(j, 2) * cols, cols), cols)
                    go(ref.at[p, :, :, :, j // 2, :, at], ref.at[1 - p, :, :, :, j // 2, :, at])
            pl.when((j >= 0) & (j < size))(run)
            start += size
    return pick


def scatter_kernel(ring, layout, count, *refs):
    n = len(layout)
    grads, out = refs[:n], refs[n]
    load, own, b1, b2, b3, load_sem, send_sem, recv_sem = refs[n + 1:]
    greet(group_peers(ring))
    pick = scatter_pick(grads, layout, out.shape[-1])

    def write(i, total):
        out[i] = total

    work = Scatter(ring, count, pick, (load, own, b1, b2, b3), (load_sem, send_sem, recv_sem), out, write)
    def body(t, carry):
        work.step(t)
        return carry
    lax.fori_loop(0, work.steps(), body, 0)
    work.drain_all()


def scatter(grads, layout, ring, collective_id):
    rows, cols = grads[0].shape[-2:]
    count = sum(size for size, _ in layout)
    return pl.pallas_call(
        functools.partial(scatter_kernel, ring, layout, count),
        out_shape=jax.ShapeDtypeStruct((count, rows, cols), jnp.float32),
        in_specs=[pl.BlockSpec(memory_space=pl.ANY)] * len(grads),
        out_specs=pl.BlockSpec(memory_space=pltpu.VMEM),
        scratch_shapes=scatter_scratch(ring, count, rows, cols),
        compiler_params=pltpu.CompilerParams(collective_id=collective_id, has_side_effects=True, vmem_limit_bytes=60 * 2**20),
        name="rsum",
    )(*grads)


class Gather:
    def __init__(self, ring, count, pick, sems):
        self.ring, self.count, self.pick = ring, count, pick
        self.local_sem, self.send_sem, self.recv_sem = sems
        self.p, self.c, self.h = place()
        self.hy, self.hx = self.h // 2, lax.rem(self.h, 2)
        self.core = (1 - self.p, self.c, self.h)
        self.xpeer = (self.p, self.c, self.hy * 2 + 1 - self.hx)
        self.ypeer = (self.p, self.c, (1 - self.hy) * 2 + self.hx)

    def remote(self, i, stage, src, dst, device):
        return pltpu.make_async_remote_copy(
            src_ref=src, dst_ref=dst, send_sem=self.send_sem.at[stage, i],
            recv_sem=self.recv_sem.at[stage, i], device_id=device, device_id_type=MESH)

    def same(self, i, stage, ref, device):
        return self.remote(i, stage, ref, ref, device)

    def begin(self, i, first_x):
        def go(src, out):
            mine = out(self.p, self.c, self.hy, self.hx)
            pltpu.make_async_copy(src, mine, self.local_sem.at[i]).start()
            for step in range(1, self.ring):
                peer = (self.p, lax.rem(self.c + step, self.ring), self.h)
                self.remote(i, 0, src, mine, peer).start()
        self.pick(i, go)

    def stage1(self, i, first_x):
        def go(src, out):
            mine = out(self.p, self.c, self.hy, self.hx)
            pltpu.make_async_copy(src, mine, self.local_sem.at[i]).wait()
            rest = out(self.p, pl.ds(0, self.ring - 1), self.hy, self.hx)
            pltpu.make_async_copy(rest, rest, self.recv_sem.at[0, i]).wait()
            column = out(self.p, ALL, self.hy, self.hx)
            self.same(i, 1, column, self.xpeer if first_x else self.ypeer).start()
            self.same(i, 3, column, self.core).start()
        self.pick(i, go)

    def first(self, out, mine, first_x):
        if first_x:
            return out(self.p, ALL, self.hy, self.hx if mine else 1 - self.hx)
        return out(self.p, ALL, self.hy if mine else 1 - self.hy, self.hx)

    def second(self, out, mine, first_x):
        if first_x:
            return out(self.p, ALL, self.hy if mine else 1 - self.hy, ALL)
        return out(self.p, ALL, ALL, self.hx if mine else 1 - self.hx)

    def stage2(self, i, first_x):
        def go(src, out):
            came = self.first(out, False, first_x)
            self.same(i, 1, came, self.core).wait_recv()
            self.same(i, 2, self.second(out, True, first_x), self.ypeer if first_x else self.xpeer).start()
            self.same(i, 3, came, self.core).start()
        self.pick(i, go)

    def stage3(self, i, first_x):
        def go(src, out):
            came = self.second(out, False, first_x)
            self.same(i, 2, came, self.core).wait_recv()
            self.same(i, 3, came, self.core).start()
        self.pick(i, go)

    def finish(self, i, first_x):
        def go(src, out):
            half = out(1 - self.p, ALL, ALL, ALL)
            pltpu.make_async_copy(half, half, self.recv_sem.at[3, i]).wait()
        self.pick(i, go)

    def drain(self, i, first_x):
        def go(src, out):
            rest = out(self.p, pl.ds(0, self.ring - 1), self.hy, self.hx)
            pltpu.make_async_copy(rest, rest, self.send_sem.at[0, i]).wait()
            self.same(i, 1, self.first(out, True, first_x), self.core).wait_send()
            self.same(i, 2, self.second(out, True, first_x), self.core).wait_send()
            half = out(self.p, ALL, ALL, ALL)
            pltpu.make_async_copy(half, half, self.send_sem.at[3, i]).wait()
        self.pick(i, go)

    def step(self, t, ahead=3, lags=(0, 2, 4, 6)):
        pairs = (self.count + 1) // 2
        def both(pair, act):
            for first_x in (True, False):
                i = 2 * pair + (0 if first_x else 1)
                guard = (pair >= 0) & (i < self.count) & (i >= 0)
                pl.when(guard)(functools.partial(act, i, first_x))
        both(t, self.begin)
        both(t - ahead - lags[0], self.stage1)
        both(t - ahead - lags[1], self.stage2)
        both(t - ahead - lags[2], self.stage3)
        both(t - ahead - lags[3], self.finish)

    def steps(self, ahead=3, lags=(0, 2, 4, 6)):
        return (self.count + 1) // 2 + ahead + lags[3]

    def drain_all(self):
        def one(t, carry):
            for first_x in (True, False):
                i = 2 * t + (0 if first_x else 1)
                pl.when(i < self.count)(functools.partial(self.drain, i, first_x))
            return carry
        lax.fori_loop(0, (self.count + 1) // 2, one, 0)


def gather_sems(count):
    return [
        pltpu.SemaphoreType.DMA((count,)),
        pltpu.SemaphoreType.DMA((4, count)),
        pltpu.SemaphoreType.DMA((4, count)),
    ]


def gather_pick(src, wide, down, n_wide):
    cols = src.shape[-1]
    def pick(i, go):
        @pl.when(i < n_wide)
        def _():
            go(src.at[i], lambda p, c, y, x: wide.at[i, p, c, y, x])
        @pl.when(i >= n_wide)
        def _():
            j = i - n_wide
            at = pl.ds(pl.multiple_of(lax.rem(j, 2) * cols, cols), cols)
            go(src.at[i], lambda p, c, y, x: down.at[p, c, y, x, j // 2, :, at])
    return pick


def gather_kernel(ring, n_wide, count, src, wide, down, *sems):
    greet(group_peers(ring))
    work = Gather(ring, count, gather_pick(src, wide, down, n_wide), sems)
    def body(t, carry):
        work.step(t)
        return carry
    lax.fori_loop(0, work.steps(), body, 0)
    work.drain_all()


def gather(src, n_wide, ring, collective_id):
    count, rows, cols = src.shape
    return pl.pallas_call(
        functools.partial(gather_kernel, ring, n_wide, count),
        out_shape=(
            jax.ShapeDtypeStruct((n_wide, 2, ring, 2, 2, rows, cols), src.dtype),
            jax.ShapeDtypeStruct((2, ring, 2, 2, (count - n_wide) // 2, rows, 2 * cols), src.dtype),
        ),
        in_specs=[ANY],
        out_specs=(ANY, ANY),
        scratch_shapes=gather_sems(count),
        compiler_params=pltpu.CompilerParams(collective_id=collective_id, has_side_effects=True),
        name="collect",
    )(src)


def dot_tb(a, b):
    return lax.dot_general(a, b, (((1,), (1,)), ((), ())), preferred_element_type=jnp.float32)


def dot(a, b):
    return jnp.dot(a, b, preferred_element_type=jnp.float32)


def lanes(rows):
    return lax.broadcasted_iota(jnp.int32, (rows, 128), 1)


def split3(x):
    hi = x.astype(jnp.bfloat16).astype(jnp.float32)
    mid = (x - hi).astype(jnp.bfloat16).astype(jnp.float32)
    lo = x - hi - mid
    return hi, mid, lo


def at_lanes(base, first, values):
    lane = lanes(base.shape[0])
    for n, value in enumerate(values):
        base = jnp.where(lane == first + n, value, base)
    return base


def halves(x):
    return x, pltpu.roll(x, 64, 1)


def build_keys(pair, k_ref, v_ref, kf_ref, ka, va, kt=None):
    at = pl.ds(pl.multiple_of(pair * 128, 128), 128)
    rows = k_ref.shape[0]
    chunk = 512
    def one(n, carry):
        r = pl.ds(pl.multiple_of(n * chunk, chunk), chunk)
        lane = lanes(chunk)
        keys = halves(k_ref[r, at].astype(jnp.float32))
        values = halves(v_ref[r, at].astype(jnp.float32))
        feat = kf_ref[r, :].astype(jnp.float32)
        for m in range(2):
            full = jnp.where(lane < 64, keys[m], feat)
            ka[m, r, :] = full.astype(jnp.bfloat16)
            if kt is not None:
                kt[m, :, r] = full.T.astype(jnp.bfloat16)
            ones = jnp.where(lane < 67, 1.0, 0.0)
            va[m, r, :] = jnp.where(lane < 64, values[m], ones).astype(jnp.bfloat16)
        return carry
    lax.fori_loop(0, rows // chunk, one, 0)


def forward_block(pair, n, q_ref, qf_ref, hs_ref, ka, va, o_ref, of_ref, qa_ref):
    at = pl.ds(pl.multiple_of(pair * 128, 128), 128)
    r = pl.ds(pl.multiple_of(n * QB, QB), QB)
    lane = lanes(QB)
    queries = halves(q_ref[r, at].astype(jnp.float32) * (1.0 / math.sqrt(HDIM)))
    feat = qf_ref[r, :].astype(jnp.float32)
    row = lax.broadcasted_iota(jnp.int32, (QB, QB), 0)
    col = lax.broadcasted_iota(jnp.int32, (QB, QB), 1)
    outs = []
    for m in range(2):
        qa = jnp.where(lane < 64, queries[m], feat * hs_ref[pl.ds(pair * 2 + m, 1), :])
        qb = qa.astype(jnp.bfloat16)
        def part(first, size, mask=None):
            keys = pl.ds(pl.multiple_of(n * QB + first, QB), size)
            s = dot_tb(qb, ka[m, keys, :])
            if mask is not None:
                s = jnp.where(mask, s, FAR)
            return dot(jnp.exp(s).astype(jnp.bfloat16), va[m, keys, :])
        o = part(0, QB, col >= row) + part(QB, SPAN - 2 * QB) + part(SPAN - QB, QB, col <= row)
        total = o[:, 64:65]
        outs.append(o * (1.0 / total))
        hi, mid, lo = split3(-jnp.log(total))
        qa_ref[pair * 2 + m, r, :] = at_lanes(qa, 80, (hi, mid, lo)).astype(jnp.bfloat16)
    both = jnp.where(lane < 64, outs[0], pltpu.roll(outs[1], 64, 1))
    of_ref[r, at] = both
    o_ref[r, at] = both.astype(jnp.bfloat16)


def forward_kernel(q_ref, k_ref, v_ref, kf_ref, qf_ref, hs_ref, o_ref, of_ref, qa_ref, ka, va):
    blocks = q_ref.shape[0] // QB
    def pair_step(pair, carry):
        build_keys(pair, k_ref, v_ref, kf_ref, ka, va)
        def step(n, c):
            forward_block(pair, n, q_ref, qf_ref, hs_ref, ka, va, o_ref, of_ref, qa_ref)
            return c
        lax.fori_loop(0, blocks, step, 0)
        return carry
    lax.fori_loop(0, 2, pair_step, 0)


def attention_forward(q, k, v, kf, qf, hs):
    rows, ext = q.shape[0], k.shape[0]
    return pl.pallas_call(
        forward_kernel,
        out_shape=(
            jax.ShapeDtypeStruct((rows, 256), jnp.bfloat16),
            jax.ShapeDtypeStruct((rows, 256), jnp.float32),
            jax.ShapeDtypeStruct((4, rows, 128), jnp.bfloat16),
        ),
        in_specs=[VM] * 6,
        out_specs=(VM, VM, VM),
        scratch_shapes=[pltpu.VMEM((2, ext, 128), jnp.bfloat16), pltpu.VMEM((2, ext, 128), jnp.bfloat16)],
        compiler_params=pltpu.CompilerParams(vmem_limit_bytes=56 * 2**20),
        name="attend",
    )(q, k, v, kf, qf, hs)


def backward_block(pair, n, qf_ref, qa_ref, do_ref, of_ref, ka, va, kt, dka, dva, dq_ref, same, every):
    at = pl.ds(pl.multiple_of(pair * 128, 128), 128)
    r = pl.ds(pl.multiple_of(n * QB, QB), QB)
    lane = lanes(QB)
    grads = do_ref[r, at].astype(jnp.float32)
    terms = grads * of_ref[r, at]
    pieces = halves(grads)
    row = lax.broadcasted_iota(jnp.int32, (QB, QB), 0)
    col = lax.broadcasted_iota(jnp.int32, (QB, QB), 1)
    dqs = []
    qft = qf_ref[r, :].astype(jnp.float32).T[64:72, :]
    for m in range(2):
        own = (lane < 64) if m == 0 else (lane >= 64)
        delta = jnp.sum(jnp.where(own, terms, 0.0), axis=1, keepdims=True)
        da = at_lanes(jnp.where(lane < 64, pieces[m], 0.0), 64, split3(-delta)).astype(jnp.bfloat16)
        qb = qa_ref[pair * 2 + m, r, :]
        dq = jnp.zeros((128, QB), jnp.float32)
        for first, size, edge in ((0, QB, 0), (QB, SPAN - 2 * QB, None), (SPAN - QB, QB, 1)):
            keys = pl.ds(pl.multiple_of(n * QB + first, QB), size)
            s = dot_tb(ka[m, keys, :], qb)
            if edge is not None:
                s = jnp.where((row >= col) if edge == 0 else (row <= col), s, FAR)
            p = jnp.exp(s)
            dp = dot_tb(va[m, keys, :], da)
            ds = (p * dp).astype(jnp.bfloat16)
            dva[m, keys, :] += dot(p.astype(jnp.bfloat16), da)
            dka[m, keys, :] += dot(ds, qb)
            dq = dq + dot(kt[m, :, keys], ds)
        dqs.append(dq[:64, :])
        sums = dq[64:72, :]
        pick = lax.broadcasted_iota(jnp.int32, (8, QB), 0) < 4
        h = pair * 2 + m
        same[h] += jnp.where(pick, sums * qft, 0.0)
        every[h] += jnp.where(pick, sums, 0.0)
    dq_ref[r, at] = (jnp.concatenate(dqs, axis=0).T * (1.0 / math.sqrt(HDIM))).astype(dq_ref.dtype)


def backward_finish(pair, dka, dva, dk_ref, dv_ref):
    at = pl.ds(pl.multiple_of(pair * 128, 128), 128)
    chunk = 512
    def one(n, carry):
        r = pl.ds(pl.multiple_of(n * chunk, chunk), chunk)
        lane = lanes(chunk)
        dk_ref[r, at] = jnp.where(lane < 64, dka[0, r, :], pltpu.roll(dka[1, r, :], 64, 1)).astype(dk_ref.dtype)
        dv_ref[r, at] = jnp.where(lane < 64, dva[0, r, :], pltpu.roll(dva[1, r, :], 64, 1)).astype(dv_ref.dtype)
        return carry
    lax.fori_loop(0, dk_ref.shape[0] // chunk, one, 0)


def backward_kernel(k_ref, v_ref, kf_ref, qf_ref, qa_ref, do_ref, of_ref, dq_ref, dk_ref, dv_ref, bias_ref, ka, va, kt, dka, dva, same, every):
    blocks = dq_ref.shape[0] // QB
    same[...] = jnp.zeros_like(same)
    every[...] = jnp.zeros_like(every)
    def pair_step(pair, carry):
        build_keys(pair, k_ref, v_ref, kf_ref, ka, va, kt)
        dka[...] = jnp.zeros_like(dka)
        dva[...] = jnp.zeros_like(dva)
        def step(n, c):
            backward_block(pair, n, qf_ref, qa_ref, do_ref, of_ref, ka, va, kt, dka, dva, dq_ref, same, every)
            return c
        lax.fori_loop(0, blocks, step, 0)
        backward_finish(pair, dka, dva, dk_ref, dv_ref)
        return carry
    lax.fori_loop(0, 2, pair_step, 0)
    def total(x):
        return jnp.sum(jnp.sum(x, axis=1, keepdims=True), axis=2, keepdims=True)
    s, e = total(same[...]), total(every[...])
    lane = lax.broadcasted_iota(jnp.int32, (4, 1, 128), 2)
    bias_ref[...] = jnp.where(lane == 0, s, jnp.where(lane == 1, e - s, 0.0))


def attention_backward(k, v, kf, qf, qa, do, of):
    rows, ext = do.shape[0], k.shape[0]
    f32, bf = jnp.float32, jnp.bfloat16
    return pl.pallas_call(
        backward_kernel,
        out_shape=(
            jax.ShapeDtypeStruct((rows, 256), f32),
            jax.ShapeDtypeStruct((ext, 256), f32),
            jax.ShapeDtypeStruct((ext, 256), f32),
            jax.ShapeDtypeStruct((4, 1, 128), f32),
        ),
        in_specs=[VM] * 7,
        out_specs=(VM,) * 4,
        scratch_shapes=[
            pltpu.VMEM((2, ext, 128), bf), pltpu.VMEM((2, ext, 128), bf), pltpu.VMEM((2, 128, ext), bf),
            pltpu.VMEM((2, ext, 128), f32), pltpu.VMEM((2, ext, 128), f32),
            pltpu.VMEM((4, 8, QB), f32), pltpu.VMEM((4, 8, QB), f32)],
        compiler_params=pltpu.CompilerParams(vmem_limit_bytes=60 * 2**20),
        name="attback",
    )(k, v, kf, qf, qa, do, of)


def key_features(seg_ext, var_ext):
    bf = jnp.bfloat16
    ids = jnp.arange(4)[None, :]
    var = (var_ext[:, None] == ids).astype(bf)
    seg = jnp.where(seg_ext[:, None] == ids, 0.0, FAR).astype(bf)
    n = seg_ext.shape[0]
    return jnp.concatenate([jnp.zeros((n, 64), bf), var, var, var, seg, jnp.ones((n, 3), bf), jnp.zeros((n, 45), bf)], axis=1)


def query_features(seg, var):
    bf = jnp.bfloat16
    ids = jnp.arange(4)[None, :]
    one = (var[:, None] == ids).astype(bf)
    doc = (seg[:, None] == ids).astype(bf)
    n = seg.shape[0]
    return jnp.concatenate([jnp.zeros((n, 64), bf), one, one, one, doc, jnp.zeros((n, 48), bf)], axis=1)


def head_scales(bias):
    hi, mid, lo = split3(bias[:, :1] - bias[:, 1:])
    n = bias.shape[0]
    wide = [jnp.broadcast_to(x, (n, 4)) for x in (hi, mid, lo)]
    return jnp.concatenate([jnp.zeros((n, 64))] + wide + [jnp.ones((n, 4)), jnp.zeros((n, 48))], axis=1)


def scale_of(x):
    return lax.rsqrt(jnp.mean(x * x, axis=-1, keepdims=True) + EPS)


def head_mean(x):
    row = lax.broadcasted_iota(jnp.int32, (128, 128), 0)
    col = lax.broadcasted_iota(jnp.int32, (128, 128), 1)
    group = jnp.where((row < 64) == (col < 64), 1.0 / HDIM, 0.0).astype(BF)
    hi = x.astype(BF)
    rest = x - hi.astype(F32)
    mid = rest.astype(BF)
    low = (rest - mid.astype(F32)).astype(BF)
    return dot(hi, group) + dot(mid, group) + dot(low, group)


def swap_halves(x):
    lane = lax.rem(lanes(x.shape[0]), 64)
    return jnp.where(lane < 32, pltpu.roll(x, 96, 1), pltpu.roll(x, 32, 1))


def project_kernel(x_ref, gain_ref, w_ref, cos_ref, sin_ref, hg_ref, raw_ref, out_ref, nrm):
    t = pl.program_id(0)

    @pl.when(t == 0)
    def _():
        x = x_ref[...].astype(F32)
        nrm[...] = (x * scale_of(x) * gain_ref[...]).astype(BF)

    raw = dot(nrm[...], w_ref[0]).astype(BF)
    raw_ref[...] = raw

    @pl.when(t >= 4)
    def _():
        out_ref[...] = raw

    @pl.when(t < 4)
    def _():
        gain = hg_ref[pl.ds(t // 2, 1), :]
        for n in range(raw.shape[1] // 128):
            u = raw[:, n * 128:(n + 1) * 128].astype(F32)
            y = u * lax.rsqrt(head_mean(u * u) + EPS) * gain
            y = y * cos_ref[...] + swap_halves(y) * sin_ref[...]
            out_ref[:, n * 128:(n + 1) * 128] = y.astype(BF)


def project(x, gain, wide, cosine, sine, head_gains):
    rows, width = x.shape
    def fixed(*shape):
        return pl.BlockSpec(shape, lambda t: (0,) * len(shape))
    tile = pl.BlockSpec((rows, 512), lambda t: (0, t))
    return pl.pallas_call(
        project_kernel,
        grid=(6,),
        out_shape=(jax.ShapeDtypeStruct((rows, 3 * width), BF),) * 2,
        in_specs=[fixed(rows, width), fixed(1, width), pl.BlockSpec((1, width, 512), lambda t: (t, 0, 0)),
                  fixed(rows, 128), fixed(rows, 128), fixed(2, 128)],
        out_specs=(tile, tile),
        scratch_shapes=[pltpu.VMEM((rows, width), BF)],
        compiler_params=pltpu.CompilerParams(vmem_limit_bytes=48 * MIB),
        name="project",
    )(x, gain, wide, cosine, sine, head_gains)


def norm_back_rows(u, r, gain, dy):
    scaled = dy * gain
    du = r * scaled - u * (r * r * r) * jnp.mean(scaled * u, axis=-1, keepdims=True)
    return du, jnp.sum(dy * u * r, axis=0, keepdims=True)


def ffn_kernel(x_ref, heads_ref, cot_ref, gain_ref, wo_ref, wg_ref, wu_ref, wd_ref,
               out_ref, dhid_ref, dheads_ref, gg_ref, gu_ref, gd_ref, go_ref, ggain_ref,
               hidden, acc, dnorm, nrm, nrm_t):
    t = pl.program_id(0)
    cot = cot_ref[...]

    @pl.when(t == 0)
    def _():
        heads = heads_ref[...]
        for n in range(2):
            at = slice(n * 512, (n + 1) * 512)
            hidden[:, at] = x_ref[:, at].astype(F32) + dot(heads, wo_ref[n])
        h = hidden[...]
        y = h * scale_of(h) * gain_ref[...]
        nrm[...] = y.astype(BF)
        nrm_t[...] = y.T.astype(BF)
        acc[...] = h
        dnorm[...] = jnp.zeros_like(dnorm)

    normed = nrm[...]
    wg, wu, wd = wg_ref[0], wu_ref[0], wd_ref[...]
    gate = dot(normed, wg)
    up = dot(normed, wu)
    d_product = dot_tb(cot, wd)
    sig = jax.nn.sigmoid(gate)
    silu = gate * sig
    product = silu * up
    prod_b = product.astype(BF)
    d_gate = (d_product * up * sig * (1.0 + gate * (1.0 - sig))).astype(BF)
    d_up = (d_product * silu).astype(BF)
    acc[...] += dot(prod_b, wd)
    gd_ref[...] = dot(prod_b.astype(F32).T.astype(BF), cot).astype(BF)
    gg_ref[0] = dot(nrm_t[...], d_gate).astype(BF)
    gu_ref[0] = dot(nrm_t[...], d_up).astype(BF)
    dnorm[...] += dot_tb(d_gate, wg) + dot_tb(d_up, wu)

    @pl.when(t == pl.num_programs(0) - 1)
    def _():
        out_ref[...] = acc[...].astype(BF)
        h = hidden[...]
        du, terms = norm_back_rows(h, scale_of(h), gain_ref[...], dnorm[...])
        ggain_ref[...] = terms
        d_hidden = cot_ref[...].astype(F32) + du
        dhid_ref[...] = d_hidden
        d_attn = d_hidden.astype(BF)
        heads_t = heads_ref[...].astype(F32).T.astype(BF)
        total = jnp.zeros(d_hidden.shape, F32)
        for n in range(2):
            at = slice(n * 512, (n + 1) * 512)
            go_ref[n] = dot(heads_t, d_attn[:, at]).astype(BF)
            total = total + dot_tb(d_attn[:, at], wo_ref[n])
        dheads_ref[...] = total.astype(BF)


def ffn(x, heads, cot, gain, wide, down):
    rows, width = x.shape
    ff = down.shape[0]
    steps = ff // 512
    def fixed(*shape):
        return pl.BlockSpec(shape, lambda t: (0,) * len(shape))
    def items(first):
        return pl.BlockSpec((1, width, 512), lambda t: (first + t, 0, 0))
    return pl.pallas_call(
        ffn_kernel,
        grid=(steps,),
        out_shape=(
            jax.ShapeDtypeStruct((rows, width), BF), jax.ShapeDtypeStruct((rows, width), F32),
            jax.ShapeDtypeStruct((rows, width), BF),
            jax.ShapeDtypeStruct((steps, width, 512), BF), jax.ShapeDtypeStruct((steps, width, 512), BF),
            jax.ShapeDtypeStruct((ff, width), BF), jax.ShapeDtypeStruct((2, width, 512), BF),
            jax.ShapeDtypeStruct((1, width), F32)),
        in_specs=[fixed(rows, width), fixed(rows, width), fixed(rows, width), fixed(1, width),
                  pl.BlockSpec((2, width, 512), lambda t: (0, 0, 0)), items(2), items(10),
                  pl.BlockSpec((512, width), lambda t: (t, 0))],
        out_specs=(fixed(rows, width), fixed(rows, width), fixed(rows, width), items(0), items(0),
                   pl.BlockSpec((512, width), lambda t: (t, 0)), fixed(2, width, 512), fixed(1, width)),
        scratch_shapes=[pltpu.VMEM((rows, width), F32), pltpu.VMEM((rows, width), F32), pltpu.VMEM((rows, width), F32),
                        pltpu.VMEM((rows, width), BF), pltpu.VMEM((width, rows), BF)],
        compiler_params=pltpu.CompilerParams(vmem_limit_bytes=60 * MIB),
        name="feedforward",
    )(x, heads, cot, gain, wide, wide, wide, down)


def unproject_kernel(x_ref, gain_ref, w_ref, cos_ref, sin_ref, hg_ref, raw_ref, d_ref, dhid_ref,
                     gw_ref, gin_ref, ggain_ref, ghead_ref, nrm_t, dnorm):
    t = pl.program_id(0)

    @pl.when(t == 0)
    def _():
        x = x_ref[...].astype(F32)
        nrm_t[...] = (x * scale_of(x) * gain_ref[...]).T.astype(BF)
        dnorm[...] = jnp.zeros_like(dnorm)
        ghead_ref[...] = jnp.zeros_like(ghead_ref)

    def use(d_proj):
        gw_ref[0] = dot(nrm_t[...], d_proj).astype(BF)
        dnorm[...] += dot_tb(d_proj, w_ref[0])

    @pl.when(t >= 4)
    def _():
        use(d_ref[...])

    @pl.when(t < 4)
    def _():
        kind = t // 2
        gain = hg_ref[pl.ds(kind, 1), :]
        pieces = []
        for n in range(d_ref.shape[1] // 128):
            at = slice(n * 128, (n + 1) * 128)
            u = raw_ref[:, at].astype(F32)
            dy = d_ref[:, at].astype(F32)
            dy = dy * cos_ref[...] - swap_halves(dy) * sin_ref[...]
            r = lax.rsqrt(head_mean(u * u) + EPS)
            scaled = dy * gain
            pieces.append((r * scaled - u * (r * r * r) * head_mean(scaled * u)).astype(BF))
            ghead_ref[pl.ds(kind, 1), :] += jnp.sum(dy * u * r, axis=0, keepdims=True)
        use(jnp.concatenate(pieces, axis=1))

    @pl.when(t == 5)
    def _():
        x = x_ref[...].astype(F32)
        du, terms = norm_back_rows(x, scale_of(x), gain_ref[...], dnorm[...])
        gin_ref[...] = dhid_ref[...] + du
        ggain_ref[...] = terms


def unproject(x, gain, wide, cosine, sine, head_gains, raw, grads, d_hidden):
    rows, width = x.shape
    def fixed(*shape):
        return pl.BlockSpec(shape, lambda t: (0,) * len(shape))
    tile = pl.BlockSpec((rows, 512), lambda t: (0, t))
    item = pl.BlockSpec((1, width, 512), lambda t: (t, 0, 0))
    return pl.pallas_call(
        unproject_kernel,
        grid=(6,),
        out_shape=(jax.ShapeDtypeStruct((6, width, 512), BF), jax.ShapeDtypeStruct((rows, width), F32),
                   jax.ShapeDtypeStruct((1, width), F32), jax.ShapeDtypeStruct((2, 128), F32)),
        in_specs=[fixed(rows, width), fixed(1, width), item, fixed(rows, 128), fixed(rows, 128), fixed(2, 128),
                  tile, tile, fixed(rows, width)],
        out_specs=(item, fixed(rows, width), fixed(1, width), fixed(2, 128)),
        scratch_shapes=[pltpu.VMEM((width, rows), BF), pltpu.VMEM((rows, width), F32)],
        compiler_params=pltpu.CompilerParams(vmem_limit_bytes=48 * MIB),
        name="unproject",
    )(x, gain, wide, cosine, sine, head_gains, raw, grads, d_hidden)


def remote(src, dst, send, recv, device):
    return pltpu.make_async_remote_copy(
        src_ref=src, dst_ref=dst, send_sem=send, recv_sem=recv, device_id=device, device_id_type=MESH)


def local_copy(src, dst, sem):
    return pltpu.make_async_copy(src, dst, sem)


def wide_at(first):
    return pl.ds(pl.multiple_of(first, 256), 256)


class Rim:
    def __init__(self, ring):
        self.p, self.c, self.h = place()
        self.ring = ring
        self.has_low, self.has_high = self.c > 0, self.c < ring - 1
        self.low = lax.rem(self.c + ring - 1, ring)
        self.high = lax.rem(self.c + 1, ring)
        self.low_edge = self.has_low & (self.h == 0)
        self.high_edge = self.has_high & (self.h == 3)

    def greet(self):
        beyond = [(self.p, block, n) for block in (self.low, self.high) for n in range(4)]
        greet(group_peers(self.ring) + [(self.p, self.c, 3 - self.h)] + beyond)


def attend_kernel(ring, n_wide, count, src, qkv, kf_ref, qf_ref, hs_ref,
                  tok_ref, of_ref, qa_ref, kx, vx, wide, down,
                  q_loc, o_loc, ka, va, local_sem, a2a_send, a2a_recv, rim_send, rim_recv, out_send, out_recv, *sems):
    p, c, h = place()
    rim = Rim(ring)
    rim.greet()
    rows = tok_ref.shape[0]
    width = tok_ref.shape[1]
    mine = pl.ds(pl.multiple_of(h * rows, rows), rows)
    mine_x = pl.ds(pl.multiple_of(HALF + h * rows, rows), rows)
    group = 4 * rows
    places = ((0, q_loc, mine), (1, kx, mine_x), (2, vx, mine_x))

    def part(kind, head):
        return qkv.at[:, wide_at(kind * width + head * 256)]

    for kind, ref, at in places:
        local_copy(part(kind, h), ref.at[at], local_sem.at[kind]).start()
        for step in range(1, 4):
            to = lax.rem(h + step, 4)
            remote(part(kind, to), ref.at[at], a2a_send.at[kind], a2a_recv.at[kind], (p, c, to)).start()

    low_rim, high_rim = pl.ds(0, HALF), pl.ds(HALF + group, HALF)
    for kind, ref in ((0, kx), (1, vx)):
        @pl.when(rim.high_edge)
        def _():
            for to in range(4):
                remote(part(kind + 1, to), ref.at[low_rim], rim_send.at[0, kind], rim_recv.at[0, kind], (p, rim.high, to)).start()
        @pl.when(rim.low_edge)
        def _():
            for to in range(4):
                remote(part(kind + 1, to), ref.at[high_rim], rim_send.at[1, kind], rim_recv.at[1, kind], (p, rim.low, to)).start()
        @pl.when(jnp.logical_not(rim.has_low))
        def _():
            ref[0:HALF, :] = jnp.zeros((HALF, 256), BF)
        @pl.when(jnp.logical_not(rim.has_high))
        def _():
            ref[HALF + group:2 * HALF + group, :] = jnp.zeros((HALF, 256), BF)

    work = Gather(ring, count, gather_pick(src, wide, down, n_wide), sems)
    def begin(t, carry):
        work.step(t)
        return carry
    lax.fori_loop(0, 3, begin, 0)

    three = pl.ds(0, 3 * rows)
    for kind, ref, at in places:
        local_copy(ref.at[at], ref.at[at], local_sem.at[kind]).wait()
        local_copy(ref.at[three], ref.at[three], a2a_recv.at[kind]).wait()
    for kind, ref in ((0, kx), (1, vx)):
        @pl.when(rim.has_low)
        def _():
            local_copy(ref.at[low_rim], ref.at[low_rim], rim_recv.at[0, kind]).wait()
        @pl.when(rim.has_high)
        def _():
            local_copy(ref.at[high_rim], ref.at[high_rim], rim_recv.at[1, kind]).wait()

    blocks = group // QB
    def pair_step(pair, carry):
        build_keys(pair, kx, vx, kf_ref, ka, va)
        def step(n, c):
            work.step(3 + pair * blocks + n)
            forward_block(pair, n, q_loc, qf_ref, hs_ref, ka, va, o_loc, of_ref, qa_ref)
            return c
        lax.fori_loop(0, blocks, step, 0)
        return carry
    lax.fori_loop(0, 2, pair_step, 0)

    heads = wide_at(h * 256)
    local_copy(o_loc.at[mine], tok_ref.at[:, heads], local_sem.at[3]).start()
    for step in range(1, 4):
        to = lax.rem(h + step, 4)
        theirs = pl.ds(pl.multiple_of(to * rows, rows), rows)
        remote(o_loc.at[theirs], tok_ref.at[:, heads], out_send, out_recv, (p, c, to)).start()
    def rest(t, carry):
        work.step(t)
        return carry
    lax.fori_loop(3 + 2 * blocks, work.steps(), rest, 0)
    local_copy(o_loc.at[mine], tok_ref.at[:, heads], local_sem.at[3]).wait()
    three_wide = tok_ref.at[:, pl.ds(0, 768)]
    local_copy(three_wide, three_wide, out_recv).wait()
    local_copy(three_wide, three_wide, out_send).wait()
    for kind, ref, at in places:
        local_copy(ref.at[three], ref.at[three], a2a_send.at[kind]).wait()
    for kind in range(2):
        four = qkv.at[:, pl.ds(0, 4 * 256)]
        @pl.when(rim.high_edge)
        def _():
            local_copy(four, four, rim_send.at[0, kind]).wait()
        @pl.when(rim.low_edge)
        def _():
            local_copy(four, four, rim_send.at[1, kind]).wait()
    work.drain_all()


def attend(src, qkv, kf, qf, hs, n_wide, ring, collective_id):
    rows, width = qkv.shape[0], qkv.shape[1] // 3
    group = 4 * rows
    ext = group + 2 * HALF
    count, r, w = src.shape
    dma = pltpu.SemaphoreType.DMA
    return pl.pallas_call(
        functools.partial(attend_kernel, ring, n_wide, count),
        out_shape=(
            jax.ShapeDtypeStruct((rows, width), BF),
            jax.ShapeDtypeStruct((group, 256), F32),
            jax.ShapeDtypeStruct((4, group, 128), BF),
            jax.ShapeDtypeStruct((ext, 256), BF),
            jax.ShapeDtypeStruct((ext, 256), BF),
            jax.ShapeDtypeStruct((n_wide, 2, ring, 2, 2, r, w), BF),
            jax.ShapeDtypeStruct((2, ring, 2, 2, (count - n_wide) // 2, r, 2 * w), BF),
        ),
        in_specs=[ANY, ANY, VM, VM, VM],
        out_specs=(VM,) * 5 + (ANY, ANY),
        scratch_shapes=[
            pltpu.VMEM((group, 256), BF), pltpu.VMEM((group, 256), BF),
            pltpu.VMEM((2, ext, 128), BF), pltpu.VMEM((2, ext, 128), BF),
            dma((4,)), dma((3,)), dma((3,)), dma((2, 2)), dma((2, 2)), dma, dma,
        ] + gather_sems(count),
        compiler_params=pltpu.CompilerParams(collective_id=collective_id, has_side_effects=True, vmem_limit_bytes=56 * MIB),
        name="attend",
    )(src, qkv, kf, qf, hs)


def return_kernel(ring, layout, count, *refs):
    n = len(layout)
    grads = refs[:n]
    (d_tok, kx, vx, kf_ref, qf_ref, qa_ref, of_ref, back, bias_ref, out,
     do_loc, dq_loc, dk_loc, dv_loc, rims, ka, va, kt, dka, dva, same, every,
     local_sem, in_send, in_recv, back_send, back_recv, rim_send, rim_recv,
     load, own, b1, b2, b3, load_sem, send_sem, recv_sem) = refs[n:]
    p, c, h = place()
    rim = Rim(ring)
    rim.greet()
    rows, width = d_tok.shape
    group = 4 * rows
    mine = pl.ds(pl.multiple_of(h * rows, rows), rows)
    three = pl.ds(0, 3 * rows)

    local_copy(d_tok.at[:, wide_at(h * 256)], do_loc.at[mine], local_sem.at[0]).start()
    for step in range(1, 4):
        to = lax.rem(h + step, 4)
        remote(d_tok.at[:, wide_at(to * 256)], do_loc.at[mine], in_send, in_recv, (p, c, to)).start()

    def write(i, total):
        out[i] = total

    work = Scatter(ring, count, scatter_pick(grads, layout, out.shape[-1]), (load, own, b1, b2, b3),
                   (load_sem, send_sem, recv_sem), out, write)
    def begin(t, carry):
        work.step(t)
        return carry
    lax.fori_loop(0, 3, begin, 0)
    same[...] = jnp.zeros_like(same)
    every[...] = jnp.zeros_like(every)
    local_copy(do_loc.at[mine], do_loc.at[mine], local_sem.at[0]).wait()
    local_copy(do_loc.at[three], do_loc.at[three], in_recv).wait()

    blocks = group // QB
    def pair_step(pair, carry):
        build_keys(pair, kx, vx, kf_ref, ka, va, kt)
        dka[...] = jnp.zeros_like(dka)
        dva[...] = jnp.zeros_like(dva)
        def step(m, c):
            work.step(3 + pair * blocks + m)
            backward_block(pair, m, qf_ref, qa_ref, do_loc, of_ref, ka, va, kt, dka, dva, dq_loc, same, every)
            return c
        lax.fori_loop(0, blocks, step, 0)
        backward_finish(pair, dka, dva, dk_loc, dv_loc)
        return carry
    lax.fori_loop(0, 2, pair_step, 0)

    heads = wide_at(h * 256)
    trios = ((0, dq_loc, 0), (1, dk_loc, HALF), (2, dv_loc, HALF))
    for kind, ref, skip in trios:
        at = wide_at(kind * width + h * 256)
        for step in range(4):
            to = lax.rem(h + step, 4)
            theirs = ref.at[pl.ds(pl.multiple_of(skip + to * rows, rows), rows)]
            if step == 0:
                local_copy(theirs, back.at[:, at], local_sem.at[1 + kind]).start()
            else:
                remote(theirs, back.at[:, at], back_send.at[kind], back_recv.at[kind], (p, c, to)).start()
    for kind, ref in ((0, dk_loc), (1, dv_loc)):
        @pl.when(rim.has_low)
        def _():
            remote(ref.at[pl.ds(0, HALF)], rims.at[kind, :, heads], rim_send.at[0, kind], rim_recv.at[kind], (p, rim.low, 3)).start()
        @pl.when(rim.has_high)
        def _():
            remote(ref.at[pl.ds(HALF + group, HALF)], rims.at[kind, :, heads], rim_send.at[1, kind], rim_recv.at[kind], (p, rim.high, 0)).start()

    def total(x):
        return jnp.sum(jnp.sum(x, axis=1, keepdims=True), axis=2, keepdims=True)
    s, e = total(same[...]), total(every[...])
    lane = lax.broadcasted_iota(jnp.int32, (4, 1, 128), 2)
    bias_ref[...] = jnp.where(lane == 0, s, jnp.where(lane == 1, e - s, 0.0))

    def rest(t, carry):
        work.step(t)
        return carry
    lax.fori_loop(3 + 2 * blocks, work.steps(), rest, 0)

    for kind, ref, skip in trios:
        at = wide_at(kind * width + h * 256)
        local_copy(back.at[:, at], back.at[:, at], local_sem.at[1 + kind]).wait()
        part = back.at[:, pl.ds(0, 768)]
        local_copy(part, part, back_recv.at[kind]).wait()
    for kind in range(2):
        @pl.when(rim.low_edge | rim.high_edge)
        def _():
            local_copy(rims.at[kind], rims.at[kind], rim_recv.at[kind]).wait()
            for n in range(4):
                rows_n = pl.ds(n * 128, 128)
                at = pl.ds((kind + 1) * width, width)
                back[rows_n, at] = (back[rows_n, at].astype(F32) + rims[kind, rows_n, :].astype(F32)).astype(BF)
    local_copy(do_loc.at[three], do_loc.at[three], in_send).wait()
    for kind in range(3):
        part = back.at[:, pl.ds(0, 768)]
        local_copy(part, part, back_send.at[kind]).wait()
    for kind, ref in ((0, dk_loc), (1, dv_loc)):
        rim_part = ref.at[pl.ds(0, HALF)]
        @pl.when(rim.has_low)
        def _():
            local_copy(rim_part, rim_part, rim_send.at[0, kind]).wait()
        @pl.when(rim.has_high)
        def _():
            local_copy(rim_part, rim_part, rim_send.at[1, kind]).wait()
    work.drain_all()


def attend_back(grads, layout, d_tok, kx, vx, kf, qf, qa, of, ring, collective_id):
    rows, width = d_tok.shape
    group = 4 * rows
    ext = group + 2 * HALF
    r, w = grads[0].shape[-2:]
    count = sum(size for size, _ in layout)
    dma = pltpu.SemaphoreType.DMA
    return pl.pallas_call(
        functools.partial(return_kernel, ring, layout, count),
        out_shape=(
            jax.ShapeDtypeStruct((rows, 3 * width), BF),
            jax.ShapeDtypeStruct((4, 1, 128), F32),
            jax.ShapeDtypeStruct((count, r, w), F32),
        ),
        in_specs=[ANY] * len(grads) + [ANY] + [VM] * 6,
        out_specs=(VM,) * 3,
        scratch_shapes=[
            pltpu.VMEM((group, 256), BF), pltpu.VMEM((group, 256), BF), pltpu.VMEM((ext, 256), BF), pltpu.VMEM((ext, 256), BF),
            pltpu.VMEM((2, HALF, width), BF),
            pltpu.VMEM((2, ext, 128), BF), pltpu.VMEM((2, ext, 128), BF), pltpu.VMEM((2, 128, ext), BF),
            pltpu.VMEM((2, ext, 128), F32), pltpu.VMEM((2, ext, 128), F32),
            pltpu.VMEM((4, 8, QB), F32), pltpu.VMEM((4, 8, QB), F32),
            dma((4,)), dma, dma, dma((3,)), dma((3,)), dma((2, 2)), dma((2,)),
        ] + scatter_scratch(ring, count, r, w),
        compiler_params=pltpu.CompilerParams(collective_id=collective_id, has_side_effects=True, vmem_limit_bytes=63 * MIB),
        name="attend_back",
    )(*grads, d_tok, kx, vx, kf, qf, qa, of)


def first_kernel(ring, src, gain_src, wide, gains, *sems):
    greet(group_peers(ring))
    count = src.shape[0]
    work = Gather(ring, count, lambda i, go: go(src.at[i], lambda p, c, y, x: wide.at[i, p, c, y, x]), sems[:3])
    small = Gather(ring, 1, lambda i, go: go(gain_src, lambda p, c, y, x: gains.at[p, c, y, x]), sems[3:])
    lags = (2, (0, 1, 2, 3))
    def body(t, carry):
        small.step(t, *lags)
        work.step(t, *lags)
        return carry
    lax.fori_loop(0, work.steps(*lags), body, 0)
    work.drain_all()
    small.drain_all()


def first_gather(src, gain_src, ring, collective_id):
    count, r, w = src.shape
    return pl.pallas_call(
        functools.partial(first_kernel, ring),
        out_shape=(jax.ShapeDtypeStruct((count, 2, ring, 2, 2, r, w), BF),
                   jax.ShapeDtypeStruct((2, ring, 2, 2) + gain_src.shape, BF)),
        in_specs=[ANY, ANY],
        out_specs=(ANY, ANY),
        scratch_shapes=gather_sems(count) + gather_sems(1),
        compiler_params=pltpu.CompilerParams(collective_id=collective_id, has_side_effects=True),
        name="collect",
    )(src, gain_src)


def last_kernel(ring, count, grads, small, out, small_out, sums, came, far, small_send, small_recv, *rest):
    greet(group_peers(ring))
    buffers, sems = rest[:5], rest[5:]
    def write(i, total):
        out[i] = total
    work = Scatter(ring, count, scatter_pick((grads,), ((count, True),), out.shape[-1]), buffers, sems, out, write)
    p, c, h = place()
    peers = (work.core, work.xpeer, work.ypeer)

    def hop(n):
        return remote(sums.at[n], came.at[n], small_send.at[n], small_recv.at[n], peers[n])

    def far_hop(step):
        return remote(sums.at[3], far.at[step - 1], small_send.at[3], small_recv.at[3], (p, lax.rem(c + step, ring), h))

    sums[0] = small[...]
    hop(0).start()
    def body(t, carry):
        work.step(t)
        for n in range(3):
            @pl.when(t == 2 + 2 * n)
            def _():
                hop(n).wait_recv()
                sums[n + 1] = sums[n] + came[n]
                if n < 2:
                    hop(n + 1).start()
                else:
                    for step in range(1, ring):
                        far_hop(step).start()
        return carry
    lax.fori_loop(0, work.steps(), body, 0)
    local_copy(far, far, small_recv.at[3]).wait()
    total = sums[3]
    for step in range(1, ring):
        total = total + far[step - 1]
    small_out[...] = total
    for n in range(3):
        hop(n).wait_send()
    local_copy(far, far, small_send.at[3]).wait()
    work.drain_all()


def last_scatter(grads, small, ring, collective_id):
    count = grads.shape[0]
    r, w = grads.shape[-2:]
    n = small.shape[0]
    dma = pltpu.SemaphoreType.DMA
    return pl.pallas_call(
        functools.partial(last_kernel, ring, count),
        out_shape=(jax.ShapeDtypeStruct((count, r, w), F32), jax.ShapeDtypeStruct((n, 128), F32)),
        in_specs=[ANY, VM],
        out_specs=(VM, VM),
        scratch_shapes=[pltpu.VMEM((4, n, 128), F32), pltpu.VMEM((3, n, 128), F32), pltpu.VMEM((ring - 1, n, 128), F32),
                        dma((4,)), dma((4,))] + scatter_scratch(ring, count, r, w),
        compiler_params=pltpu.CompilerParams(collective_id=collective_id, has_side_effects=True, vmem_limit_bytes=40 * MIB),
        name="rsum",
    )(grads, small)


def edges(ids, ring):
    up = [(i, i + 1) for i in range(ring - 1)]
    down = [(i + 1, i) for i in range(ring - 1)]
    below = lax.ppermute(ids[:, -HALF:] + 1, "cp", up) - 1
    above = lax.ppermute(ids[:, :HALF] + 1, "cp", down) - 1
    return jnp.concatenate([below, ids, above], axis=1)


def local(
    inputs, cotangent, w_qkv, w_out, w_gate, w_up, w_down, gain_attn, gain_ffn, q_gain, k_gain, head_bias,
    segment_ids, variate_ids, time_index,
):
    ring = lax.axis_size("cp")
    head = lax.axis_index("hd")
    rows, width = inputs.shape
    depth = w_qkv.shape[0]
    r, w = item_shape(depth)

    def pieces(weight):
        return weight.reshape(depth, -1, 512).swapaxes(0, 1).reshape(-1, r, w)

    first = pieces(w_qkv)
    down_pieces = w_down.reshape(4, r, 2, w).swapaxes(1, 2).reshape(8, r, w)
    second = jnp.concatenate([pieces(w_out), pieces(w_gate), pieces(w_up), down_pieces])
    gain_src = jnp.pad(jnp.stack([gain_attn, gain_ffn]), ((0, 14), (0, 128 - depth)))
    qkv_wide, gains = first_gather(first, gain_src, ring, 0)
    qkv_wide = qkv_wide.reshape(-1, width, 512)
    gains = gains[..., :2, :depth].reshape(-1, 2, depth).swapaxes(0, 1).reshape(2, 1, width).astype(F32)

    times = lax.dynamic_slice_in_dim(time_index, head * rows, rows, 0)
    frequency = jnp.exp(-math.log(theta_base) * 2.0 * jnp.arange(HDIM // 2, dtype=jnp.float32) / HDIM)
    angle = times.astype(F32)[:, None] * frequency[None, :]
    cosine, sine = jnp.cos(angle), jnp.sin(angle)
    cosine = jnp.concatenate([cosine] * 4, axis=1)
    sine = jnp.concatenate([-sine, sine, -sine, sine], axis=1)
    head_gains = jnp.stack([jnp.concatenate([q_gain, q_gain]), jnp.concatenate([k_gain, k_gain])])

    ids = edges(jnp.stack([segment_ids, variate_ids]), ring)
    kf = key_features(ids[0], ids[1])
    qf = query_features(segment_ids, variate_ids)
    hs = head_scales(lax.dynamic_slice_in_dim(head_bias, head * 4, 4, 0))

    raw, rotated = project(inputs, gains[0], qkv_wide, cosine, sine, head_gains)
    heads_out, of, qa, kx, vx, wide, down = attend(second, rotated, kf, qf, hs, 18, ring, 1)
    layer_out, d_hidden, d_heads, g_gate, g_up, g_down, g_out, g_gffn = ffn(
        inputs, heads_out, cotangent, gains[1], wide.reshape(-1, width, 512), down.reshape(-1, width))

    def blocks(grad):
        return grad.reshape(-1, 2, ring, 2, 2, r, w)

    grads = (blocks(g_out), blocks(g_gate), blocks(g_up), g_down.reshape(2, ring, 2, 2, 4, r, 2 * w))
    layout = ((2, True), (8, True), (8, True), (8, False))
    d_proj, g_bias, items = attend_back(grads, layout, d_heads, kx, vx, kf, qf, qa, of, ring, 2)
    g_qkv, grad_inputs, g_gattn, g_heads = unproject(
        inputs, gains[0], qkv_wide, cosine, sine, head_gains, raw, d_proj, d_hidden)
    bias_all = lax.dynamic_update_slice_in_dim(jnp.zeros((HEADS, 2), F32), g_bias[:, 0, :2], head * 4, 0)
    small = jnp.concatenate([
        g_gattn.reshape(8, 128), g_gffn.reshape(8, 128), g_heads,
        jnp.pad(bias_all.reshape(1, 32), ((0, 5), (0, 96)))])
    last, small = last_scatter(blocks(g_qkv), small, ring, 3)

    def columns(part):
        return part.reshape(-1, depth, 512).swapaxes(0, 1).reshape(depth, -1)

    me = (lax.axis_index("pack") * ring + lax.axis_index("cp")) * 4 + head
    own_gains = lax.dynamic_slice_in_dim(small[:16].reshape(2, width), me * depth, depth, 1)
    own_heads = small[16:18, :HDIM] + small[16:18, HDIM:]
    return (
        layer_out, grad_inputs, columns(last), columns(items[:2]), columns(items[2:10]), columns(items[10:18]),
        items[18:].reshape(4, 2, r, w).swapaxes(1, 2).reshape(w_down.shape),
        own_gains[0], own_gains[1], own_heads[0], own_heads[1], small[18, :32].reshape(HEADS, 2),
    )


def solution(mesh):
    return jax.shard_map(
        local,
        mesh=mesh,
        in_specs=(
            P(("pack", "cp", "hd"), None),
            P(("pack", "cp", "hd"), None),
            P(("pack", "cp", "hd"), None),
            P(("pack", "cp", "hd"), None),
            P(("pack", "cp", "hd"), None),
            P(("pack", "cp", "hd"), None),
            P(("pack", "cp", "hd"), None),
            P(("pack", "cp", "hd")),
            P(("pack", "cp", "hd")),
            P(),
            P(),
            P(),
            P(("pack", "cp")),
            P(("pack", "cp")),
            P(("pack", "cp")),
        ),
        out_specs=(
            P(("pack", "cp", "hd"), None),
            P(("pack", "cp", "hd"), None),
            P(("pack", "cp", "hd"), None),
            P(("pack", "cp", "hd"), None),
            P(("pack", "cp", "hd"), None),
            P(("pack", "cp", "hd"), None),
            P(("pack", "cp", "hd"), None),
            P(("pack", "cp", "hd")),
            P(("pack", "cp", "hd")),
            P(),
            P(),
            P(),
        ),
        check_vma=False,
    )
```

time: 1220 us -> 622 us (0.51); the launches traced: 1200 us -> 621 us
  Pallas kernels: 159 us -> 571 us
  local copies, waits for them, and re-layouts: 384 us -> 31.9 us
  matrix products: 256 us -> 0 us
  waiting for transfers between devices: 125 us -> 0.01 us
  other arithmetic: 93.9 us -> 10.5 us
  blocking collectives: 81.5 us -> 0 us
  starting transfers between devices: 51.3 us -> 6.85 us
  loops' own time: 37.5 us -> 0 us
  between operations: 15.2 us -> 1.02 us
    pallas_call x1 -> x7, Pallas kernels: 159 us -> 571 us  [the longest x1 198 us: attend(): pl.pallas_call(functools.partial(attend_kernel, ring, n_wide, count), out...]
    dot_general x43 -> x0, matrix products: 256 us -> none  [the longest x8 59.7 us: block_scores(): jnp.einsum('qhd,khd->hqk', q_blk, k_blk, preferred_element_type=jnp.float32)]
    dynamic_update_slice x21 -> x1, local copies, waits for them, and re-layouts: 127 us -> 0.68 us  [local(): lax.dynamic_update_slice_in_dim(jnp.zeros((HEADS, 2), F32), g_bias[:, 0,...]
    all_gather x5 -> x0, waiting for transfers between devices: 84.7 us -> none  [the longest x1 57.6 us: local(): lax.all_gather(w_down, ('pack', 'cp', 'hd'), axis=0, tiled=True)]
    unnamed x2 -> x0, blocking collectives: 81.5 us -> none
    reshape x13 -> x10, local copies, waits for them, and re-layouts: 66.2 us -> 5.04 us  [the longest x4 3.11 us: columns(): return part.reshape(-1, depth, 512).swapaxes(0, 1).reshape(depth, -1)]
    reduce_sum x15 -> x0, other arithmetic: 51.6 us -> none  [the longest x4 31.1 us: backward_block(): same_total = jnp.sum(jnp.where(same_var[None], d_wide, 0.0), axis=(1, 2))]
    mul x22 -> x0, local copies, waits for them, and re-layouts: 45.3 us -> none  [the longest x12 27.7 us: norm_back(): values * inv_rms ** 3 * jnp.mean(scaled * values, axis=-1, keepdims=True)]
  transfers between devices with their start and end apart: 19 -> 2, of which waited for: 8 -> 0; matrix products, arithmetic and copies ran while one was open for 29% -> 3% of each run, Pallas kernels for 0% -> 9%
where the time goes in v2:
time: 622 us; the launch traced here: 621 us
  Pallas kernels  571 us (92%)
  local copies, waits for them, and re-layouts  31.9 us (5%)
  other arithmetic  10.5 us (2%)
  starting transfers between devices  6.85 us (1%)
    pallas_call x1, Pallas kernels, attend(): pl.pallas_call(functools.partial(attend_kernel, ring, n_wide, count), out...  198 us
    pallas_call x1, Pallas kernels, attend_back(): pl.pallas_call(functools.partial(return_kernel, ring, layout, count), out...  189 us
    pallas_call x1, Pallas kernels, ffn(): pl.pallas_call(ffn_kernel, grid=(steps,), out_shape=(jax.ShapeDtypeStruct...  56.5 us
    pallas_call x1, Pallas kernels, last_scatter(): pl.pallas_call(functools.partial(last_kernel, ring, count), out_shape=(ja...  51.8 us
    pallas_call x1, Pallas kernels, first_gather(): pl.pallas_call(functools.partial(first_kernel, ring), out_shape=(jax.Shap...  45.3 us
    pallas_call x1, Pallas kernels, unproject(): pl.pallas_call(unproject_kernel, grid=(6,), out_shape=(jax.ShapeDtypeStru...  18.8 us
  transfers between devices with their start and end apart: 2, of which 0 were waited for; matrix products, arithmetic and copies ran while one was open for 3% of the time, Pallas kernels for 9%

profile of v2, /device:TPU:0, one launch (start us, length us, event | category | flops | bytes accessed | tf_op | source)
XLA Modules:
  0.0 620.9 jit_solution(4580865455889924532)
XLA Ops:
  0.7 0.8 add_add_fusion
  1.5 1.3 collective-permute-start.1
  2.8 5.6 collective-permute-start
  8.4 2.1 fusion.1
  10.6 1.6 copy.77
  12.2 1.3 fusion.9.gain_src
  13.5 45.3 %collect.1 = (bf16[6,2,4,2,2,32,512]{6,5,4,3,2,1,0:T(8,128)(2,1)}, bf16[2,4,2,2,16,128]{5,4,3,2,1,0:T(8,128)(2,1)}) custom-call(bf16[6,32,512]{2,1,0:T(8,128)(2,1)} %bitcast.106, bf16[16,128]{1,0:T(8,128)(2,1)} %fusion.9.gain_src), custom_call_target="tpu_custom_call" | custom-call | tf_op jit(solution)/shard_map/collect/pallas_call | solution.py:1119
  58.8 0.9 slice.69
  60.8 1.0 fusion.3
  62.5 1.0 pad_maximum_fusion.src
  64.2 0.9 broadcast_in_dim.64
  65.1 0.9 broadcast_in_dim.65
  66.0 3.9 concatenate.37.qf_ref.refs_8_
  69.8 11.6 %project.1 = (bf16[512,3072]{1,0:T(8,128)(2,1)S(1)}, bf16[512,3072]{1,0:T(8,128)(2,1)}) custom-call(bf16[512,1024]{1,0:T(8,128)(2,1)S(1)} %copy-done.2, f32[1,1024]{1,0:T(1,128)S(1)} %squeeze.22.gain_ref, bf16[6,1024,512]{2,1,0:T(8,128)(2,1)} %bitcast.96, f32[512,128]{1,0:T(8,128)S(1)} %get-tuple-element.126.cos_ref, ...), custom_call_target="tpu_custom_call" | custom-call | tf_op jit(solution)/shard_map/project/pallas_call | solution.py:650
  81.4 1.6 copy-done.5
  84.0 1.4 fusion
  85.4 1.4 select_convert_fusion
  86.9 1.0 broadcast_in_dim.62
  87.9 1.0 broadcast_in_dim.63
  88.9 5.4 concatenate.36.kf_ref.refs_7_
  94.3 197.7 %attend.1 = (bf16[512,1024]{1,0:T(8,128)(2,1)}, f32[2048,256]{1,0:T(8,128)}, bf16[4,2048,128]{2,1,0:T(8,128)(2,1)}, bf16[3072,256]{1,0:T(8,128)(2,1)}, bf16[3072...) custom-call(bf16[26,32,512]{2,1,0:T(8,128)(2,1)} %pad_maximum_fusion.src, ...), custom_call_target="tpu_custom_call" | custom-call | tf_op jit(solution)/shard_map/attend/pallas_call | solution.py:944
  292.0 56.5 %feedforward.1 = (bf16[512,1024]{1,0:T(8,128)(2,1)}, f32[512,1024]{1,0:T(8,128)}, bf16[512,1024]{1,0:T(8,128)(2,1)}, bf16[8,1024,512]{2,1,0:T(8,128)(2,1)}, bf16...) custom-call(bf16[512,1024]{1,0:T(8,128)(2,1)} %x_ref.5, ...), custom_call_target="tpu_custom_call" | custom-call | tf_op jit(solution)/shard_map/feedforward/pallas_call | solution.py:731
  348.4 188.9 %attend_back.1 = (bf16[512,3072]{1,0:T(8,128)(2,1)}, f32[4,1,128]{2,1,0:T(1,128)}, f32[26,32,512]{2,1,0:T(8,128)}) custom-call(bf16[2,2,4,2,2,32,512]{6,5,4,3,2,1,0:T(8,128)(2,1)} %bitcast.102, bf16[8,2,4,2,2,32,512]{6,5,4,3,2,1,0:T(8,128)(2,1)} %bitcast.99, bf16[8,2,4,2,2,32,512]{6,5,4,3,2,1,0:T(8,128)(2,1)} %bitcast.100, ...), custom_call_target="tpu_custom_call" | custom-call | tf_op jit(solution)/shard_map/attend_back/pallas_call | solution.py:1080
  538.2 1.2 copy-done.3
  539.4 1.6 copy-done.6
  541.0 18.8 %unproject.1 = (bf16[6,1024,512]{2,1,0:T(8,128)(2,1)}, f32[512,1024]{1,0:T(8,128)}, f32[1,1024]{1,0:T(1,128)S(1)}, f32[2,128]{1,0:T(2,128)S(1)}) custom-call(bf16[512,1024]{1,0:T(8,128)(2,1)S(1)} %copy-done.3, f32[1,1024]{1,0:T(1,128)S(1)} %squeeze.22.gain_ref, bf16[6,1024,512]{2,1,0:T(8,128)(2,1)} %bitcast.97, f32[512,128]{1,0:T(8,128)S(1)} %get-tuple-element.126.cos_ref, ...), custom_call_target="tpu_custom_call" | custom-call | tf_op jit(solution)/shard_map/unproject/pallas_call | solution.py:801
  559.8 2.8 copy-done.4
  562.5 51.8 %rsum.1 = (f32[6,32,512]{2,1,0:T(8,128)S(1)}, f32[24,128]{1,0:T(8,128)S(1)}) custom-call(bf16[6,2,4,2,2,32,512]{6,5,4,3,2,1,0:T(8,128)(2,1)S(1)} %bitcast.90, f32[24,128]{1,0:T(8,128)S(1)} %select_maximum_fusion.small), custom_call_target="tpu_custom_call" | custom-call | tf_op jit(solution)/shard_map/rsum/pallas_call | solution.py:1178
  614.6 0.8 copy.67
  617.7 0.9 copy.71
  618.6 0.8 copy.69
  619.4 0.8 copy.70
  (78 shorter events, 7.5 us)
Async XLA Ops:
  0.6 59.1 %copy-start = (f32[16,2]{0,1:T(2,128)S(1)}, f32[16,2]{0,1:T(2,128)}, u32[]{:S(2)}) copy-start(f32[16,2]{0,1:T(2,128)} %param.26) | copy-start | bytes 388
  0.7 59.2 %copy-start.8 = (bf16[128,1024]{1,0:T(8,128)(2,1)S(1)}, bf16[128,1024]{1,0:T(8,128)(2,1)}, u32[]{:S(2)}) copy-start(bf16[128,1024]{1,0:T(8,128)(2,1)} %param.21) | copy-start | bytes 786436
  0.7 59.4 %copy-start.13 = (bf16[32,1024]{1,0:T(8,128)(2,1)S(1)}, bf16[32,1024]{1,0:T(8,128)(2,1)}, u32[]{:S(2)}) copy-start(bf16[32,1024]{1,0:T(8,128)(2,1)} %param.18) | copy-start | bytes 196612
  0.7 61.2 %copy-start.15 = (f32[64]{0:T(128)S(1)}, f32[64]{0:T(128)}, u32[]{:S(2)}) copy-start(f32[64]{0:T(128)} %param.24) | copy-start | bytes 772
  0.7 61.2 %copy-start.16 = (f32[64]{0:T(128)S(1)}, f32[64]{0:T(128)}, u32[]{:S(2)}) copy-start(f32[64]{0:T(128)} %param.25) | copy-start | bytes 772
  0.7 61.2 %copy-start.10 = (bf16[32,4096]{1,0:T(8,128)(2,1)S(1)}, bf16[32,4096]{1,0:T(8,128)(2,1)}, u32[]{:S(2)}) copy-start(bf16[32,4096]{1,0:T(8,128)(2,1)} %param.19) | copy-start | bytes 786436
  0.7 61.2 %copy-start.9 = (bf16[32,4096]{1,0:T(8,128)(2,1)S(1)}, bf16[32,4096]{1,0:T(8,128)(2,1)}, u32[]{:S(2)}) copy-start(bf16[32,4096]{1,0:T(8,128)(2,1)} %param.20) | copy-start | bytes 786436
  1.5 82.3 %collective-permute-start.1 = (s32[2,512]{1,0:T(2,128)S(1)}, s32[2,512]{1,0:T(2,128)S(1)}, u32[]{:S(2)}, u32[]{:S(2)}) collective-permute-start(s32[2,512]{1,0:T(2,128)S(1)} %get-tuple-element.114), channel_id=1, source_target_pairs={{4,0},{8,4},{12,8},{5,1},{9,5},{13,9},{6,2},{10,6},{14,10},{7,3},{... | collective-permute-start | bytes 12296 | tf_op jit(solution)/shard_map/ppermute | solution.py:1194
  2.8 81.1 %collective-permute-start = (s32[2,512]{1,0:T(2,128)S(1)}, s32[2,512]{1,0:T(2,128)S(1)}, u32[]{:S(2)}, u32[]{:S(2)}) collective-permute-start(s32[2,512]{1,0:T(2,128)S(1)} %get-tuple-element.113), channel_id=1, source_target_pairs={{0,4},{4,8},{8,12},{1,5},{5,9},{9,13},{2,6},{6,10},{10,14},{3,7},{... | collective-permute-start | bytes 12296 | tf_op jit(solution)/shard_map/ppermute | solution.py:1193
  65.1 4.7 copy-start.2
  69.8 14.1 %copy-start.11 = (s32[2048]{0:T(1024)S(1)}, s32[2048]{0:T(1024)}, u32[]{:S(2)}) copy-start(s32[2048]{0:T(1024)} %param.28) | copy-start | bytes 24580
  69.8 14.1 %copy-start.12 = (s32[2048]{0:T(1024)S(1)}, s32[2048]{0:T(1024)}, u32[]{:S(2)}) copy-start(s32[2048]{0:T(1024)} %param.27) | copy-start | bytes 24580
  81.4 1.6 copy-start.5
  538.2 1.2 copy-start.3
  539.4 1.6 copy-start.6
  541.0 18.8 %copy-start.14 = (f32[1,1024]{1,0:T(1,128)S(1)}, f32[1,1024]{1,0:T(1,128)}, u32[]{:S(2)}) copy-start(f32[1,1024]{1,0:T(1,128)} %get-tuple-element.62) | copy-start | bytes 12292
  559.8 2.8 copy-start.4
  562.5 52.0 %copy-start.7 = (f32[26,32,512]{2,1,0:T(8,128)S(1)}, f32[26,32,512]{2,1,0:T(8,128)}, u32[]{:S(2)}) copy-start(f32[26,32,512]{2,1,0:T(8,128)} %get-tuple-element.66) | copy-start | bytes 5111812
  617.3 3.6 copy-start.1

commit v3 on v2

--- a/solution.py
+++ b/solution.py
@@ -89,12 +89,18 @@
             self.copy0(i, other).start()
         self.pick(i, self.p, go)
 
-    def stage1(self, i, first_y):
+    def mine(self, i, k):
+        return self.load[lax.rem(i, self.slots), k]
+
+    def landed(self, i):
         slot = lax.rem(i, self.slots)
         pltpu.make_async_copy(self.load.at[slot], self.load.at[slot], self.load_sem.at[slot]).wait()
+
+    def stage1(self, i, first_y):
+        self.landed(i)
         self.copy0(i, self.own.at[i]).wait_recv()
         def add(k, carry):
-            self.own[i, k] = self.own[i, k] + self.load[slot, k]
+            self.own[i, k] = self.own[i, k] + self.mine(i, k)
             return carry
         lax.fori_loop(0, self.ring, add, 0)
         self.copy1(i, first_y).start()
@@ -157,10 +163,31 @@
         lax.fori_loop(0, (self.count + 1) // 2, one, 0)
 
 
-def scatter_scratch(ring, count, rows, cols):
+class StagedScatter(Scatter):
+    def begin(self, i):
+        self.copy0(i, self.load.at[lax.rem(i, self.slots), 1 - self.p]).start()
+
+    def mine(self, i, k):
+        return self.load[lax.rem(i, self.slots), self.p, k]
+
+    def landed(self, i):
+        pass
+
+    def reuse(self, i):
+        self.copy0(i, self.own.at[i]).wait_send()
+
+    def drain(self, i, first_y):
+        pl.when(i >= self.count - self.slots)(lambda: self.reuse(i))
+        self.copy1(i, first_y).wait_send()
+        self.copy2(i, first_y).wait_send()
+        pltpu.make_async_copy(self.b3.at[i], self.b3.at[i], self.send_sem.at[3, i]).wait()
+
+
+def scatter_scratch(ring, count, rows, cols, staged=0):
     bf = jnp.bfloat16
+    load = (staged, 2) if staged else (8,)
     return [
-        pltpu.VMEM((8, ring, 2, 2, rows, cols), bf),
+        pltpu.VMEM(load + (ring, 2, 2, rows, cols), bf),
         pltpu.VMEM((count, ring, 2, 2, rows, cols), bf),
         pltpu.VMEM((count, ring, 2, rows, cols), bf),
         pltpu.VMEM((count, ring, rows, cols), bf),
@@ -401,7 +428,7 @@
     return x, pltpu.roll(x, 64, 1)
 
 
-def build_keys(pair, k_ref, v_ref, kf_ref, ka, va, kt=None):
+def build_keys(pair, k_ref, v_ref, kf_ref, ka, va, kt=None, first=0, last=None):
     at = pl.ds(pl.multiple_of(pair * 128, 128), 128)
     rows = k_ref.shape[0]
     chunk = 512
@@ -419,7 +446,7 @@
             ones = jnp.where(lane < 67, 1.0, 0.0)
             va[m, r, :] = jnp.where(lane < 64, values[m], ones).astype(jnp.bfloat16)
         return carry
-    lax.fori_loop(0, rows // chunk, one, 0)
+    lax.fori_loop(first, rows // chunk if last is None else last, one, 0)
 
 
 def forward_block(pair, n, q_ref, qf_ref, hs_ref, ka, va, o_ref, of_ref, qa_ref):
@@ -448,35 +475,6 @@
     both = jnp.where(lane < 64, outs[0], pltpu.roll(outs[1], 64, 1))
     of_ref[r, at] = both
     o_ref[r, at] = both.astype(jnp.bfloat16)
-
-
-def forward_kernel(q_ref, k_ref, v_ref, kf_ref, qf_ref, hs_ref, o_ref, of_ref, qa_ref, ka, va):
-    blocks = q_ref.shape[0] // QB
-    def pair_step(pair, carry):
-        build_keys(pair, k_ref, v_ref, kf_ref, ka, va)
-        def step(n, c):
-            forward_block(pair, n, q_ref, qf_ref, hs_ref, ka, va, o_ref, of_ref, qa_ref)
-            return c
-        lax.fori_loop(0, blocks, step, 0)
-        return carry
-    lax.fori_loop(0, 2, pair_step, 0)
-
-
-def attention_forward(q, k, v, kf, qf, hs):
-    rows, ext = q.shape[0], k.shape[0]
-    return pl.pallas_call(
-        forward_kernel,
-        out_shape=(
-            jax.ShapeDtypeStruct((rows, 256), jnp.bfloat16),
-            jax.ShapeDtypeStruct((rows, 256), jnp.float32),
-            jax.ShapeDtypeStruct((4, rows, 128), jnp.bfloat16),
-        ),
-        in_specs=[VM] * 6,
-        out_specs=(VM, VM, VM),
-        scratch_shapes=[pltpu.VMEM((2, ext, 128), jnp.bfloat16), pltpu.VMEM((2, ext, 128), jnp.bfloat16)],
-        compiler_params=pltpu.CompilerParams(vmem_limit_bytes=56 * 2**20),
-        name="attend",
-    )(q, k, v, kf, qf, hs)
 
 
 def backward_block(pair, n, qf_ref, qa_ref, do_ref, of_ref, ka, va, kt, dka, dva, dq_ref, same, every):
@@ -528,73 +526,21 @@
     lax.fori_loop(0, dk_ref.shape[0] // chunk, one, 0)
 
 
-def backward_kernel(k_ref, v_ref, kf_ref, qf_ref, qa_ref, do_ref, of_ref, dq_ref, dk_ref, dv_ref, bias_ref, ka, va, kt, dka, dva, same, every):
-    blocks = dq_ref.shape[0] // QB
-    same[...] = jnp.zeros_like(same)
-    every[...] = jnp.zeros_like(every)
-    def pair_step(pair, carry):
-        build_keys(pair, k_ref, v_ref, kf_ref, ka, va, kt)
-        dka[...] = jnp.zeros_like(dka)
-        dva[...] = jnp.zeros_like(dva)
-        def step(n, c):
-            backward_block(pair, n, qf_ref, qa_ref, do_ref, of_ref, ka, va, kt, dka, dva, dq_ref, same, every)
-            return c
-        lax.fori_loop(0, blocks, step, 0)
-        backward_finish(pair, dka, dva, dk_ref, dv_ref)
-        return carry
-    lax.fori_loop(0, 2, pair_step, 0)
-    def total(x):
-        return jnp.sum(jnp.sum(x, axis=1, keepdims=True), axis=2, keepdims=True)
-    s, e = total(same[...]), total(every[...])
-    lane = lax.broadcasted_iota(jnp.int32, (4, 1, 128), 2)
-    bias_ref[...] = jnp.where(lane == 0, s, jnp.where(lane == 1, e - s, 0.0))
-
-
-def attention_backward(k, v, kf, qf, qa, do, of):
-    rows, ext = do.shape[0], k.shape[0]
-    f32, bf = jnp.float32, jnp.bfloat16
-    return pl.pallas_call(
-        backward_kernel,
-        out_shape=(
-            jax.ShapeDtypeStruct((rows, 256), f32),
-            jax.ShapeDtypeStruct((ext, 256), f32),
-            jax.ShapeDtypeStruct((ext, 256), f32),
-            jax.ShapeDtypeStruct((4, 1, 128), f32),
-        ),
-        in_specs=[VM] * 7,
-        out_specs=(VM,) * 4,
-        scratch_shapes=[
-            pltpu.VMEM((2, ext, 128), bf), pltpu.VMEM((2, ext, 128), bf), pltpu.VMEM((2, 128, ext), bf),
-            pltpu.VMEM((2, ext, 128), f32), pltpu.VMEM((2, ext, 128), f32),
-            pltpu.VMEM((4, 8, QB), f32), pltpu.VMEM((4, 8, QB), f32)],
-        compiler_params=pltpu.CompilerParams(vmem_limit_bytes=60 * 2**20),
-        name="attback",
-    )(k, v, kf, qf, qa, do, of)
-
-
-def key_features(seg_ext, var_ext):
-    bf = jnp.bfloat16
-    ids = jnp.arange(4)[None, :]
-    var = (var_ext[:, None] == ids).astype(bf)
-    seg = jnp.where(seg_ext[:, None] == ids, 0.0, FAR).astype(bf)
-    n = seg_ext.shape[0]
-    return jnp.concatenate([jnp.zeros((n, 64), bf), var, var, var, seg, jnp.ones((n, 3), bf), jnp.zeros((n, 45), bf)], axis=1)
-
-
-def query_features(seg, var):
-    bf = jnp.bfloat16
-    ids = jnp.arange(4)[None, :]
-    one = (var[:, None] == ids).astype(bf)
-    doc = (seg[:, None] == ids).astype(bf)
-    n = seg.shape[0]
-    return jnp.concatenate([jnp.zeros((n, 64), bf), one, one, one, doc, jnp.zeros((n, 48), bf)], axis=1)
+def features(seg, var):
+    lane = jnp.arange(128)[None, :]
+    same = (var[:, None] == (lane - 64) % 4) & (lane >= 64) & (lane < 76)
+    doc = (lane >= 76) & (lane < 80)
+    here = seg[:, None] == lane - 76
+    keys = jnp.where(doc & ~here, FAR, jnp.where(same | ((lane >= 80) & (lane < 83)), 1.0, 0.0))
+    queries = jnp.where(same | (doc & here), 1.0, 0.0)
+    return queries.astype(jnp.bfloat16), keys.astype(jnp.bfloat16)
 
 
 def head_scales(bias):
     hi, mid, lo = split3(bias[:, :1] - bias[:, 1:])
-    n = bias.shape[0]
-    wide = [jnp.broadcast_to(x, (n, 4)) for x in (hi, mid, lo)]
-    return jnp.concatenate([jnp.zeros((n, 64))] + wide + [jnp.ones((n, 4)), jnp.zeros((n, 48))], axis=1)
+    lane = jnp.arange(128)[None, :]
+    parts = jnp.where(lane < 68, hi, jnp.where(lane < 72, mid, lo))
+    return jnp.where(lane < 64, 0.0, jnp.where(lane < 76, parts, jnp.where(lane < 80, 1.0, 0.0)))
 
 
 def scale_of(x):
@@ -617,63 +563,41 @@
     return jnp.where(lane < 32, pltpu.roll(x, 96, 1), pltpu.roll(x, 32, 1))
 
 
-def project_kernel(x_ref, gain_ref, w_ref, cos_ref, sin_ref, hg_ref, raw_ref, out_ref, nrm):
-    t = pl.program_id(0)
-
-    @pl.when(t == 0)
-    def _():
-        x = x_ref[...].astype(F32)
-        nrm[...] = (x * scale_of(x) * gain_ref[...]).astype(BF)
-
-    raw = dot(nrm[...], w_ref[0]).astype(BF)
-    raw_ref[...] = raw
-
-    @pl.when(t >= 4)
-    def _():
-        out_ref[...] = raw
-
-    @pl.when(t < 4)
-    def _():
-        gain = hg_ref[pl.ds(t // 2, 1), :]
-        for n in range(raw.shape[1] // 128):
-            u = raw[:, n * 128:(n + 1) * 128].astype(F32)
-            y = u * lax.rsqrt(head_mean(u * u) + EPS) * gain
-            y = y * cos_ref[...] + swap_halves(y) * sin_ref[...]
-            out_ref[:, n * 128:(n + 1) * 128] = y.astype(BF)
-
-
-def project(x, gain, wide, cosine, sine, head_gains):
-    rows, width = x.shape
-    def fixed(*shape):
-        return pl.BlockSpec(shape, lambda t: (0,) * len(shape))
-    tile = pl.BlockSpec((rows, 512), lambda t: (0, t))
-    return pl.pallas_call(
-        project_kernel,
-        grid=(6,),
-        out_shape=(jax.ShapeDtypeStruct((rows, 3 * width), BF),) * 2,
-        in_specs=[fixed(rows, width), fixed(1, width), pl.BlockSpec((1, width, 512), lambda t: (t, 0, 0)),
-                  fixed(rows, 128), fixed(rows, 128), fixed(2, 128)],
-        out_specs=(tile, tile),
-        scratch_shapes=[pltpu.VMEM((rows, width), BF)],
-        compiler_params=pltpu.CompilerParams(vmem_limit_bytes=48 * MIB),
-        name="project",
-    )(x, gain, wide, cosine, sine, head_gains)
-
-
 def norm_back_rows(u, r, gain, dy):
     scaled = dy * gain
     du = r * scaled - u * (r * r * r) * jnp.mean(scaled * u, axis=-1, keepdims=True)
     return du, jnp.sum(dy * u * r, axis=0, keepdims=True)
 
 
-def ffn_kernel(x_ref, heads_ref, cot_ref, gain_ref, wo_ref, wg_ref, wu_ref, wd_ref,
-               out_ref, dhid_ref, dheads_ref, gg_ref, gu_ref, gd_ref, go_ref, ggain_ref,
-               hidden, acc, dnorm, nrm, nrm_t):
+def as_blocks(value, shape):
+    rows, cols = shape[-2:]
+    if cols == value.shape[1]:
+        return value.astype(BF).reshape(shape)
+    depth = rows * cols // value.shape[1]
+    parts = value.reshape(-1, depth, value.shape[1])
+    parts = [parts[:, :, n:n + cols] for n in range(0, value.shape[1], cols)]
+    return jnp.concatenate(parts, axis=1).astype(BF).reshape(shape)
+
+
+FFN_LAGS = (1, (0, 1, 2, 4))
+SLOTS = 6
+
+
+def ffn_kernel(ring, x_ref, heads_ref, cot_ref, gain_ref, wo_ref, wg_ref, wu_ref, wd_ref,
+               out_ref, dhid_ref, dheads_ref, gd_ref, go_ref, ggain_ref, sums_ref,
+               hidden, acc, nrm, nrm_t, load, own, b1, b2, b3, load_sem, send_sem, recv_sem):
     t = pl.program_id(0)
+    steps = pl.num_programs(0)
     cot = cot_ref[...]
+
+    def write(i, total):
+        sums_ref[i] = total
+
+    work = StagedScatter(ring, own.shape[0], None, (load, own, b1, b2, b3), (load_sem, send_sem, recv_sem), sums_ref, write)
 
     @pl.when(t == 0)
     def _():
+        greet(group_peers(ring))
         heads = heads_ref[...]
         for n in range(2):
             at = slice(n * 512, (n + 1) * 512)
@@ -683,7 +607,7 @@
         nrm[...] = y.astype(BF)
         nrm_t[...] = y.T.astype(BF)
         acc[...] = h
-        dnorm[...] = jnp.zeros_like(dnorm)
+        dhid_ref[...] = jnp.zeros_like(dhid_ref)
 
     normed = nrm[...]
     wg, wu, wd = wg_ref[0], wu_ref[0], wd_ref[...]
@@ -696,20 +620,28 @@
     prod_b = product.astype(BF)
     d_gate = (d_product * up * sig * (1.0 + gate * (1.0 - sig))).astype(BF)
     d_up = (d_product * silu).astype(BF)
+    slot = lax.rem(2 * t, SLOTS)
+    @pl.when(t >= SLOTS // 2)
+    def _():
+        work.reuse(2 * t - SLOTS)
+        work.reuse(2 * t + 1 - SLOTS)
+    load[slot] = as_blocks(dot(nrm_t[...], d_gate), load.shape[1:])
+    load[slot + 1] = as_blocks(dot(nrm_t[...], d_up), load.shape[1:])
+    work.step(t, *FFN_LAGS)
     acc[...] += dot(prod_b, wd)
     gd_ref[...] = dot(prod_b.astype(F32).T.astype(BF), cot).astype(BF)
-    gg_ref[0] = dot(nrm_t[...], d_gate).astype(BF)
-    gu_ref[0] = dot(nrm_t[...], d_up).astype(BF)
-    dnorm[...] += dot_tb(d_gate, wg) + dot_tb(d_up, wu)
-
-    @pl.when(t == pl.num_programs(0) - 1)
+    dhid_ref[...] += dot_tb(d_gate, wg) + dot_tb(d_up, wu)
+
+    @pl.when(t == steps - 1)
     def _():
+        work.step(t + 1, *FFN_LAGS)
         out_ref[...] = acc[...].astype(BF)
         h = hidden[...]
-        du, terms = norm_back_rows(h, scale_of(h), gain_ref[...], dnorm[...])
+        du, terms = norm_back_rows(h, scale_of(h), gain_ref[...], dhid_ref[...])
         ggain_ref[...] = terms
         d_hidden = cot_ref[...].astype(F32) + du
         dhid_ref[...] = d_hidden
+        work.step(t + 2, *FFN_LAGS)
         d_attn = d_hidden.astype(BF)
         heads_t = heads_ref[...].astype(F32).T.astype(BF)
         total = jnp.zeros(d_hidden.shape, F32)
@@ -718,33 +650,41 @@
             go_ref[n] = dot(heads_t, d_attn[:, at]).astype(BF)
             total = total + dot_tb(d_attn[:, at], wo_ref[n])
         dheads_ref[...] = total.astype(BF)
-
-
-def ffn(x, heads, cot, gain, wide, down):
+        def rest(n, carry):
+            work.step(n, *FFN_LAGS)
+            return carry
+        lax.fori_loop(t + 3, work.steps(*FFN_LAGS), rest, 0)
+        work.drain_all()
+
+
+def ffn(x, heads, cot, gain, wide, down, ring, item, collective_id):
     rows, width = x.shape
     ff = down.shape[0]
     steps = ff // 512
+    once = pl.Buffered(1)
     def fixed(*shape):
+        return pl.BlockSpec(shape, lambda t: (0,) * len(shape), pipeline_mode=once)
+    def out(*shape):
         return pl.BlockSpec(shape, lambda t: (0,) * len(shape))
     def items(first):
         return pl.BlockSpec((1, width, 512), lambda t: (first + t, 0, 0))
     return pl.pallas_call(
-        ffn_kernel,
+        functools.partial(ffn_kernel, ring),
         grid=(steps,),
         out_shape=(
             jax.ShapeDtypeStruct((rows, width), BF), jax.ShapeDtypeStruct((rows, width), F32),
             jax.ShapeDtypeStruct((rows, width), BF),
-            jax.ShapeDtypeStruct((steps, width, 512), BF), jax.ShapeDtypeStruct((steps, width, 512), BF),
             jax.ShapeDtypeStruct((ff, width), BF), jax.ShapeDtypeStruct((2, width, 512), BF),
-            jax.ShapeDtypeStruct((1, width), F32)),
+            jax.ShapeDtypeStruct((1, width), F32), jax.ShapeDtypeStruct((2 * steps,) + item, F32)),
         in_specs=[fixed(rows, width), fixed(rows, width), fixed(rows, width), fixed(1, width),
-                  pl.BlockSpec((2, width, 512), lambda t: (0, 0, 0)), items(2), items(10),
+                  pl.BlockSpec((2, width, 512), lambda t: (3, 0, 0), pipeline_mode=once), items(8), items(16),
                   pl.BlockSpec((512, width), lambda t: (t, 0))],
-        out_specs=(fixed(rows, width), fixed(rows, width), fixed(rows, width), items(0), items(0),
-                   pl.BlockSpec((512, width), lambda t: (t, 0)), fixed(2, width, 512), fixed(1, width)),
-        scratch_shapes=[pltpu.VMEM((rows, width), F32), pltpu.VMEM((rows, width), F32), pltpu.VMEM((rows, width), F32),
-                        pltpu.VMEM((rows, width), BF), pltpu.VMEM((width, rows), BF)],
-        compiler_params=pltpu.CompilerParams(vmem_limit_bytes=60 * MIB),
+        out_specs=(VM, VM, VM,
+                   pl.BlockSpec((512, width), lambda t: (t, 0)), VM, VM, VM),
+        scratch_shapes=[pltpu.VMEM((rows, width), F32), pltpu.VMEM((rows, width), F32),
+                        pltpu.VMEM((rows, width), BF), pltpu.VMEM((width, rows), BF)]
+        + scatter_scratch(ring, 2 * steps, item[0], item[1], SLOTS),
+        compiler_params=pltpu.CompilerParams(collective_id=collective_id, has_side_effects=True, vmem_limit_bytes=62 * MIB),
         name="feedforward",
     )(x, heads, cot, gain, wide, wide, wide, down)
 
@@ -840,103 +780,189 @@
         greet(group_peers(self.ring) + [(self.p, self.c, 3 - self.h)] + beyond)
 
 
-def attend_kernel(ring, n_wide, count, src, qkv, kf_ref, qf_ref, hs_ref,
-                  tok_ref, of_ref, qa_ref, kx, vx, wide, down,
-                  q_loc, o_loc, ka, va, local_sem, a2a_send, a2a_recv, rim_send, rim_recv, out_send, out_recv, *sems):
+def pair_at(first, pair):
+    return pl.ds(pl.multiple_of(first + pair * 128, 128), 128)
+
+
+LAGS = (2, (0, 1, 2, 3))
+
+
+def as_matrix(value):
+    rows, cols = value.shape[-2:]
+    if cols == 512:
+        return value.reshape(-1, 512)
+    depth = rows * cols // 512
+    parts = value.astype(F32).reshape(-1, rows, cols)
+    parts = [parts[:, n:n + depth] for n in range(0, rows, depth)]
+    return jnp.concatenate(parts, axis=2).reshape(-1, 512).astype(BF)
+
+
+def attend_kernel(ring, n_wide, count, x_ref, cos_ref, sin_ref, hg_ref, kf_own, qf_ref, hs_ref, src, gain_src,
+                  tok_ref, of_ref, qa_ref, kx, vx, kf_ref, raw_ref, gain_ref, wide, down,
+                  rot, nrm, w_tile, gains, q_loc, o_loc, ka, va, tile_sem, local_sem, a2a_send, a2a_recv, rim_send, rim_recv,
+                  kf_send, kf_recv, out_send, out_recv, *sems):
     p, c, h = place()
     rim = Rim(ring)
-    rim.greet()
-    rows = tok_ref.shape[0]
-    width = tok_ref.shape[1]
+    greet(group_peers(ring) + [(p, c, 3 - h)])
+    rows, width = tok_ref.shape
+    group = 4 * rows
     mine = pl.ds(pl.multiple_of(h * rows, rows), rows)
     mine_x = pl.ds(pl.multiple_of(HALF + h * rows, rows), rows)
-    group = 4 * rows
     places = ((0, q_loc, mine), (1, kx, mine_x), (2, vx, mine_x))
-
-    def part(kind, head):
-        return qkv.at[:, wide_at(kind * width + head * 256)]
-
-    for kind, ref, at in places:
-        local_copy(part(kind, h), ref.at[at], local_sem.at[kind]).start()
-        for step in range(1, 4):
-            to = lax.rem(h + step, 4)
-            remote(part(kind, to), ref.at[at], a2a_send.at[kind], a2a_recv.at[kind], (p, c, to)).start()
-
-    low_rim, high_rim = pl.ds(0, HALF), pl.ds(HALF + group, HALF)
-    for kind, ref in ((0, kx), (1, vx)):
-        @pl.when(rim.high_edge)
+    three = pl.ds(0, 3 * rows)
+    sides = ((rim.has_high, rim.high, group, 0), (rim.has_low, rim.low, HALF, HALF + group))
+
+    small = Gather(ring, 1, lambda i, go: go(gain_src, lambda p, c, y, x: gains.at[p, c, y, x]), sems[:3])
+    work = Gather(ring, count, gather_pick(src, wide, down, n_wide), sems[3:])
+
+    def kf_copy(side):
+        there, block, first, to = sides[side]
+        return remote(kf_own.at[pl.ds(first - HALF * side if side else first - HALF, HALF)], kf_ref.at[pl.ds(to, HALF)],
+                      kf_send.at[side], kf_recv.at[side], (p, block, h))
+
+    def begin(t, carry):
+        small.step(t, *LAGS)
+        work.step(t, *LAGS)
+        return carry
+    lax.fori_loop(0, 2, begin, 0)
+    for side in range(2):
+        pl.when(sides[side][0])(lambda: kf_copy(side).start())
+    kf_ref[HALF:HALF + group, :] = kf_own[...]
+    lane = lax.broadcasted_iota(jnp.int32, (HALF, 128), 1)
+    nothing = jnp.where((lane >= 76) & (lane < 80), FAR, 0.0).astype(BF)
+    @pl.when(jnp.logical_not(rim.has_low))
+    def _():
+        kf_ref[0:HALF, :] = nothing
+        for ref in (kx, vx):
+            ref[0:HALF, :] = jnp.zeros((HALF, 256), BF)
+    @pl.when(jnp.logical_not(rim.has_high))
+    def _():
+        kf_ref[HALF + group:2 * HALF + group, :] = nothing
+        for ref in (kx, vx):
+            ref[HALF + group:2 * HALF + group, :] = jnp.zeros((HALF, 256), BF)
+    lax.fori_loop(2, 5, begin, 0)
+
+    def share(kind, head, pair):
+        ref, at = places[kind][1:]
+        cols = pair_at(0, pair)
+        part = rot.at[:, pair_at(kind * width + head * 256, pair)]
+        there = ref.at[at, cols]
+        @pl.when(head == h)
         def _():
-            for to in range(4):
-                remote(part(kind + 1, to), ref.at[low_rim], rim_send.at[0, kind], rim_recv.at[0, kind], (p, rim.high, to)).start()
-        @pl.when(rim.low_edge)
+            local_copy(part, there, local_sem.at[kind, pair]).start()
+        @pl.when(head != h)
         def _():
-            for to in range(4):
-                remote(part(kind + 1, to), ref.at[high_rim], rim_send.at[1, kind], rim_recv.at[1, kind], (p, rim.low, to)).start()
-        @pl.when(jnp.logical_not(rim.has_low))
-        def _():
-            ref[0:HALF, :] = jnp.zeros((HALF, 256), BF)
-        @pl.when(jnp.logical_not(rim.has_high))
-        def _():
-            ref[HALF + group:2 * HALF + group, :] = jnp.zeros((HALF, 256), BF)
-
-    work = Gather(ring, count, gather_pick(src, wide, down, n_wide), sems)
-    def begin(t, carry):
-        work.step(t)
-        return carry
-    lax.fori_loop(0, 3, begin, 0)
-
-    three = pl.ds(0, 3 * rows)
-    for kind, ref, at in places:
-        local_copy(ref.at[at], ref.at[at], local_sem.at[kind]).wait()
-        local_copy(ref.at[three], ref.at[three], a2a_recv.at[kind]).wait()
-    for kind, ref in ((0, kx), (1, vx)):
-        @pl.when(rim.has_low)
-        def _():
-            local_copy(ref.at[low_rim], ref.at[low_rim], rim_recv.at[0, kind]).wait()
-        @pl.when(rim.has_high)
-        def _():
-            local_copy(ref.at[high_rim], ref.at[high_rim], rim_recv.at[1, kind]).wait()
+            remote(part, there, a2a_send.at[kind, pair], a2a_recv.at[kind, pair], (p, c, head)).start()
+
+    def tile_copy(t):
+        return local_copy(wide.at[t], w_tile.at[lax.rem(t, 2)], tile_sem.at[lax.rem(t, 2)])
+
+    for k in range(3):
+        begin(5 + k, 0)
+        for m in range(2):
+            tile_copy(2 * k + m).start()
+        if k == 0:
+            total = gains[0, 0, 0, 0].astype(F32)
+            for d in range(1, 8 * ring):
+                total = total + gains[d // (4 * ring), d // 4 % ring, d // 2 % 2, d % 2].astype(F32)
+            gain_ref[...] = total
+            def norm(n, carry):
+                at = pl.ds(pl.multiple_of(n * 128, 128), 128)
+                x = x_ref[at, :].astype(F32)
+                y = x * scale_of(x)
+                for m in range(width // 128):
+                    part = slice(m * 128, (m + 1) * 128)
+                    nrm[at, part] = (y[:, part] * total[m:m + 1, :]).astype(BF)
+                return carry
+            lax.fori_loop(0, rows // 128, norm, 0)
+        for m in range(2):
+            t = 2 * k + m
+            tile_copy(t).wait()
+            def project(n, carry):
+                at = pl.ds(pl.multiple_of(n * 128, 128), 128)
+                raw = dot(nrm[at, :], as_matrix(w_tile[t % 2])).astype(BF)
+                if t < 4:
+                    raw_ref[at, t * 512:(t + 1) * 512] = raw
+                    gain = hg_ref[t // 2:t // 2 + 1, :]
+                    for m in range(4):
+                        u = raw[:, m * 128:(m + 1) * 128].astype(F32)
+                        y = u * lax.rsqrt(head_mean(u * u) + EPS) * gain
+                        y = y * cos_ref[at, :] + swap_halves(y) * sin_ref[at, :]
+                        rot[at, t * 512 + m * 128:t * 512 + (m + 1) * 128] = y.astype(BF)
+                else:
+                    rot[at, t * 512:(t + 1) * 512] = raw
+                return carry
+            lax.fori_loop(0, rows // 128, project, 0)
+            for pair in range(2):
+                for m2 in range(2):
+                    share(t // 2, t % 2 * 2 + m2, pair)
+
+    def rim_copy(ref, side, kind, pair):
+        there, block, first, to = sides[side]
+        return remote(ref.at[pl.ds(first, HALF), pair_at(0, pair)], ref.at[pl.ds(to, HALF), pair_at(0, pair)],
+                      rim_send.at[side, kind, pair], rim_recv.at[side, kind, pair], (p, block, h))
 
     blocks = group // QB
+    margin = HALF // QB
     def pair_step(pair, carry):
-        build_keys(pair, kx, vx, kf_ref, ka, va)
+        cols = pair_at(0, pair)
+        for kind, ref, at in places:
+            local_copy(ref.at[at, cols], ref.at[at, cols], local_sem.at[kind, pair]).wait()
+            local_copy(ref.at[three, cols], ref.at[three, cols], a2a_recv.at[kind, pair]).wait()
+        for side in range(2):
+            @pl.when(sides[side][0])
+            def _():
+                for kind, ref in ((0, kx), (1, vx)):
+                    rim_copy(ref, side, kind, pair).start()
+        build_keys(pair, kx, vx, kf_ref, ka, va, None, 1, 1 + group // HALF)
         def step(n, c):
-            work.step(3 + pair * blocks + n)
-            forward_block(pair, n, q_loc, qf_ref, hs_ref, ka, va, o_loc, of_ref, qa_ref)
+            work.step(8 + pair * blocks + n, *LAGS)
+            forward_block(pair, lax.rem(n + margin, blocks), q_loc, qf_ref, hs_ref, ka, va, o_loc, of_ref, qa_ref)
             return c
-        lax.fori_loop(0, blocks, step, 0)
+        lax.fori_loop(0, blocks - 2 * margin, step, 0)
+        for side in range(2):
+            @pl.when(sides[1 - side][0])
+            def _():
+                for kind, ref in ((0, kx), (1, vx)):
+                    rim_copy(ref, side, kind, pair).wait_recv()
+                pl.when(pair == 0)(lambda: kf_copy(side).wait_recv())
+        build_keys(pair, kx, vx, kf_ref, ka, va, None, 0, 1)
+        build_keys(pair, kx, vx, kf_ref, ka, va, None, 1 + group // HALF, 2 + group // HALF)
+        lax.fori_loop(blocks - 2 * margin, blocks, step, 0)
+        to_cols = pair_at(h * 256, pair)
+        local_copy(o_loc.at[mine, cols], tok_ref.at[:, to_cols], local_sem.at[3, pair]).start()
+        for step_ in range(1, 4):
+            to = lax.rem(h + step_, 4)
+            theirs = pl.ds(pl.multiple_of(to * rows, rows), rows)
+            remote(o_loc.at[theirs, cols], tok_ref.at[:, to_cols], out_send.at[pair], out_recv.at[pair], (p, c, to)).start()
         return carry
     lax.fori_loop(0, 2, pair_step, 0)
 
-    heads = wide_at(h * 256)
-    local_copy(o_loc.at[mine], tok_ref.at[:, heads], local_sem.at[3]).start()
-    for step in range(1, 4):
-        to = lax.rem(h + step, 4)
-        theirs = pl.ds(pl.multiple_of(to * rows, rows), rows)
-        remote(o_loc.at[theirs], tok_ref.at[:, heads], out_send, out_recv, (p, c, to)).start()
     def rest(t, carry):
-        work.step(t)
+        work.step(t, *LAGS)
         return carry
-    lax.fori_loop(3 + 2 * blocks, work.steps(), rest, 0)
-    local_copy(o_loc.at[mine], tok_ref.at[:, heads], local_sem.at[3]).wait()
-    three_wide = tok_ref.at[:, pl.ds(0, 768)]
-    local_copy(three_wide, three_wide, out_recv).wait()
-    local_copy(three_wide, three_wide, out_send).wait()
-    for kind, ref, at in places:
-        local_copy(ref.at[three], ref.at[three], a2a_send.at[kind]).wait()
-    for kind in range(2):
-        four = qkv.at[:, pl.ds(0, 4 * 256)]
-        @pl.when(rim.high_edge)
-        def _():
-            local_copy(four, four, rim_send.at[0, kind]).wait()
-        @pl.when(rim.low_edge)
-        def _():
-            local_copy(four, four, rim_send.at[1, kind]).wait()
+    lax.fori_loop(8 + 2 * blocks, jnp.maximum(8 + 2 * blocks, work.steps(*LAGS)), rest, 0)
+    for pair in range(2):
+        cols = pair_at(0, pair)
+        local_copy(o_loc.at[mine, cols], tok_ref.at[:, pair_at(h * 256, pair)], local_sem.at[3, pair]).wait()
+        part = tok_ref.at[:, pl.ds(0, 384)]
+        local_copy(part, part, out_recv.at[pair]).wait()
+        local_copy(part, part, out_send.at[pair]).wait()
+        for kind, ref, at in places:
+            local_copy(ref.at[three, cols], ref.at[three, cols], a2a_send.at[kind, pair]).wait()
+        for side in range(2):
+            @pl.when(sides[side][0])
+            def _():
+                for kind, ref in ((0, kx), (1, vx)):
+                    rim_copy(ref, side, kind, pair).wait_send()
+                if pair == 0:
+                    kf_copy(side).wait_send()
+    small.drain_all()
     work.drain_all()
 
 
-def attend(src, qkv, kf, qf, hs, n_wide, ring, collective_id):
-    rows, width = qkv.shape[0], qkv.shape[1] // 3
+def attend(x, cosine, sine, head_gains, kf, qf, hs, src, gain_src, n_wide, ring, collective_id):
+    rows, width = x.shape
     group = 4 * rows
     ext = group + 2 * HALF
     count, r, w = src.shape
@@ -949,19 +975,24 @@
             jax.ShapeDtypeStruct((4, group, 128), BF),
             jax.ShapeDtypeStruct((ext, 256), BF),
             jax.ShapeDtypeStruct((ext, 256), BF),
+            jax.ShapeDtypeStruct((ext, 128), BF),
+            jax.ShapeDtypeStruct((rows, 2 * width), BF),
+            jax.ShapeDtypeStruct((16, 128), F32),
             jax.ShapeDtypeStruct((n_wide, 2, ring, 2, 2, r, w), BF),
             jax.ShapeDtypeStruct((2, ring, 2, 2, (count - n_wide) // 2, r, 2 * w), BF),
         ),
-        in_specs=[ANY, ANY, VM, VM, VM],
-        out_specs=(VM,) * 5 + (ANY, ANY),
+        in_specs=[VM] * 7 + [ANY, ANY],
+        out_specs=(VM,) * 8 + (ANY, ANY),
         scratch_shapes=[
+            pltpu.VMEM((rows, 3 * width), BF), pltpu.VMEM((rows, width), BF), pltpu.VMEM((2, 2, ring, 2, 2, r, w), BF),
+            pltpu.VMEM((2, ring, 2, 2, 16, 128), BF),
             pltpu.VMEM((group, 256), BF), pltpu.VMEM((group, 256), BF),
             pltpu.VMEM((2, ext, 128), BF), pltpu.VMEM((2, ext, 128), BF),
-            dma((4,)), dma((3,)), dma((3,)), dma((2, 2)), dma((2, 2)), dma, dma,
-        ] + gather_sems(count),
-        compiler_params=pltpu.CompilerParams(collective_id=collective_id, has_side_effects=True, vmem_limit_bytes=56 * MIB),
+            dma((2,)), dma((4, 2)), dma((3, 2)), dma((3, 2)), dma((2, 2, 2)), dma((2, 2, 2)), dma((2,)), dma((2,)), dma((2,)), dma((2,)),
+        ] + gather_sems(1) + gather_sems(count),
+        compiler_params=pltpu.CompilerParams(collective_id=collective_id, has_side_effects=True, vmem_limit_bytes=60 * MIB),
         name="attend",
-    )(src, qkv, kf, qf, hs)
+    )(x, cosine, sine, head_gains, kf, qf, hs, src, gain_src)
 
 
 def return_kernel(ring, layout, count, *refs):
@@ -973,16 +1004,17 @@
      load, own, b1, b2, b3, load_sem, send_sem, recv_sem) = refs[n:]
     p, c, h = place()
     rim = Rim(ring)
-    rim.greet()
+    greet(group_peers(ring) + [(p, c, 3 - h)])
     rows, width = d_tok.shape
     group = 4 * rows
     mine = pl.ds(pl.multiple_of(h * rows, rows), rows)
     three = pl.ds(0, 3 * rows)
-
-    local_copy(d_tok.at[:, wide_at(h * 256)], do_loc.at[mine], local_sem.at[0]).start()
-    for step in range(1, 4):
-        to = lax.rem(h + step, 4)
-        remote(d_tok.at[:, wide_at(to * 256)], do_loc.at[mine], in_send, in_recv, (p, c, to)).start()
+    for pair in range(2):
+        cols = pair_at(0, pair)
+        local_copy(d_tok.at[:, pair_at(h * 256, pair)], do_loc.at[mine, cols], local_sem.at[0, pair]).start()
+        for step in range(1, 4):
+            to = lax.rem(h + step, 4)
+            remote(d_tok.at[:, pair_at(to * 256, pair)], do_loc.at[mine, cols], in_send.at[pair], in_recv.at[pair], (p, c, to)).start()
 
     def write(i, total):
         out[i] = total
@@ -995,78 +1027,102 @@
     lax.fori_loop(0, 3, begin, 0)
     same[...] = jnp.zeros_like(same)
     every[...] = jnp.zeros_like(every)
-    local_copy(do_loc.at[mine], do_loc.at[mine], local_sem.at[0]).wait()
-    local_copy(do_loc.at[three], do_loc.at[three], in_recv).wait()
+
+    trios = ((0, dq_loc, 0), (1, dk_loc, HALF), (2, dv_loc, HALF))
+    kinds = ((0, dk_loc), (1, dv_loc))
+    sides = ((rim.has_high, rim.high, HALF + group), (rim.has_low, rim.low, 0))
+
+    def rim_copy(ref, side, kind, pair):
+        there, block, first = sides[side]
+        cols = pair_at(0, pair)
+        return remote(ref.at[pl.ds(first, HALF), cols], rims.at[side, kind, :, cols],
+                      rim_send.at[side, kind, pair], rim_recv.at[side, kind, pair], (p, block, h))
+
+    def give(kind, pair, wanted):
+        _, ref, skip = trios[kind]
+        cols, at = pair_at(0, pair), pair_at(kind * width + h * 256, pair)
+        for step in range(4):
+            to = lax.rem(h + step, 4)
+            theirs = ref.at[pl.ds(pl.multiple_of(skip + to * rows, rows), rows), cols]
+            def go():
+                if step == 0:
+                    local_copy(theirs, back.at[:, at], local_sem.at[1 + kind, pair]).start()
+                else:
+                    remote(theirs, back.at[:, at], back_send.at[kind, pair], back_recv.at[kind, pair], (p, c, to)).start()
+            if wanted is None:
+                go()
+            else:
+                edge = (to == 0) | (to == 3)
+                pl.when(edge if wanted else jnp.logical_not(edge))(go)
+
+    def edges_back(pair):
+        cols = pair_at(0, pair)
+        for side in range(2):
+            first = HALF if side == 0 else group
+            @pl.when(sides[1 - side][0])
+            def _():
+                for kind, ref in kinds:
+                    rim_copy(ref, side, kind, pair).wait_recv()
+                    for m in range(4):
+                        to = pl.ds(first + m * 128, 128)
+                        more = rims[side, kind, pl.ds(m * 128, 128), cols].astype(F32)
+                        ref[to, cols] = (ref[to, cols].astype(F32) + more).astype(BF)
+        give(1, pair, True)
+        give(2, pair, True)
 
     blocks = group // QB
     def pair_step(pair, carry):
+        cols = pair_at(0, pair)
         build_keys(pair, kx, vx, kf_ref, ka, va, kt)
         dka[...] = jnp.zeros_like(dka)
         dva[...] = jnp.zeros_like(dva)
+        local_copy(do_loc.at[mine, cols], do_loc.at[mine, cols], local_sem.at[0, pair]).wait()
+        local_copy(do_loc.at[three, cols], do_loc.at[three, cols], in_recv.at[pair]).wait()
         def step(m, c):
             work.step(3 + pair * blocks + m)
             backward_block(pair, m, qf_ref, qa_ref, do_loc, of_ref, ka, va, kt, dka, dva, dq_loc, same, every)
             return c
-        lax.fori_loop(0, blocks, step, 0)
+        lax.fori_loop(0, blocks // 2, step, 0)
+        pl.when(pair == 1)(lambda: edges_back(0))
+        lax.fori_loop(blocks // 2, blocks, step, 0)
         backward_finish(pair, dka, dva, dk_loc, dv_loc)
+        for side in range(2):
+            @pl.when(sides[side][0])
+            def _():
+                for kind, ref in kinds:
+                    rim_copy(ref, side, kind, pair).start()
+        give(1, pair, False)
+        give(2, pair, False)
+        give(0, pair, None)
         return carry
     lax.fori_loop(0, 2, pair_step, 0)
-
-    heads = wide_at(h * 256)
-    trios = ((0, dq_loc, 0), (1, dk_loc, HALF), (2, dv_loc, HALF))
-    for kind, ref, skip in trios:
-        at = wide_at(kind * width + h * 256)
-        for step in range(4):
-            to = lax.rem(h + step, 4)
-            theirs = ref.at[pl.ds(pl.multiple_of(skip + to * rows, rows), rows)]
-            if step == 0:
-                local_copy(theirs, back.at[:, at], local_sem.at[1 + kind]).start()
-            else:
-                remote(theirs, back.at[:, at], back_send.at[kind], back_recv.at[kind], (p, c, to)).start()
-    for kind, ref in ((0, dk_loc), (1, dv_loc)):
-        @pl.when(rim.has_low)
-        def _():
-            remote(ref.at[pl.ds(0, HALF)], rims.at[kind, :, heads], rim_send.at[0, kind], rim_recv.at[kind], (p, rim.low, 3)).start()
-        @pl.when(rim.has_high)
-        def _():
-            remote(ref.at[pl.ds(HALF + group, HALF)], rims.at[kind, :, heads], rim_send.at[1, kind], rim_recv.at[kind], (p, rim.high, 0)).start()
 
     def total(x):
         return jnp.sum(jnp.sum(x, axis=1, keepdims=True), axis=2, keepdims=True)
     s, e = total(same[...]), total(every[...])
     lane = lax.broadcasted_iota(jnp.int32, (4, 1, 128), 2)
     bias_ref[...] = jnp.where(lane == 0, s, jnp.where(lane == 1, e - s, 0.0))
+    edges_back(1)
 
     def rest(t, carry):
         work.step(t)
         return carry
-    lax.fori_loop(3 + 2 * blocks, work.steps(), rest, 0)
-
-    for kind, ref, skip in trios:
-        at = wide_at(kind * width + h * 256)
-        local_copy(back.at[:, at], back.at[:, at], local_sem.at[1 + kind]).wait()
-        part = back.at[:, pl.ds(0, 768)]
-        local_copy(part, part, back_recv.at[kind]).wait()
-    for kind in range(2):
-        @pl.when(rim.low_edge | rim.high_edge)
-        def _():
-            local_copy(rims.at[kind], rims.at[kind], rim_recv.at[kind]).wait()
-            for n in range(4):
-                rows_n = pl.ds(n * 128, 128)
-                at = pl.ds((kind + 1) * width, width)
-                back[rows_n, at] = (back[rows_n, at].astype(F32) + rims[kind, rows_n, :].astype(F32)).astype(BF)
-    local_copy(do_loc.at[three], do_loc.at[three], in_send).wait()
-    for kind in range(3):
-        part = back.at[:, pl.ds(0, 768)]
-        local_copy(part, part, back_send.at[kind]).wait()
-    for kind, ref in ((0, dk_loc), (1, dv_loc)):
-        rim_part = ref.at[pl.ds(0, HALF)]
-        @pl.when(rim.has_low)
-        def _():
-            local_copy(rim_part, rim_part, rim_send.at[0, kind]).wait()
-        @pl.when(rim.has_high)
-        def _():
-            local_copy(rim_part, rim_part, rim_send.at[1, kind]).wait()
+    lax.fori_loop(3 + 2 * blocks, jnp.maximum(3 + 2 * blocks, work.steps()), rest, 0)
+
+    part = back.at[:, pl.ds(0, 384)]
+    for pair in range(2):
+        cols = pair_at(0, pair)
+        for kind in range(3):
+            at = pair_at(kind * width + h * 256, pair)
+            local_copy(back.at[:, at], back.at[:, at], local_sem.at[1 + kind, pair]).wait()
+            local_copy(part, part, back_recv.at[kind, pair]).wait()
+            local_copy(part, part, back_send.at[kind, pair]).wait()
+        local_copy(do_loc.at[three, cols], do_loc.at[three, cols], in_send.at[pair]).wait()
+        for side in range(2):
+            @pl.when(sides[side][0])
+            def _():
+                for kind, ref in kinds:
+                    rim_copy(ref, side, kind, pair).wait_send()
     work.drain_all()
 
 
@@ -1088,44 +1144,15 @@
         out_specs=(VM,) * 3,
         scratch_shapes=[
             pltpu.VMEM((group, 256), BF), pltpu.VMEM((group, 256), BF), pltpu.VMEM((ext, 256), BF), pltpu.VMEM((ext, 256), BF),
-            pltpu.VMEM((2, HALF, width), BF),
+            pltpu.VMEM((2, 2, HALF, 256), BF),
             pltpu.VMEM((2, ext, 128), BF), pltpu.VMEM((2, ext, 128), BF), pltpu.VMEM((2, 128, ext), BF),
             pltpu.VMEM((2, ext, 128), F32), pltpu.VMEM((2, ext, 128), F32),
             pltpu.VMEM((4, 8, QB), F32), pltpu.VMEM((4, 8, QB), F32),
-            dma((4,)), dma, dma, dma((3,)), dma((3,)), dma((2, 2)), dma((2,)),
+            dma((4, 2)), dma((2,)), dma((2,)), dma((3, 2)), dma((3, 2)), dma((2, 2, 2)), dma((2, 2, 2)),
         ] + scatter_scratch(ring, count, r, w),
         compiler_params=pltpu.CompilerParams(collective_id=collective_id, has_side_effects=True, vmem_limit_bytes=63 * MIB),
         name="attend_back",
     )(*grads, d_tok, kx, vx, kf, qf, qa, of)
-
-
-def first_kernel(ring, src, gain_src, wide, gains, *sems):
-    greet(group_peers(ring))
-    count = src.shape[0]
-    work = Gather(ring, count, lambda i, go: go(src.at[i], lambda p, c, y, x: wide.at[i, p, c, y, x]), sems[:3])
-    small = Gather(ring, 1, lambda i, go: go(gain_src, lambda p, c, y, x: gains.at[p, c, y, x]), sems[3:])
-    lags = (2, (0, 1, 2, 3))
-    def body(t, carry):
-        small.step(t, *lags)
-        work.step(t, *lags)
-        return carry
-    lax.fori_loop(0, work.steps(*lags), body, 0)
-    work.drain_all()
-    small.drain_all()
-
-
-def first_gather(src, gain_src, ring, collective_id):
-    count, r, w = src.shape
-    return pl.pallas_call(
-        functools.partial(first_kernel, ring),
-        out_shape=(jax.ShapeDtypeStruct((count, 2, ring, 2, 2, r, w), BF),
-                   jax.ShapeDtypeStruct((2, ring, 2, 2) + gain_src.shape, BF)),
-        in_specs=[ANY, ANY],
-        out_specs=(ANY, ANY),
-        scratch_shapes=gather_sems(count) + gather_sems(1),
-        compiler_params=pltpu.CompilerParams(collective_id=collective_id, has_side_effects=True),
-        name="collect",
-    )(src, gain_src)
 
 
 def last_kernel(ring, count, grads, small, out, small_out, sums, came, far, small_send, small_recv, *rest):
@@ -1187,12 +1214,14 @@
     )(grads, small)
 
 
-def edges(ids, ring):
-    up = [(i, i + 1) for i in range(ring - 1)]
-    down = [(i + 1, i) for i in range(ring - 1)]
-    below = lax.ppermute(ids[:, -HALF:] + 1, "cp", up) - 1
-    above = lax.ppermute(ids[:, :HALF] + 1, "cp", down) - 1
-    return jnp.concatenate([below, ids, above], axis=1)
+def to_blocks(weight, depth, r, w):
+    parts = weight.reshape(-1, depth, weight.shape[1] // 512, r // depth, w)
+    return parts.transpose(2, 0, 3, 1, 4).reshape(weight.shape[1] // 512, -1, r, w)
+
+
+def from_blocks(blocks, depth):
+    n, (r, w) = blocks.shape[0], blocks.shape[-2:]
+    return blocks.reshape(n, -1, r // depth, depth, w).swapaxes(2, 3).reshape(n, -1, 512)
 
 
 def local(
@@ -1205,43 +1234,39 @@
     depth = w_qkv.shape[0]
     r, w = item_shape(depth)
 
-    def pieces(weight):
-        return weight.reshape(depth, -1, 512).swapaxes(0, 1).reshape(-1, r, w)
-
-    first = pieces(w_qkv)
+    me = (lax.axis_index("pack") * ring + lax.axis_index("cp")) * 4 + head
     down_pieces = w_down.reshape(4, r, 2, w).swapaxes(1, 2).reshape(8, r, w)
-    second = jnp.concatenate([pieces(w_out), pieces(w_gate), pieces(w_up), down_pieces])
-    gain_src = jnp.pad(jnp.stack([gain_attn, gain_ffn]), ((0, 14), (0, 128 - depth)))
-    qkv_wide, gains = first_gather(first, gain_src, ring, 0)
-    qkv_wide = qkv_wide.reshape(-1, width, 512)
-    gains = gains[..., :2, :depth].reshape(-1, 2, depth).swapaxes(0, 1).reshape(2, 1, width).astype(F32)
+    src = jnp.concatenate([to_blocks(weight, depth, r, w)[:, 0] for weight in (w_qkv, w_out, w_gate, w_up)] + [down_pieces])
+    gain_src = lax.dynamic_update_slice(jnp.zeros((2, width), BF), jnp.stack([gain_attn, gain_ffn]), (0, me * depth))
+    gain_src = gain_src.reshape(16, 128)
 
     times = lax.dynamic_slice_in_dim(time_index, head * rows, rows, 0)
-    frequency = jnp.exp(-math.log(theta_base) * 2.0 * jnp.arange(HDIM // 2, dtype=jnp.float32) / HDIM)
+    lane = jnp.arange(128)
+    frequency = jnp.exp(-math.log(theta_base) * 2.0 * (lane % 32).astype(F32) / HDIM)
     angle = times.astype(F32)[:, None] * frequency[None, :]
-    cosine, sine = jnp.cos(angle), jnp.sin(angle)
-    cosine = jnp.concatenate([cosine] * 4, axis=1)
-    sine = jnp.concatenate([-sine, sine, -sine, sine], axis=1)
+    cosine = jnp.cos(angle)
+    sine = jnp.sin(angle) * jnp.where(lane % 64 < 32, -1.0, 1.0)[None, :]
     head_gains = jnp.stack([jnp.concatenate([q_gain, q_gain]), jnp.concatenate([k_gain, k_gain])])
 
-    ids = edges(jnp.stack([segment_ids, variate_ids]), ring)
-    kf = key_features(ids[0], ids[1])
-    qf = query_features(segment_ids, variate_ids)
+    qf, kf_own = features(segment_ids, variate_ids)
     hs = head_scales(lax.dynamic_slice_in_dim(head_bias, head * 4, 4, 0))
 
-    raw, rotated = project(inputs, gains[0], qkv_wide, cosine, sine, head_gains)
-    heads_out, of, qa, kx, vx, wide, down = attend(second, rotated, kf, qf, hs, 18, ring, 1)
-    layer_out, d_hidden, d_heads, g_gate, g_up, g_down, g_out, g_gffn = ffn(
-        inputs, heads_out, cotangent, gains[1], wide.reshape(-1, width, 512), down.reshape(-1, width))
+    heads_out, of, qa, kx, vx, kf, raw, gains, wide, down = attend(
+        inputs, cosine, sine, head_gains, kf_own, qf, hs, src, gain_src, 24, ring, 1)
+    wide = from_blocks(wide, depth)
+    gains = gains.reshape(2, 1, width)
+    layer_out, d_hidden, d_heads, g_down, g_out, g_gffn, pairs = ffn(
+        inputs, heads_out, cotangent, gains[1], wide, down.reshape(-1, width), ring, (r, w), 4)
 
     def blocks(grad):
-        return grad.reshape(-1, 2, ring, 2, 2, r, w)
-
-    grads = (blocks(g_out), blocks(g_gate), blocks(g_up), g_down.reshape(2, ring, 2, 2, 4, r, 2 * w))
-    layout = ((2, True), (8, True), (8, True), (8, False))
+        parts = grad.reshape(grad.shape[0], -1, depth, r // depth, w).swapaxes(2, 3)
+        return parts.reshape(-1, 2, ring, 2, 2, r, w)
+
+    grads = (blocks(g_out), g_down.reshape(2, ring, 2, 2, 4, r, 2 * w))
+    layout = ((2, True), (8, False))
     d_proj, g_bias, items = attend_back(grads, layout, d_heads, kx, vx, kf, qf, qa, of, ring, 2)
     g_qkv, grad_inputs, g_gattn, g_heads = unproject(
-        inputs, gains[0], qkv_wide, cosine, sine, head_gains, raw, d_proj, d_hidden)
+        inputs, gains[0], wide, cosine, sine, head_gains, raw, d_proj, d_hidden)
     bias_all = lax.dynamic_update_slice_in_dim(jnp.zeros((HEADS, 2), F32), g_bias[:, 0, :2], head * 4, 0)
     small = jnp.concatenate([
         g_gattn.reshape(8, 128), g_gffn.reshape(8, 128), g_heads,
@@ -1249,14 +1274,14 @@
     last, small = last_scatter(blocks(g_qkv), small, ring, 3)
 
     def columns(part):
-        return part.reshape(-1, depth, 512).swapaxes(0, 1).reshape(depth, -1)
-
-    me = (lax.axis_index("pack") * ring + lax.axis_index("cp")) * 4 + head
+        return from_blocks(part, depth).swapaxes(0, 1).reshape(depth, -1)
+
+    pairs = pairs.reshape(8, 2, r, w)
     own_gains = lax.dynamic_slice_in_dim(small[:16].reshape(2, width), me * depth, depth, 1)
     own_heads = small[16:18, :HDIM] + small[16:18, HDIM:]
     return (
-        layer_out, grad_inputs, columns(last), columns(items[:2]), columns(items[2:10]), columns(items[10:18]),
-        items[18:].reshape(4, 2, r, w).swapaxes(1, 2).reshape(w_down.shape),
+        layer_out, grad_inputs, columns(last), columns(items[:2]), columns(pairs[:, 0]), columns(pairs[:, 1]),
+        items[2:].reshape(4, 2, r, w).swapaxes(1, 2).reshape(w_down.shape),
         own_gains[0], own_gains[1], own_heads[0], own_heads[1], small[18, :32].reshape(HEADS, 2),
     )
 

time: 622 us -> 531 us (0.85); the launches traced: 621 us -> 523 us
  Pallas kernels: 571 us -> 493 us
  local copies, waits for them, and re-layouts: 31.9 us -> 20.3 us
  starting transfers between devices: 6.85 us -> 0 us
    pallas_call x1, Pallas kernels: 189 us -> 112 us  [attend_back(): pl.pallas_call(functools.partial(return_kernel, ring, layout, count), out...]
    pallas_call x1, Pallas kernels: 198 us -> 221 us  [attend(): pl.pallas_call(functools.partial(attend_kernel, ring, n_wide, count), out...]
    pallas_call x3 -> x1, Pallas kernels: 113 us -> 99.7 us  [ffn(): pl.pallas_call(functools.partial(ffn_kernel, ring), grid=(steps,), out_sh...]
    pallas_call x1, Pallas kernels: 51.8 us -> 41.7 us  [last_scatter(): pl.pallas_call(functools.partial(last_kernel, ring, count), out_shape=(ja...]
    concatenate x3 -> x1, local copies, waits for them, and re-layouts: 9.9 us -> 0.02 us  [local(): jnp.concatenate([to_blocks(weight, depth, r, w)[:, 0] for weight in (w_qk...]
    ppermute x2 -> x0, starting transfers between devices: 6.85 us -> none  [the longest x1 5.56 us: edges(): below = lax.ppermute(ids[:, -HALF:] + 1, 'cp', up) - 1]
  transfers between devices with their start and end apart: 2 -> 0, of which waited for: 0 -> 0; matrix products, arithmetic and copies ran while one was open for 3% -> 0% of each run, Pallas kernels for 9% -> 0%
where the time goes in v3:
time: 531 us; the launch traced here: 523 us
  Pallas kernels  493 us (93%)
  local copies, waits for them, and re-layouts  20.3 us (4%)
  other arithmetic  8.53 us (2%)
    pallas_call x1, Pallas kernels, attend(): pl.pallas_call(functools.partial(attend_kernel, ring, n_wide, count), out...  221 us
    pallas_call x1, Pallas kernels, attend_back(): pl.pallas_call(functools.partial(return_kernel, ring, layout, count), out...  112 us
    pallas_call x1, Pallas kernels, ffn(): pl.pallas_call(functools.partial(ffn_kernel, ring), grid=(steps,), out_sh...  99.7 us
    pallas_call x1, Pallas kernels, last_scatter(): pl.pallas_call(functools.partial(last_kernel, ring, count), out_shape=(ja...  41.7 us
    pallas_call x1, Pallas kernels, unproject(): pl.pallas_call(unproject_kernel, grid=(6,), out_shape=(jax.ShapeDtypeStru...  18.4 us
    unnamed x49, local copies, waits for them, and re-layouts  11.9 us

profile of v3, /device:TPU:0, one launch (start us, length us, event | category | flops | bytes accessed | tf_op | source)
XLA Modules:
  0.0 523.3 jit_solution(10317743025790689098)
XLA Ops:
  0.7 0.6 copy-done
  1.5 0.7 select_select_fusion.hs_ref
  2.1 0.7 pad_maximum_fusion.1
  3.0 0.6 reshape.198.gain_src
  3.6 0.8 dynamic-slice_convert_fusion
  4.3 1.8 fusion.2
  6.2 3.1 select_convert_fusion
  9.3 0.8 maximum_bitcast_fusion
  10.1 0.6 pad_maximum_fusion.hg_ref
  10.7 1.2 reshape.192
  12.4 0.2 reshape.196
  12.6 1.0 copy-done.9
  13.6 221.3 %attend.1 = (bf16[512,1024]{1,0:T(8,128)(2,1)}, f32[2048,256]{1,0:T(8,128)}, bf16[4,2048,128]{2,1,0:T(8,128)(2,1)}, bf16[3072,256]{1,0:T(8,128)(2,1)}, bf16[3072...) custom-call(bf16[512,1024]{1,0:T(8,128)(2,1)} %x_ref.5, ...), custom_call_target="tpu_custom_call" | custom-call | tf_op jit(solution)/shard_map/attend/pallas_call | solution.py:970
  234.9 1.3 fusion.7
  236.1 99.7 %feedforward.1 = (bf16[512,1024]{1,0:T(8,128)(2,1)}, f32[512,1024]{1,0:T(8,128)}, bf16[512,1024]{1,0:T(8,128)(2,1)}, bf16[4096,1024]{1,0:T(8,128)(2,1)}, bf16[2,...) custom-call(bf16[512,1024]{1,0:T(8,128)(2,1)} %x_ref.5, ...), custom_call_target="tpu_custom_call" | custom-call | tf_op jit(solution)/shard_map/feedforward/pallas_call | solution.py:671
  335.9 111.9 %attend_back.1 = (bf16[512,3072]{1,0:T(8,128)(2,1)}, f32[4,1,128]{2,1,0:T(1,128)}, f32[10,32,512]{2,1,0:T(8,128)}) custom-call(bf16[2,2,4,2,2,32,512]{6,5,4,3,2,1,0:T(8,128)(2,1)} %bitcast.94, bf16[2,4,2,2,4,32,1024]{6,5,4,3,2,1,0:T(8,128)(2,1)} %bitcast.92, bf16[512,1024]{1,0:T(8,128)(2,1)} %get-tuple-element.46.refs_2_, ...), custom_call_target="tpu_custom_call" | custom-call | tf_op jit(solution)/shard_map/attend_back/pallas_call | solution.py:1136
  447.9 1.2 copy-done.2
  449.1 1.6 copy-done.6
  450.7 1.6 copy-done.7
  452.3 18.4 %unproject.1 = (bf16[6,1024,512]{2,1,0:T(8,128)(2,1)}, f32[512,1024]{1,0:T(8,128)}, f32[1,1024]{1,0:T(1,128)S(1)}, f32[2,128]{1,0:T(2,128)S(1)}) custom-call(bf16[512,1024]{1,0:T(8,128)(2,1)S(1)} %copy-done.2, f32[1,1024]{1,0:T(1,128)S(1)} %bitcast.86, bf16[24,1024,512]{2,1,0:T(8,128)(2,1)} %bitcast.91, f32[512,128]{1,0:T(8,128)S(1)} %copy-done.5, ...), custom_call_target="tpu_custom_call" | custom-call | tf_op jit(solution)/shard_map/unproject/pallas_call | solution.py:741
  470.8 2.8 copy-done.3
  473.6 41.7 %rsum.1 = (f32[6,32,512]{2,1,0:T(8,128)S(1)}, f32[24,128]{1,0:T(8,128)S(1)}) custom-call(bf16[6,2,4,2,2,32,512]{6,5,4,3,2,1,0:T(8,128)(2,1)S(1)} %bitcast.84, f32[24,128]{1,0:T(8,128)S(1)} %select_maximum_fusion.small), custom_call_target="tpu_custom_call" | custom-call | tf_op jit(solution)/shard_map/rsum/pallas_call | solution.py:1205
  515.4 0.8 copy.48
  516.2 0.5 slice_bitcast_fusion.5
  516.9 0.7 copy.46
  517.6 0.5 slice_bitcast_fusion.3
  518.1 0.4 copy.45
  518.6 0.9 copy.54
  519.5 0.7 copy.49
  520.2 0.8 copy.50
  521.1 0.8 copy.51
  521.9 1.0 copy.66
  (66 shorter events, 1.4 us)
Async XLA Ops:
  0.6 0.7 copy-start
  0.7 11.3 %copy-start.16 = (bf16[32,1024]{1,0:T(8,128)(2,1)S(1)}, bf16[32,1024]{1,0:T(8,128)(2,1)}, u32[]{:S(2)}) copy-start(bf16[32,1024]{1,0:T(8,128)(2,1)} %param.18) | copy-start | bytes 196612
  0.7 11.3 %copy-start.13 = (bf16[32,4096]{1,0:T(8,128)(2,1)S(1)}, bf16[32,4096]{1,0:T(8,128)(2,1)}, u32[]{:S(2)}) copy-start(bf16[32,4096]{1,0:T(8,128)(2,1)} %param.19) | copy-start | bytes 786436
  0.7 11.5 %copy-start.14 = (bf16[32,4096]{1,0:T(8,128)(2,1)S(1)}, bf16[32,4096]{1,0:T(8,128)(2,1)}, u32[]{:S(2)}) copy-start(bf16[32,4096]{1,0:T(8,128)(2,1)} %param.20) | copy-start | bytes 786436
  6.2 6.2 %copy-start.15 = (bf16[128,1024]{1,0:T(8,128)(2,1)S(1)}, bf16[128,1024]{1,0:T(8,128)(2,1)}, u32[]{:S(2)}) copy-start(bf16[128,1024]{1,0:T(8,128)(2,1)} %param.21) | copy-start | bytes 786436
  12.6 1.0 copy-start.9
  335.9 112.0 %copy-start.4 = (f32[512,128]{1,0:T(8,128)S(1)}, f32[512,128]{1,0:T(8,128)}, u32[]{:S(2)}) copy-start(f32[512,128]{1,0:T(8,128)} %get-tuple-element.96.sin_ref) | copy-start | bytes 786436
  335.9 112.0 %copy-start.5 = (f32[512,128]{1,0:T(8,128)S(1)}, f32[512,128]{1,0:T(8,128)}, u32[]{:S(2)}) copy-start(f32[512,128]{1,0:T(8,128)} %get-tuple-element.97.cos_ref) | copy-start | bytes 786436
  335.9 112.0 %copy-start.8 = (f32[2,128]{1,0:T(2,128)S(1)}, f32[2,128]{1,0:T(2,128)}, u32[]{:S(2)}) copy-start(f32[2,128]{1,0:T(2,128)} %pad_maximum_fusion.hg_ref) | copy-start | bytes 3076
  447.9 1.2 copy-start.2
  449.1 1.6 copy-start.6
  450.7 1.6 copy-start.7
  452.3 18.4 %copy-start.18 = (f32[4,1,128]{2,1,0:T(1,128)S(1)}, f32[4,1,128]{2,1,0:T(1,128)}, u32[]{:S(2)}) copy-start(f32[4,1,128]{2,1,0:T(1,128)} %get-tuple-element.59) | copy-start | bytes 6148
  452.3 18.5 %copy-start.17 = (f32[1,1024]{1,0:T(1,128)S(1)}, f32[1,1024]{1,0:T(1,128)}, u32[]{:S(2)}) copy-start(f32[1,1024]{1,0:T(1,128)} %get-tuple-element.57) | copy-start | bytes 12292
  470.8 2.8 copy-start.3
  473.6 44.5 %copy-start.12 = (f32[10,32,512]{2,1,0:T(8,128)S(1)}, f32[10,32,512]{2,1,0:T(8,128)}, u32[]{:S(2)}) copy-start(f32[10,32,512]{2,1,0:T(8,128)} %get-tuple-element.61) | copy-start | bytes 1966084
  515.4 4.8 copy-start.11
  520.1 1.8 copy-start.10
  520.2 2.7 copy-start.1

commit v4 on v3

--- a/solution.py
+++ b/solution.py
@@ -163,36 +163,15 @@
         lax.fori_loop(0, (self.count + 1) // 2, one, 0)
 
 
-class StagedScatter(Scatter):
-    def begin(self, i):
-        self.copy0(i, self.load.at[lax.rem(i, self.slots), 1 - self.p]).start()
-
-    def mine(self, i, k):
-        return self.load[lax.rem(i, self.slots), self.p, k]
-
-    def landed(self, i):
-        pass
-
-    def reuse(self, i):
-        self.copy0(i, self.own.at[i]).wait_send()
-
-    def drain(self, i, first_y):
-        pl.when(i >= self.count - self.slots)(lambda: self.reuse(i))
-        self.copy1(i, first_y).wait_send()
-        self.copy2(i, first_y).wait_send()
-        pltpu.make_async_copy(self.b3.at[i], self.b3.at[i], self.send_sem.at[3, i]).wait()
-
-
-def scatter_scratch(ring, count, rows, cols, staged=0):
+def scatter_scratch(ring, count, rows, cols):
     bf = jnp.bfloat16
-    load = (staged, 2) if staged else (8,)
     return [
-        pltpu.VMEM(load + (ring, 2, 2, rows, cols), bf),
+        pltpu.VMEM((4, ring, 2, 2, rows, cols), bf),
         pltpu.VMEM((count, ring, 2, 2, rows, cols), bf),
         pltpu.VMEM((count, ring, 2, rows, cols), bf),
         pltpu.VMEM((count, ring, rows, cols), bf),
         pltpu.VMEM((count, ring - 1, rows, cols), bf),
-        pltpu.SemaphoreType.DMA((8,)),
+        pltpu.SemaphoreType.DMA((4,)),
         pltpu.SemaphoreType.DMA((4, count)),
         pltpu.SemaphoreType.DMA((4, count)),
     ]
@@ -214,38 +193,6 @@
     return pick
 
 
-def scatter_kernel(ring, layout, count, *refs):
-    n = len(layout)
-    grads, out = refs[:n], refs[n]
-    load, own, b1, b2, b3, load_sem, send_sem, recv_sem = refs[n + 1:]
-    greet(group_peers(ring))
-    pick = scatter_pick(grads, layout, out.shape[-1])
-
-    def write(i, total):
-        out[i] = total
-
-    work = Scatter(ring, count, pick, (load, own, b1, b2, b3), (load_sem, send_sem, recv_sem), out, write)
-    def body(t, carry):
-        work.step(t)
-        return carry
-    lax.fori_loop(0, work.steps(), body, 0)
-    work.drain_all()
-
-
-def scatter(grads, layout, ring, collective_id):
-    rows, cols = grads[0].shape[-2:]
-    count = sum(size for size, _ in layout)
-    return pl.pallas_call(
-        functools.partial(scatter_kernel, ring, layout, count),
-        out_shape=jax.ShapeDtypeStruct((count, rows, cols), jnp.float32),
-        in_specs=[pl.BlockSpec(memory_space=pl.ANY)] * len(grads),
-        out_specs=pl.BlockSpec(memory_space=pltpu.VMEM),
-        scratch_shapes=scatter_scratch(ring, count, rows, cols),
-        compiler_params=pltpu.CompilerParams(collective_id=collective_id, has_side_effects=True, vmem_limit_bytes=60 * 2**20),
-        name="rsum",
-    )(*grads)
-
-
 class Gather:
     def __init__(self, ring, count, pick, sems):
         self.ring, self.count, self.pick = ring, count, pick
@@ -264,23 +211,45 @@
     def same(self, i, stage, ref, device):
         return self.remote(i, stage, ref, ref, device)
 
-    def begin(self, i, first_x):
+    def begin(self, i, first_x, mid):
         def go(src, out):
             mine = out(self.p, self.c, self.hy, self.hx)
             pltpu.make_async_copy(src, mine, self.local_sem.at[i]).start()
+            if mid:
+                self.remote(i, 0, src, mine, self.near(first_x)).start()
+                return
             for step in range(1, self.ring):
                 peer = (self.p, lax.rem(self.c + step, self.ring), self.h)
                 self.remote(i, 0, src, mine, peer).start()
         self.pick(i, go)
 
-    def stage1(self, i, first_x):
+    def near(self, first_x):
+        return self.xpeer if first_x else self.ypeer
+
+    def block(self, out, first_x, mine):
+        if first_x:
+            return out(self.p, self.c, self.hy, self.hx if mine else 1 - self.hx)
+        return out(self.p, self.c, self.hy if mine else 1 - self.hy, self.hx)
+
+    def couple(self, out, first_x, at):
+        return out(self.p, at, self.hy, ALL) if first_x else out(self.p, at, ALL, self.hx)
+
+    def wait_for(self, ref, sem):
+        pltpu.make_async_copy(ref, ref, sem).wait()
+
+    def stage1(self, i, first_x, mid):
         def go(src, out):
             mine = out(self.p, self.c, self.hy, self.hx)
             pltpu.make_async_copy(src, mine, self.local_sem.at[i]).wait()
-            rest = out(self.p, pl.ds(0, self.ring - 1), self.hy, self.hx)
-            pltpu.make_async_copy(rest, rest, self.recv_sem.at[0, i]).wait()
+            if mid:
+                self.same(i, 0, self.block(out, first_x, False), self.core).wait_recv()
+                both = self.couple(out, first_x, self.c)
+                for step in range(1, self.ring):
+                    self.same(i, 1, both, (self.p, lax.rem(self.c + step, self.ring), self.h)).start()
+                return
+            self.wait_for(out(self.p, pl.ds(0, self.ring - 1), self.hy, self.hx), self.recv_sem.at[0, i])
             column = out(self.p, ALL, self.hy, self.hx)
-            self.same(i, 1, column, self.xpeer if first_x else self.ypeer).start()
+            self.same(i, 1, column, self.near(first_x)).start()
             self.same(i, 3, column, self.core).start()
         self.pick(i, go)
 
@@ -294,58 +263,65 @@
             return out(self.p, ALL, self.hy if mine else 1 - self.hy, ALL)
         return out(self.p, ALL, ALL, self.hx if mine else 1 - self.hx)
 
-    def stage2(self, i, first_x):
+    def stage2(self, i, first_x, mid):
         def go(src, out):
+            half = self.second(out, True, first_x)
+            if mid:
+                self.wait_for(self.couple(out, first_x, pl.ds(0, self.ring - 1)), self.recv_sem.at[1, i])
+                self.same(i, 2, half, self.near(not first_x)).start()
+                self.same(i, 3, half, self.core).start()
+                return
             came = self.first(out, False, first_x)
             self.same(i, 1, came, self.core).wait_recv()
-            self.same(i, 2, self.second(out, True, first_x), self.ypeer if first_x else self.xpeer).start()
+            self.same(i, 2, half, self.near(not first_x)).start()
             self.same(i, 3, came, self.core).start()
         self.pick(i, go)
 
-    def stage3(self, i, first_x):
+    def stage3(self, i, first_x, mid):
         def go(src, out):
             came = self.second(out, False, first_x)
             self.same(i, 2, came, self.core).wait_recv()
             self.same(i, 3, came, self.core).start()
         self.pick(i, go)
 
-    def finish(self, i, first_x):
+    def finish(self, i, first_x, mid):
         def go(src, out):
-            half = out(1 - self.p, ALL, ALL, ALL)
-            pltpu.make_async_copy(half, half, self.recv_sem.at[3, i]).wait()
+            self.wait_for(out(1 - self.p, ALL, ALL, ALL), self.recv_sem.at[3, i])
         self.pick(i, go)
 
-    def drain(self, i, first_x):
+    def drain(self, i, first_x, mid):
         def go(src, out):
-            rest = out(self.p, pl.ds(0, self.ring - 1), self.hy, self.hx)
-            pltpu.make_async_copy(rest, rest, self.send_sem.at[0, i]).wait()
-            self.same(i, 1, self.first(out, True, first_x), self.core).wait_send()
+            if mid:
+                self.same(i, 0, self.block(out, first_x, True), self.core).wait_send()
+                self.wait_for(self.couple(out, first_x, pl.ds(0, self.ring - 1)), self.send_sem.at[1, i])
+            else:
+                self.wait_for(out(self.p, pl.ds(0, self.ring - 1), self.hy, self.hx), self.send_sem.at[0, i])
+                self.same(i, 1, self.first(out, True, first_x), self.core).wait_send()
             self.same(i, 2, self.second(out, True, first_x), self.core).wait_send()
-            half = out(self.p, ALL, ALL, ALL)
-            pltpu.make_async_copy(half, half, self.send_sem.at[3, i]).wait()
+            self.wait_for(out(self.p, ALL, ALL, ALL), self.send_sem.at[3, i])
         self.pick(i, go)
 
-    def step(self, t, ahead=3, lags=(0, 2, 4, 6)):
-        pairs = (self.count + 1) // 2
-        def both(pair, act):
-            for first_x in (True, False):
-                i = 2 * pair + (0 if first_x else 1)
-                guard = (pair >= 0) & (i < self.count) & (i >= 0)
-                pl.when(guard)(functools.partial(act, i, first_x))
-        both(t, self.begin)
-        both(t - ahead - lags[0], self.stage1)
-        both(t - ahead - lags[1], self.stage2)
-        both(t - ahead - lags[2], self.stage3)
-        both(t - ahead - lags[3], self.finish)
-
-    def steps(self, ahead=3, lags=(0, 2, 4, 6)):
+    def both(self, pair, act):
+        middle = lax.rem(pair, 2) != 0
+        for first_x in (True, False):
+            i = 2 * pair + (0 if first_x else 1)
+            there = (pair >= 0) & (i < self.count) & (i >= 0)
+            pl.when(there & middle)(functools.partial(act, i, first_x, True))
+            pl.when(there & jnp.logical_not(middle))(functools.partial(act, i, first_x, False))
+
+    def step(self, t, ahead=2, lags=(0, 1, 2, 3)):
+        self.both(t, self.begin)
+        self.both(t - ahead - lags[0], self.stage1)
+        self.both(t - ahead - lags[1], self.stage2)
+        self.both(t - ahead - lags[2], self.stage3)
+        self.both(t - ahead - lags[3], self.finish)
+
+    def steps(self, ahead=2, lags=(0, 1, 2, 3)):
         return (self.count + 1) // 2 + ahead + lags[3]
 
     def drain_all(self):
         def one(t, carry):
-            for first_x in (True, False):
-                i = 2 * t + (0 if first_x else 1)
-                pl.when(i < self.count)(functools.partial(self.drain, i, first_x))
+            self.both(t, self.drain)
             return carry
         lax.fori_loop(0, (self.count + 1) // 2, one, 0)
 
@@ -370,32 +346,6 @@
             at = pl.ds(pl.multiple_of(lax.rem(j, 2) * cols, cols), cols)
             go(src.at[i], lambda p, c, y, x: down.at[p, c, y, x, j // 2, :, at])
     return pick
-
-
-def gather_kernel(ring, n_wide, count, src, wide, down, *sems):
-    greet(group_peers(ring))
-    work = Gather(ring, count, gather_pick(src, wide, down, n_wide), sems)
-    def body(t, carry):
-        work.step(t)
-        return carry
-    lax.fori_loop(0, work.steps(), body, 0)
-    work.drain_all()
-
-
-def gather(src, n_wide, ring, collective_id):
-    count, rows, cols = src.shape
-    return pl.pallas_call(
-        functools.partial(gather_kernel, ring, n_wide, count),
-        out_shape=(
-            jax.ShapeDtypeStruct((n_wide, 2, ring, 2, 2, rows, cols), src.dtype),
-            jax.ShapeDtypeStruct((2, ring, 2, 2, (count - n_wide) // 2, rows, 2 * cols), src.dtype),
-        ),
-        in_specs=[ANY],
-        out_specs=(ANY, ANY),
-        scratch_shapes=gather_sems(count),
-        compiler_params=pltpu.CompilerParams(collective_id=collective_id, has_side_effects=True),
-        name="collect",
-    )(src)
 
 
 def dot_tb(a, b):
@@ -482,7 +432,7 @@
     r = pl.ds(pl.multiple_of(n * QB, QB), QB)
     lane = lanes(QB)
     grads = do_ref[r, at].astype(jnp.float32)
-    terms = grads * of_ref[r, at]
+    terms = grads * of_ref[r, :]
     pieces = halves(grads)
     row = lax.broadcasted_iota(jnp.int32, (QB, QB), 0)
     col = lax.broadcasted_iota(jnp.int32, (QB, QB), 1)
@@ -492,7 +442,7 @@
         own = (lane < 64) if m == 0 else (lane >= 64)
         delta = jnp.sum(jnp.where(own, terms, 0.0), axis=1, keepdims=True)
         da = at_lanes(jnp.where(lane < 64, pieces[m], 0.0), 64, split3(-delta)).astype(jnp.bfloat16)
-        qb = qa_ref[pair * 2 + m, r, :]
+        qb = qa_ref[m, r, :]
         dq = jnp.zeros((128, QB), jnp.float32)
         for first, size, edge in ((0, QB, 0), (QB, SPAN - 2 * QB, None), (SPAN - QB, QB, 1)):
             keys = pl.ds(pl.multiple_of(n * QB + first, QB), size)
@@ -579,179 +529,6 @@
     return jnp.concatenate(parts, axis=1).astype(BF).reshape(shape)
 
 
-FFN_LAGS = (1, (0, 1, 2, 4))
-SLOTS = 6
-
-
-def ffn_kernel(ring, x_ref, heads_ref, cot_ref, gain_ref, wo_ref, wg_ref, wu_ref, wd_ref,
-               out_ref, dhid_ref, dheads_ref, gd_ref, go_ref, ggain_ref, sums_ref,
-               hidden, acc, nrm, nrm_t, load, own, b1, b2, b3, load_sem, send_sem, recv_sem):
-    t = pl.program_id(0)
-    steps = pl.num_programs(0)
-    cot = cot_ref[...]
-
-    def write(i, total):
-        sums_ref[i] = total
-
-    work = StagedScatter(ring, own.shape[0], None, (load, own, b1, b2, b3), (load_sem, send_sem, recv_sem), sums_ref, write)
-
-    @pl.when(t == 0)
-    def _():
-        greet(group_peers(ring))
-        heads = heads_ref[...]
-        for n in range(2):
-            at = slice(n * 512, (n + 1) * 512)
-            hidden[:, at] = x_ref[:, at].astype(F32) + dot(heads, wo_ref[n])
-        h = hidden[...]
-        y = h * scale_of(h) * gain_ref[...]
-        nrm[...] = y.astype(BF)
-        nrm_t[...] = y.T.astype(BF)
-        acc[...] = h
-        dhid_ref[...] = jnp.zeros_like(dhid_ref)
-
-    normed = nrm[...]
-    wg, wu, wd = wg_ref[0], wu_ref[0], wd_ref[...]
-    gate = dot(normed, wg)
-    up = dot(normed, wu)
-    d_product = dot_tb(cot, wd)
-    sig = jax.nn.sigmoid(gate)
-    silu = gate * sig
-    product = silu * up
-    prod_b = product.astype(BF)
-    d_gate = (d_product * up * sig * (1.0 + gate * (1.0 - sig))).astype(BF)
-    d_up = (d_product * silu).astype(BF)
-    slot = lax.rem(2 * t, SLOTS)
-    @pl.when(t >= SLOTS // 2)
-    def _():
-        work.reuse(2 * t - SLOTS)
-        work.reuse(2 * t + 1 - SLOTS)
-    load[slot] = as_blocks(dot(nrm_t[...], d_gate), load.shape[1:])
-    load[slot + 1] = as_blocks(dot(nrm_t[...], d_up), load.shape[1:])
-    work.step(t, *FFN_LAGS)
-    acc[...] += dot(prod_b, wd)
-    gd_ref[...] = dot(prod_b.astype(F32).T.astype(BF), cot).astype(BF)
-    dhid_ref[...] += dot_tb(d_gate, wg) + dot_tb(d_up, wu)
-
-    @pl.when(t == steps - 1)
-    def _():
-        work.step(t + 1, *FFN_LAGS)
-        out_ref[...] = acc[...].astype(BF)
-        h = hidden[...]
-        du, terms = norm_back_rows(h, scale_of(h), gain_ref[...], dhid_ref[...])
-        ggain_ref[...] = terms
-        d_hidden = cot_ref[...].astype(F32) + du
-        dhid_ref[...] = d_hidden
-        work.step(t + 2, *FFN_LAGS)
-        d_attn = d_hidden.astype(BF)
-        heads_t = heads_ref[...].astype(F32).T.astype(BF)
-        total = jnp.zeros(d_hidden.shape, F32)
-        for n in range(2):
-            at = slice(n * 512, (n + 1) * 512)
-            go_ref[n] = dot(heads_t, d_attn[:, at]).astype(BF)
-            total = total + dot_tb(d_attn[:, at], wo_ref[n])
-        dheads_ref[...] = total.astype(BF)
-        def rest(n, carry):
-            work.step(n, *FFN_LAGS)
-            return carry
-        lax.fori_loop(t + 3, work.steps(*FFN_LAGS), rest, 0)
-        work.drain_all()
-
-
-def ffn(x, heads, cot, gain, wide, down, ring, item, collective_id):
-    rows, width = x.shape
-    ff = down.shape[0]
-    steps = ff // 512
-    once = pl.Buffered(1)
-    def fixed(*shape):
-        return pl.BlockSpec(shape, lambda t: (0,) * len(shape), pipeline_mode=once)
-    def out(*shape):
-        return pl.BlockSpec(shape, lambda t: (0,) * len(shape))
-    def items(first):
-        return pl.BlockSpec((1, width, 512), lambda t: (first + t, 0, 0))
-    return pl.pallas_call(
-        functools.partial(ffn_kernel, ring),
-        grid=(steps,),
-        out_shape=(
-            jax.ShapeDtypeStruct((rows, width), BF), jax.ShapeDtypeStruct((rows, width), F32),
-            jax.ShapeDtypeStruct((rows, width), BF),
-            jax.ShapeDtypeStruct((ff, width), BF), jax.ShapeDtypeStruct((2, width, 512), BF),
-            jax.ShapeDtypeStruct((1, width), F32), jax.ShapeDtypeStruct((2 * steps,) + item, F32)),
-        in_specs=[fixed(rows, width), fixed(rows, width), fixed(rows, width), fixed(1, width),
-                  pl.BlockSpec((2, width, 512), lambda t: (3, 0, 0), pipeline_mode=once), items(8), items(16),
-                  pl.BlockSpec((512, width), lambda t: (t, 0))],
-        out_specs=(VM, VM, VM,
-                   pl.BlockSpec((512, width), lambda t: (t, 0)), VM, VM, VM),
-        scratch_shapes=[pltpu.VMEM((rows, width), F32), pltpu.VMEM((rows, width), F32),
-                        pltpu.VMEM((rows, width), BF), pltpu.VMEM((width, rows), BF)]
-        + scatter_scratch(ring, 2 * steps, item[0], item[1], SLOTS),
-        compiler_params=pltpu.CompilerParams(collective_id=collective_id, has_side_effects=True, vmem_limit_bytes=62 * MIB),
-        name="feedforward",
-    )(x, heads, cot, gain, wide, wide, wide, down)
-
-
-def unproject_kernel(x_ref, gain_ref, w_ref, cos_ref, sin_ref, hg_ref, raw_ref, d_ref, dhid_ref,
-                     gw_ref, gin_ref, ggain_ref, ghead_ref, nrm_t, dnorm):
-    t = pl.program_id(0)
-
-    @pl.when(t == 0)
-    def _():
-        x = x_ref[...].astype(F32)
-        nrm_t[...] = (x * scale_of(x) * gain_ref[...]).T.astype(BF)
-        dnorm[...] = jnp.zeros_like(dnorm)
-        ghead_ref[...] = jnp.zeros_like(ghead_ref)
-
-    def use(d_proj):
-        gw_ref[0] = dot(nrm_t[...], d_proj).astype(BF)
-        dnorm[...] += dot_tb(d_proj, w_ref[0])
-
-    @pl.when(t >= 4)
-    def _():
-        use(d_ref[...])
-
-    @pl.when(t < 4)
-    def _():
-        kind = t // 2
-        gain = hg_ref[pl.ds(kind, 1), :]
-        pieces = []
-        for n in range(d_ref.shape[1] // 128):
-            at = slice(n * 128, (n + 1) * 128)
-            u = raw_ref[:, at].astype(F32)
-            dy = d_ref[:, at].astype(F32)
-            dy = dy * cos_ref[...] - swap_halves(dy) * sin_ref[...]
-            r = lax.rsqrt(head_mean(u * u) + EPS)
-            scaled = dy * gain
-            pieces.append((r * scaled - u * (r * r * r) * head_mean(scaled * u)).astype(BF))
-            ghead_ref[pl.ds(kind, 1), :] += jnp.sum(dy * u * r, axis=0, keepdims=True)
-        use(jnp.concatenate(pieces, axis=1))
-
-    @pl.when(t == 5)
-    def _():
-        x = x_ref[...].astype(F32)
-        du, terms = norm_back_rows(x, scale_of(x), gain_ref[...], dnorm[...])
-        gin_ref[...] = dhid_ref[...] + du
-        ggain_ref[...] = terms
-
-
-def unproject(x, gain, wide, cosine, sine, head_gains, raw, grads, d_hidden):
-    rows, width = x.shape
-    def fixed(*shape):
-        return pl.BlockSpec(shape, lambda t: (0,) * len(shape))
-    tile = pl.BlockSpec((rows, 512), lambda t: (0, t))
-    item = pl.BlockSpec((1, width, 512), lambda t: (t, 0, 0))
-    return pl.pallas_call(
-        unproject_kernel,
-        grid=(6,),
-        out_shape=(jax.ShapeDtypeStruct((6, width, 512), BF), jax.ShapeDtypeStruct((rows, width), F32),
-                   jax.ShapeDtypeStruct((1, width), F32), jax.ShapeDtypeStruct((2, 128), F32)),
-        in_specs=[fixed(rows, width), fixed(1, width), item, fixed(rows, 128), fixed(rows, 128), fixed(2, 128),
-                  tile, tile, fixed(rows, width)],
-        out_specs=(item, fixed(rows, width), fixed(1, width), fixed(2, 128)),
-        scratch_shapes=[pltpu.VMEM((width, rows), BF), pltpu.VMEM((rows, width), F32)],
-        compiler_params=pltpu.CompilerParams(vmem_limit_bytes=48 * MIB),
-        name="unproject",
-    )(x, gain, wide, cosine, sine, head_gains, raw, grads, d_hidden)
-
-
 def remote(src, dst, send, recv, device):
     return pltpu.make_async_remote_copy(
         src_ref=src, dst_ref=dst, send_sem=send, recv_sem=recv, device_id=device, device_id_type=MESH)
@@ -785,6 +562,9 @@
 
 
 LAGS = (2, (0, 1, 2, 3))
+FIRST = LAGS[0] + LAGS[1][3]
+EXTRA = 2
+EVERY = 4
 
 
 def as_matrix(value):
@@ -840,7 +620,7 @@
         kf_ref[HALF + group:2 * HALF + group, :] = nothing
         for ref in (kx, vx):
             ref[HALF + group:2 * HALF + group, :] = jnp.zeros((HALF, 256), BF)
-    lax.fori_loop(2, 5, begin, 0)
+    lax.fori_loop(2, FIRST, begin, 0)
 
     def share(kind, head, pair):
         ref, at = places[kind][1:]
@@ -858,7 +638,7 @@
         return local_copy(wide.at[t], w_tile.at[lax.rem(t, 2)], tile_sem.at[lax.rem(t, 2)])
 
     for k in range(3):
-        begin(5 + k, 0)
+        begin(FIRST + k, 0)
         for m in range(2):
             tile_copy(2 * k + m).start()
         if k == 0:
@@ -904,6 +684,10 @@
 
     blocks = group // QB
     margin = HALF // QB
+    def more(t, carry):
+        work.step(t, *LAGS)
+        return carry
+    lax.fori_loop(FIRST + 3, FIRST + 3 + EXTRA, more, 0)
     def pair_step(pair, carry):
         cols = pair_at(0, pair)
         for kind, ref, at in places:
@@ -916,7 +700,9 @@
                     rim_copy(ref, side, kind, pair).start()
         build_keys(pair, kx, vx, kf_ref, ka, va, None, 1, 1 + group // HALF)
         def step(n, c):
-            work.step(8 + pair * blocks + n, *LAGS)
+            @pl.when(lax.rem(n, EVERY) == 0)
+            def _():
+                work.step(FIRST + 3 + EXTRA + (pair * blocks + n) // EVERY, *LAGS)
             forward_block(pair, lax.rem(n + margin, blocks), q_loc, qf_ref, hs_ref, ka, va, o_loc, of_ref, qa_ref)
             return c
         lax.fori_loop(0, blocks - 2 * margin, step, 0)
@@ -938,10 +724,8 @@
         return carry
     lax.fori_loop(0, 2, pair_step, 0)
 
-    def rest(t, carry):
-        work.step(t, *LAGS)
-        return carry
-    lax.fori_loop(8 + 2 * blocks, jnp.maximum(8 + 2 * blocks, work.steps(*LAGS)), rest, 0)
+    done = FIRST + 3 + EXTRA + 2 * blocks // EVERY
+    lax.fori_loop(done, max(done, work.steps(*LAGS)), more, 0)
     for pair in range(2):
         cols = pair_at(0, pair)
         local_copy(o_loc.at[mine, cols], tok_ref.at[:, pair_at(h * 256, pair)], local_sem.at[3, pair]).wait()
@@ -995,16 +779,141 @@
     )(x, cosine, sine, head_gains, kf, qf, hs, src, gain_src)
 
 
-def return_kernel(ring, layout, count, *refs):
-    n = len(layout)
-    grads = refs[:n]
-    (d_tok, kx, vx, kf_ref, qf_ref, qa_ref, of_ref, back, bias_ref, out,
-     do_loc, dq_loc, dk_loc, dv_loc, rims, ka, va, kt, dka, dva, same, every,
-     local_sem, in_send, in_recv, back_send, back_recv, rim_send, rim_recv,
-     load, own, b1, b2, b3, load_sem, send_sem, recv_sem) = refs[n:]
+BACK_LAGS = (1, (0, 1, 2, 3))
+BACK_EVERY = 1
+
+
+def down_blocks(value, shape):
+    rows, cols = shape[-2:]
+    if cols == value.shape[1]:
+        return value.astype(BF).reshape(shape)
+    depth = rows * cols // value.shape[1]
+    parts = value.reshape(-1, depth, value.shape[1])
+    parts = [parts[:, :, n:n + cols] for n in range(0, value.shape[1], cols)]
+    return jnp.concatenate(parts, axis=1).astype(BF).reshape(shape)
+
+
+def feed_phase(work, heads_hbm, cot_hbm, x_hbm, gain, wide, down, g_gu, g_go, g_gd, out_hbm, dhid_hbm, d_tok, gffn_ref,
+               back, hidden, acc, dnorm, nrm_t, w_gu, w_d, stage, stage_d, in_sem, w_sem, stage_sem, out_sem):
+    tiles = down.shape[0] // 512
+    width = back.shape[1] // 3
+    heads, cot, nrm = (back.at[:, n * width:(n + 1) * width] for n in range(3))
+    spots = g_gd.shape[1] * g_gd.shape[0] // tiles
+
+    def weights(t, slot):
+        return [local_copy(wide.at[8 + t], w_gu.at[slot, 0], w_sem.at[slot, 0]),
+                local_copy(wide.at[16 + t], w_gu.at[slot, 1], w_sem.at[slot, 1]),
+                local_copy(down.at[pl.ds(pl.multiple_of(t * 512, 512), 512)], w_d.at[slot], w_sem.at[slot, 2])]
+
+    def out_weight(slot):
+        return [local_copy(wide.at[6 + n], w_gu.at[slot, n], w_sem.at[slot, n]) for n in range(2)]
+
+    def staged(t):
+        per = g_gd.shape[1] // spots
+        return [local_copy(stage.at[0], g_gu.at[2 * t], stage_sem.at[0]),
+                local_copy(stage.at[1], g_gu.at[2 * t + 1], stage_sem.at[1]),
+                local_copy(stage_d, g_gd.at[t // per, pl.ds(lax.rem(t, per) * spots, spots)], stage_sem.at[2])]
+
+    first = [local_copy(heads_hbm, heads, in_sem.at[0]), local_copy(cot_hbm, cot, in_sem.at[1]),
+             local_copy(x_hbm, w_d.at[1], in_sem.at[2])] + out_weight(1)
+    for copy in first + weights(0, 0):
+        copy.start()
+    for copy in first:
+        copy.wait()
+    for n in range(2):
+        at = slice(n * 512, (n + 1) * 512)
+        hidden[:, at] = w_d[1, :, at].astype(F32) + dot(heads[...], w_gu[1, n])
+    def normalise(n, carry):
+        at = pl.ds(pl.multiple_of(n * 128, 128), 128)
+        h = hidden[at, :]
+        y = h * scale_of(h) * gain
+        nrm[at, :] = y.astype(BF)
+        nrm_t[:, at] = y.T.astype(BF)
+        acc[at, :] = h
+        dnorm[at, :] = jnp.zeros_like(h)
+        return carry
+    lax.fori_loop(0, 4, normalise, 0)
+
+    def tile(t, carry):
+        slot = lax.rem(t, 2)
+        for copy in weights(t, slot):
+            copy.wait()
+        @pl.when(t < tiles - 1)
+        def _():
+            for copy in weights(t + 1, 1 - slot):
+                copy.start()
+        @pl.when(t == tiles - 1)
+        def _():
+            for copy in out_weight(tiles % 2):
+                copy.start()
+        normed = nrm[...]
+        wg, wu, wd = w_gu[slot, 0], w_gu[slot, 1], w_d[slot]
+        gate = dot(normed, wg)
+        up = dot(normed, wu)
+        d_product = dot_tb(cot[...], wd)
+        sig = jax.nn.sigmoid(gate)
+        silu = gate * sig
+        product = silu * up
+        prod_b = product.astype(BF)
+        d_gate = (d_product * up * sig * (1.0 + gate * (1.0 - sig))).astype(BF)
+        d_up = (d_product * silu).astype(BF)
+        acc[...] += dot(prod_b, wd)
+        dnorm[...] += dot_tb(d_gate, wg) + dot_tb(d_up, wu)
+        @pl.when(t > 0)
+        def _():
+            for copy in staged(t - 1):
+                copy.wait()
+            work.step(t - 1, *BACK_LAGS)
+        stage[0] = as_blocks(dot(nrm_t[...], d_gate), stage.shape[1:])
+        stage[1] = as_blocks(dot(nrm_t[...], d_up), stage.shape[1:])
+        stage_d[...] = down_blocks(dot(product.T.astype(BF), cot[...]), stage_d.shape)
+        for copy in staged(t):
+            copy.start()
+        return carry
+    lax.fori_loop(0, tiles, tile, 0)
+    for copy in staged(tiles - 1):
+        copy.wait()
+    work.step(tiles - 1, *BACK_LAGS)
+
+    def finish(n, carry):
+        at = pl.ds(pl.multiple_of(n * 128, 128), 128)
+        h = hidden[at, :]
+        du, terms = norm_back_rows(h, scale_of(h), gain, dnorm[at, :])
+        d_hidden = cot[at, :].astype(F32) + du
+        hidden[at, :] = d_hidden
+        nrm[at, :] = d_hidden.astype(BF)
+        heads_t = heads[at, :].astype(F32).T.astype(BF)
+        nrm_t[:, at] = heads_t
+        cot[at, :] = acc[at, :].astype(BF)
+        return carry + terms
+    gffn_ref[...] = lax.fori_loop(0, 4, finish, jnp.zeros(gffn_ref.shape, F32))
+    last = [local_copy(cot, out_hbm, out_sem.at[0]), local_copy(hidden, dhid_hbm, out_sem.at[1])]
+    for copy in last:
+        copy.start()
+    for copy in out_weight(tiles % 2):
+        copy.wait()
+    d_attn = nrm[...]
+    total = jnp.zeros(hidden.shape, F32)
+    for n in range(2):
+        at = slice(n * 512, (n + 1) * 512)
+        total = total + dot_tb(d_attn[:, at], w_gu[tiles % 2, n])
+    d_tok[...] = total.astype(BF)
+    for n in range(2):
+        at = slice(n * 512, (n + 1) * 512)
+        stage[n] = as_blocks(dot(nrm_t[...], d_attn[:, at]), stage.shape[1:])
+        copy = local_copy(stage.at[n], g_go.at[n], stage_sem.at[n])
+        copy.start()
+    for n in range(2):
+        local_copy(stage.at[n], g_go.at[n], stage_sem.at[n]).wait()
+    for copy in last:
+        copy.wait()
+
+
+def score_phase(work, first_step, ring, d_tok, kx_hbm, vx_hbm, kf_ref, qf_ref, qa_hbm, of_hbm, do_loc, rims, back, same, every,
+                kx, vx, qa, of, dq_loc, dk_loc, dv_loc, ka, va, kt, dka, dva,
+                load_sem, local_sem, in_send, in_recv, back_send, back_recv, rim_send, rim_recv):
     p, c, h = place()
     rim = Rim(ring)
-    greet(group_peers(ring) + [(p, c, 3 - h)])
     rows, width = d_tok.shape
     group = 4 * rows
     mine = pl.ds(pl.multiple_of(h * rows, rows), rows)
@@ -1015,16 +924,6 @@
         for step in range(1, 4):
             to = lax.rem(h + step, 4)
             remote(d_tok.at[:, pair_at(to * 256, pair)], do_loc.at[mine, cols], in_send.at[pair], in_recv.at[pair], (p, c, to)).start()
-
-    def write(i, total):
-        out[i] = total
-
-    work = Scatter(ring, count, scatter_pick(grads, layout, out.shape[-1]), (load, own, b1, b2, b3),
-                   (load_sem, send_sem, recv_sem), out, write)
-    def begin(t, carry):
-        work.step(t)
-        return carry
-    lax.fori_loop(0, 3, begin, 0)
     same[...] = jnp.zeros_like(same)
     every[...] = jnp.zeros_like(every)
 
@@ -1073,14 +972,22 @@
     blocks = group // QB
     def pair_step(pair, carry):
         cols = pair_at(0, pair)
-        build_keys(pair, kx, vx, kf_ref, ka, va, kt)
+        loads = [local_copy(kx_hbm.at[:, cols], kx, load_sem.at[0]), local_copy(vx_hbm.at[:, cols], vx, load_sem.at[1]),
+                 local_copy(qa_hbm.at[pl.ds(pair * 2, 2)], qa, load_sem.at[2]), local_copy(of_hbm.at[:, cols], of, load_sem.at[3])]
+        for copy in loads:
+            copy.start()
         dka[...] = jnp.zeros_like(dka)
         dva[...] = jnp.zeros_like(dva)
+        for copy in loads:
+            copy.wait()
+        build_keys(0, kx, vx, kf_ref, ka, va, kt)
         local_copy(do_loc.at[mine, cols], do_loc.at[mine, cols], local_sem.at[0, pair]).wait()
         local_copy(do_loc.at[three, cols], do_loc.at[three, cols], in_recv.at[pair]).wait()
         def step(m, c):
-            work.step(3 + pair * blocks + m)
-            backward_block(pair, m, qf_ref, qa_ref, do_loc, of_ref, ka, va, kt, dka, dva, dq_loc, same, every)
+            @pl.when(lax.rem(m, BACK_EVERY) == 0)
+            def _():
+                work.step(first_step + (pair * blocks + m) // BACK_EVERY, *BACK_LAGS)
+            backward_block(pair, m, qf_ref, qa, do_loc, of, ka, va, kt, dka, dva, dq_loc, same, every)
             return c
         lax.fori_loop(0, blocks // 2, step, 0)
         pl.when(pair == 1)(lambda: edges_back(0))
@@ -1096,18 +1003,13 @@
         give(0, pair, None)
         return carry
     lax.fori_loop(0, 2, pair_step, 0)
-
-    def total(x):
-        return jnp.sum(jnp.sum(x, axis=1, keepdims=True), axis=2, keepdims=True)
-    s, e = total(same[...]), total(every[...])
-    lane = lax.broadcasted_iota(jnp.int32, (4, 1, 128), 2)
-    bias_ref[...] = jnp.where(lane == 0, s, jnp.where(lane == 1, e - s, 0.0))
     edges_back(1)
-
-    def rest(t, carry):
-        work.step(t)
+    done = first_step + 2 * blocks // BACK_EVERY
+    def more(t, carry):
+        work.step(t, *BACK_LAGS)
         return carry
-    lax.fori_loop(3 + 2 * blocks, jnp.maximum(3 + 2 * blocks, work.steps()), rest, 0)
+    lax.fori_loop(done, max(done, work.steps(*BACK_LAGS)), more, 0)
+    work.drain_all()
 
     part = back.at[:, pl.ds(0, 384)]
     for pair in range(2):
@@ -1123,95 +1025,201 @@
             def _():
                 for kind, ref in kinds:
                     rim_copy(ref, side, kind, pair).wait_send()
-    work.drain_all()
-
-
-def attend_back(grads, layout, d_tok, kx, vx, kf, qf, qa, of, ring, collective_id):
+
+
+def unproject_phase(work, x_hbm, gain, wide, raw_hbm, cos_ref, sin_ref, hg_ref, dhid_hbm, back, g_qkv, gin_hbm, gattn_ref, ghead_ref,
+                    before, x, nrm_t, dnorm, w, raw, stage, dhid, in_sem, w_sem, stage_sem):
+    def tile_copies(t, slot):
+        copies = [local_copy(wide.at[t], w.at[slot], w_sem.at[slot, 0])]
+        if t < 4:
+            copies.append(local_copy(raw_hbm.at[:, t * 512:(t + 1) * 512], raw.at[slot], w_sem.at[slot, 1]))
+        return copies
+    late = local_copy(dhid_hbm, dhid, in_sem.at[1])
+    load = local_copy(x_hbm, x, in_sem.at[0])
+    load.start()
+    late.start()
+    for copy in tile_copies(0, 0):
+        copy.start()
+    load.wait()
+    def normalise(n, carry):
+        at = pl.ds(pl.multiple_of(n * 128, 128), 128)
+        u = x[at, :].astype(F32)
+        nrm_t[:, at] = (u * scale_of(u) * gain).T.astype(BF)
+        return carry
+    lax.fori_loop(0, 4, normalise, 0)
+    before()
+    ghead_ref[...] = jnp.zeros_like(ghead_ref)
+    for t in range(6):
+        slot = t % 2
+        if t < 5:
+            for copy in tile_copies(t + 1, 1 - slot):
+                copy.start()
+        for copy in tile_copies(t, slot):
+            copy.wait()
+        if t < 4:
+            kind = t // 2
+            head_gain = hg_ref[kind:kind + 1, :]
+            def unrotate(n, carry):
+                at = pl.ds(pl.multiple_of(n * 128, 128), 128)
+                for m in range(4):
+                    part = slice(m * 128, (m + 1) * 128)
+                    wide_part = slice(t * 512 + m * 128, t * 512 + (m + 1) * 128)
+                    u = raw[slot, at, part].astype(F32)
+                    dy = back[at, wide_part].astype(F32)
+                    dy = dy * cos_ref[at, :] - swap_halves(dy) * sin_ref[at, :]
+                    r = lax.rsqrt(head_mean(u * u) + EPS)
+                    scaled = dy * head_gain
+                    back[at, wide_part] = (r * scaled - u * (r * r * r) * head_mean(scaled * u)).astype(BF)
+                    ghead_ref[kind:kind + 1, :] += jnp.sum(dy * u * r, axis=0, keepdims=True)
+                return carry
+            lax.fori_loop(0, 4, unrotate, 0)
+        d_proj = back[:, t * 512:(t + 1) * 512]
+        stage[slot] = as_blocks(dot(nrm_t[...], d_proj), stage.shape[1:])
+        copy = local_copy(stage.at[slot], g_qkv.at[t], stage_sem.at[slot])
+        copy.start()
+        part = dot_tb(d_proj, w[slot])
+        if t == 0:
+            dnorm[...] = part
+        else:
+            dnorm[...] += part
+        copy.wait()
+        if t % 2:
+            work.step(t // 2, *BACK_LAGS)
+    late.wait()
+    def finish(n, carry):
+        at = pl.ds(pl.multiple_of(n * 128, 128), 128)
+        u = x[at, :].astype(F32)
+        du, terms = norm_back_rows(u, scale_of(u), gain, dnorm[at, :])
+        dhid[at, :] = dhid[at, :] + du
+        return carry + terms
+    gattn_ref[...] = lax.fori_loop(0, 4, finish, jnp.zeros(gattn_ref.shape, F32))
+    copy = local_copy(dhid, gin_hbm, in_sem.at[1])
+    copy.start()
+    copy.wait()
+
+
+def train_kernel(ring, x, heads, cot, gains, wide, down, kx, vx, kf, qf, qa, of, raw, cos_ref, sin_ref, hg_ref,
+                 out, gin, sums, small_out, dhid, g_gu, g_go, g_gd, g_qkv,
+                 d_tok, do_loc, rims, back, same, every, gffn, gattn, ghead,
+                 small, came, far, small_send, small_recv, credit,
+                 local_sem, in_send, in_recv, back_send, back_recv, rim_send, rim_recv, *buffers):
+    p, c, h = place()
+    peers = group_peers(ring)
+    greet(peers + [(p, c, 3 - h)])
     rows, width = d_tok.shape
-    group = 4 * rows
-    ext = group + 2 * HALF
-    r, w = grads[0].shape[-2:]
-    count = sum(size for size, _ in layout)
+    group, ext = 4 * rows, 4 * rows + 2 * HALF
+    r, w = sums.shape[-2:]
+    block = (2, ring, 2, 2, r, w)
+    bufs, sems = buffers[:5], buffers[5:]
     dma = pltpu.SemaphoreType.DMA
-    return pl.pallas_call(
-        functools.partial(return_kernel, ring, layout, count),
-        out_shape=(
-            jax.ShapeDtypeStruct((rows, 3 * width), BF),
-            jax.ShapeDtypeStruct((4, 1, 128), F32),
-            jax.ShapeDtypeStruct((count, r, w), F32),
-        ),
-        in_specs=[ANY] * len(grads) + [ANY] + [VM] * 6,
-        out_specs=(VM,) * 3,
-        scratch_shapes=[
-            pltpu.VMEM((group, 256), BF), pltpu.VMEM((group, 256), BF), pltpu.VMEM((ext, 256), BF), pltpu.VMEM((ext, 256), BF),
-            pltpu.VMEM((2, 2, HALF, 256), BF),
-            pltpu.VMEM((2, ext, 128), BF), pltpu.VMEM((2, ext, 128), BF), pltpu.VMEM((2, 128, ext), BF),
-            pltpu.VMEM((2, ext, 128), F32), pltpu.VMEM((2, ext, 128), F32),
-            pltpu.VMEM((4, 8, QB), F32), pltpu.VMEM((4, 8, QB), F32),
-            dma((4, 2)), dma((2,)), dma((2,)), dma((3, 2)), dma((3, 2)), dma((2, 2, 2)), dma((2, 2, 2)),
-        ] + scatter_scratch(ring, count, r, w),
-        compiler_params=pltpu.CompilerParams(collective_id=collective_id, has_side_effects=True, vmem_limit_bytes=63 * MIB),
-        name="attend_back",
-    )(*grads, d_tok, kx, vx, kf, qf, qa, of)
-
-
-def last_kernel(ring, count, grads, small, out, small_out, sums, came, far, small_send, small_recv, *rest):
-    greet(group_peers(ring))
-    buffers, sems = rest[:5], rest[5:]
+    count = 26
+
     def write(i, total):
-        out[i] = total
-    work = Scatter(ring, count, scatter_pick((grads,), ((count, True),), out.shape[-1]), buffers, sems, out, write)
-    p, c, h = place()
-    peers = (work.core, work.xpeer, work.ypeer)
+        sums[i] = total
+
+    def write_last(i, total):
+        sums[count + i] = total
+
+    work = Scatter(ring, count, scatter_pick((g_gu, g_go, g_gd), ((16, True), (2, True), (8, False)), w), bufs, sems, sums, write)
+    last = Scatter(ring, 6, scatter_pick((g_qkv,), ((6, True),), w), bufs, sems, sums, write_last)
+    vm = pltpu.VMEM
+    tiles = down.shape[0] // 512
+    spots = g_gd.shape[0] * g_gd.shape[1] // tiles
+
+    pl.run_scoped(
+        functools.partial(feed_phase, work, heads, cot, x, gains[1], wide, down, g_gu, g_go, g_gd, out, dhid, d_tok, gffn, back),
+        vm((rows, width), F32), vm((rows, width), F32), vm((rows, width), F32), vm((width, rows), BF), vm((2, 2, width, 512), BF), vm((2, 512, width), BF),
+        vm((2,) + block, BF), vm((spots,) + g_gd.shape[2:], BF), dma((3,)), dma((2, 3)), dma((3,)), dma((2,)))
+    def score(kx_p, vx_p, qa_p, of_p, dq_loc, dk_loc, dv_loc, ka, va, kt, dka, dva, load_sem):
+        score_phase(work, tiles, ring, d_tok, kx, vx, kf, qf, qa, of, do_loc, rims, back, same, every,
+                    kx_p, vx_p, qa_p, of_p, dq_loc, dk_loc, dv_loc, ka, va, kt, dka, dva,
+                    load_sem, local_sem, in_send, in_recv, back_send, back_recv, rim_send, rim_recv)
+
+    pl.run_scoped(
+        score,
+        vm((ext, 128), BF), vm((ext, 128), BF), vm((2, group, 128), BF), vm((group, 128), F32),
+        vm((group, 256), BF), vm((ext, 256), BF), vm((ext, 256), BF),
+        vm((2, ext, 128), BF), vm((2, ext, 128), BF), vm((2, 128, ext), BF), vm((2, ext, 128), F32), vm((2, ext, 128), F32),
+        dma((4,)))
+    for peer in peers:
+        pl.semaphore_signal(credit, inc=1, device_id=peer, device_id_type=MESH)
+    pl.run_scoped(
+        functools.partial(unproject_phase, last, x, gains[0], wide, raw, cos_ref, sin_ref, hg_ref, dhid, back, g_qkv, gin, gattn, ghead,
+                          lambda: pl.semaphore_wait(credit, len(peers))),
+        vm((rows, width), BF), vm((width, rows), BF), vm((rows, width), F32), vm((2, width, 512), BF), vm((2, rows, 512), BF),
+        vm((2,) + block, BF), vm((rows, width), F32), dma((2,)), dma((2, 2)), dma((2,)))
+
+    def total_of(value):
+        return jnp.sum(jnp.sum(value, axis=1, keepdims=True), axis=2, keepdims=True)
+    s, e = total_of(same[...]), total_of(every[...])
+    lane = lax.broadcasted_iota(jnp.int32, (1, 128), 1)
+    bias = jnp.zeros((1, 128), F32)
+    for m in range(4):
+        bias = jnp.where(lane == h * 8 + 2 * m, s[m], jnp.where(lane == h * 8 + 2 * m + 1, e[m] - s[m], bias))
+    for n in range(8):
+        at = slice(n * 128, (n + 1) * 128)
+        small[0, n:n + 1, :] = gattn[:, at]
+        small[0, 8 + n:9 + n, :] = gffn[:, at]
+    small[0, 16:18, :] = ghead[...]
+    small[0, 18:19, :] = bias
+    small[0, 19:24, :] = jnp.zeros((5, 128), F32)
+    hops = (last.core, last.xpeer, last.ypeer)
 
     def hop(n):
-        return remote(sums.at[n], came.at[n], small_send.at[n], small_recv.at[n], peers[n])
-
-    def far_hop(step):
-        return remote(sums.at[3], far.at[step - 1], small_send.at[3], small_recv.at[3], (p, lax.rem(c + step, ring), h))
-
-    sums[0] = small[...]
+        return remote(small.at[n], came.at[n], small_send.at[n], small_recv.at[n], hops[n])
+
     hop(0).start()
-    def body(t, carry):
-        work.step(t)
+    def rest(t, carry):
+        last.step(t, *BACK_LAGS)
         for n in range(3):
-            @pl.when(t == 2 + 2 * n)
+            @pl.when(t == 3 + n)
             def _():
                 hop(n).wait_recv()
-                sums[n + 1] = sums[n] + came[n]
+                small[n + 1] = small[n] + came[n]
                 if n < 2:
                     hop(n + 1).start()
                 else:
                     for step in range(1, ring):
-                        far_hop(step).start()
+                        remote(small.at[3], far.at[step - 1], small_send.at[3], small_recv.at[3], (p, lax.rem(c + step, ring), h)).start()
         return carry
-    lax.fori_loop(0, work.steps(), body, 0)
+    lax.fori_loop(3, last.steps(*BACK_LAGS), rest, 0)
     local_copy(far, far, small_recv.at[3]).wait()
-    total = sums[3]
+    total = small[3]
     for step in range(1, ring):
         total = total + far[step - 1]
     small_out[...] = total
     for n in range(3):
         hop(n).wait_send()
     local_copy(far, far, small_send.at[3]).wait()
-    work.drain_all()
-
-
-def last_scatter(grads, small, ring, collective_id):
-    count = grads.shape[0]
-    r, w = grads.shape[-2:]
-    n = small.shape[0]
+    last.drain_all()
+
+
+def train(x, heads, cot, gains, wide, down, kx, vx, kf, qf, qa, of, raw, cosine, sine, head_gains, ring, item, collective_id):
+    rows, width = x.shape
+    group, ext = 4 * rows, 4 * rows + 2 * HALF
+    r, w = item
+    block = (2, ring, 2, 2, r, w)
     dma = pltpu.SemaphoreType.DMA
+    vm = pltpu.VMEM
+    shape = jax.ShapeDtypeStruct
     return pl.pallas_call(
-        functools.partial(last_kernel, ring, count),
-        out_shape=(jax.ShapeDtypeStruct((count, r, w), F32), jax.ShapeDtypeStruct((n, 128), F32)),
-        in_specs=[ANY, VM],
-        out_specs=(VM, VM),
-        scratch_shapes=[pltpu.VMEM((4, n, 128), F32), pltpu.VMEM((3, n, 128), F32), pltpu.VMEM((ring - 1, n, 128), F32),
-                        dma((4,)), dma((4,))] + scatter_scratch(ring, count, r, w),
-        compiler_params=pltpu.CompilerParams(collective_id=collective_id, has_side_effects=True, vmem_limit_bytes=40 * MIB),
-        name="rsum",
-    )(grads, small)
+        functools.partial(train_kernel, ring),
+        out_shape=(
+            shape((rows, width), BF), shape((rows, width), F32), shape((32, r, w), F32), shape((24, 128), F32),
+            shape((rows, width), F32), shape((16,) + block, BF), shape((2,) + block, BF),
+            shape((2, ring, 2, 2, 4, r, 2 * w), BF), shape((6,) + block, BF)),
+        in_specs=[ANY] * 3 + [VM] + [ANY] * 4 + [VM] * 2 + [ANY] * 3 + [VM] * 3,
+        out_specs=(ANY, ANY, VM, VM) + (ANY,) * 5,
+        scratch_shapes=[
+            vm((rows, width), BF), vm((group, 256), BF), vm((2, 2, HALF, 256), BF), vm((rows, 3 * width), BF),
+            vm((4, 8, QB), F32), vm((4, 8, QB), F32), vm((1, width), F32), vm((1, width), F32), vm((2, 128), F32),
+            vm((4, 24, 128), F32), vm((3, 24, 128), F32), vm((ring - 1, 24, 128), F32), dma((4,)), dma((4,)),
+            pltpu.SemaphoreType.REGULAR,
+            dma((4, 2)), dma((2,)), dma((2,)), dma((3, 2)), dma((3, 2)), dma((2, 2, 2)), dma((2, 2, 2)),
+        ] + scatter_scratch(ring, 26, r, w),
+        compiler_params=pltpu.CompilerParams(collective_id=collective_id, has_side_effects=True, vmem_limit_bytes=63 * MIB),
+        name="train",
+    )(x, heads, cot, gains, wide, down, kx, vx, kf, qf, qa, of, raw, cosine, sine, head_gains)
 
 
 def to_blocks(weight, depth, r, w):
@@ -1255,34 +1263,21 @@
         inputs, cosine, sine, head_gains, kf_own, qf, hs, src, gain_src, 24, ring, 1)
     wide = from_blocks(wide, depth)
     gains = gains.reshape(2, 1, width)
-    layer_out, d_hidden, d_heads, g_down, g_out, g_gffn, pairs = ffn(
-        inputs, heads_out, cotangent, gains[1], wide, down.reshape(-1, width), ring, (r, w), 4)
-
-    def blocks(grad):
-        parts = grad.reshape(grad.shape[0], -1, depth, r // depth, w).swapaxes(2, 3)
-        return parts.reshape(-1, 2, ring, 2, 2, r, w)
-
-    grads = (blocks(g_out), g_down.reshape(2, ring, 2, 2, 4, r, 2 * w))
-    layout = ((2, True), (8, False))
-    d_proj, g_bias, items = attend_back(grads, layout, d_heads, kx, vx, kf, qf, qa, of, ring, 2)
-    g_qkv, grad_inputs, g_gattn, g_heads = unproject(
-        inputs, gains[0], wide, cosine, sine, head_gains, raw, d_proj, d_hidden)
-    bias_all = lax.dynamic_update_slice_in_dim(jnp.zeros((HEADS, 2), F32), g_bias[:, 0, :2], head * 4, 0)
-    small = jnp.concatenate([
-        g_gattn.reshape(8, 128), g_gffn.reshape(8, 128), g_heads,
-        jnp.pad(bias_all.reshape(1, 32), ((0, 5), (0, 96)))])
-    last, small = last_scatter(blocks(g_qkv), small, ring, 3)
+    layer_out, grad_inputs, items, small, *_ = train(
+        inputs, heads_out, cotangent, gains, wide, down.reshape(-1, width), kx, vx, kf, qf, qa, of, raw,
+        cosine, sine, head_gains, ring, (r, w), 2)
 
     def columns(part):
         return from_blocks(part, depth).swapaxes(0, 1).reshape(depth, -1)
 
-    pairs = pairs.reshape(8, 2, r, w)
+    pairs = items[:16].reshape(8, 2, r, w)
+    down_depth = w_down.shape[0] // 4
+    own_down = items[18:26].reshape(4, 2, r // down_depth, down_depth, w).transpose(0, 3, 2, 1, 4).reshape(w_down.shape)
     own_gains = lax.dynamic_slice_in_dim(small[:16].reshape(2, width), me * depth, depth, 1)
     own_heads = small[16:18, :HDIM] + small[16:18, HDIM:]
     return (
-        layer_out, grad_inputs, columns(last), columns(items[:2]), columns(pairs[:, 0]), columns(pairs[:, 1]),
-        items[2:].reshape(4, 2, r, w).swapaxes(1, 2).reshape(w_down.shape),
-        own_gains[0], own_gains[1], own_heads[0], own_heads[1], small[18, :32].reshape(HEADS, 2),
+        layer_out, grad_inputs, columns(items[26:]), columns(items[16:18]), columns(pairs[:, 0]), columns(pairs[:, 1]),
+        own_down, own_gains[0], own_gains[1], own_heads[0], own_heads[1], small[18, :32].reshape(HEADS, 2),
     )
 
 

time: 531 us -> 493 us (0.928)
  Pallas kernels: 493 us -> 457 us
    pallas_call x1, Pallas kernels: 221 us -> 199 us  [attend(): pl.pallas_call(functools.partial(attend_kernel, ring, n_wide, count), out...]
    pallas_call x4 -> x1, Pallas kernels: 272 us -> 258 us  [train(): pl.pallas_call(functools.partial(train_kernel, ring), out_shape=(shape((r...]
    unnamed x49 -> x29, local copies, waits for them, and re-layouts: 11.9 us -> 8.2 us
where the time goes in v4:
time: 493 us; the launch traced here: 485 us
  Pallas kernels  457 us (93%)
  local copies, waits for them, and re-layouts  18.6 us (4%)
  other arithmetic  8.61 us (2%)
    pallas_call x1, Pallas kernels, train(): pl.pallas_call(functools.partial(train_kernel, ring), out_shape=(shape((r...  258 us
    pallas_call x1, Pallas kernels, attend(): pl.pallas_call(functools.partial(attend_kernel, ring, n_wide, count), out...  199 us

profile of v4, /device:TPU:0, one launch (start us, length us, event | category | flops | bytes accessed | tf_op | source)
XLA Modules:
  0.0 485.1 jit_solution(1794814364564054499)
XLA Ops:
  0.7 0.7 pad_maximum_fusion.1
  1.5 0.8 maximum_bitcast_fusion
  2.3 0.6 pad_maximum_fusion.hg_ref
  2.9 0.7 select_select_fusion.hs_ref
  3.5 0.8 dynamic-slice_convert_fusion
  4.3 0.1 dynamic_update_slice.3
  4.4 0.6 reshape.184.gain_src
  5.0 0.9 reshape.179
  5.9 1.2 reshape.178
  7.1 1.0 copy.47
  8.2 1.0 copy.48
  9.2 1.2 reshape.182
  10.4 1.8 fusion.2
  12.5 2.4 select_convert_fusion
  14.9 198.9 %attend.1 = (bf16[512,1024]{1,0:T(8,128)(2,1)}, f32[2048,256]{1,0:T(8,128)}, bf16[4,2048,128]{2,1,0:T(8,128)(2,1)}, bf16[3072,256]{1,0:T(8,128)(2,1)}, bf16[3072...) custom-call(bf16[512,1024]{1,0:T(8,128)(2,1)} %x.1, ...), custom_call_target="tpu_custom_call" | custom-call | tf_op jit(solution)/shard_map/attend/pallas_call | solution.py:754
  213.8 257.9 %train.1 = (bf16[512,1024]{1,0:T(8,128)(2,1)}, f32[512,1024]{1,0:T(8,128)}, f32[32,32,512]{2,1,0:T(8,128)}, f32[24,128]{1,0:T(8,128)}, f32[512,1024]{1,0:T(8,128...) custom-call(bf16[512,1024]{1,0:T(8,128)(2,1)} %x.1, ...), custom_call_target="tpu_custom_call" | custom-call | tf_op jit(solution)/shard_map/train/pallas_call | solution.py:1205
  471.7 0.8 slice_reduce_fusion
  472.5 0.8 slice_add_fusion
  473.4 0.7 slice.56
  474.2 0.5 slice_bitcast_fusion.6
  474.7 0.5 slice_bitcast_fusion.4
  475.3 0.7 copy.42
  475.9 0.9 slice_bitcast_fusion.3
  476.8 0.7 copy.44
  477.5 1.0 slice_bitcast_fusion.2
  478.5 0.8 copy.43
  479.5 0.4 copy.41
  479.9 0.9 copy.49
  480.9 0.8 copy.46
  481.7 0.8 copy.45
  482.6 1.0 copy.61
  483.5 1.3 copy.62
  (39 shorter events, 0.9 us)
Async XLA Ops:
  0.6 0.7 copy-start
  8.1 4.4 copy-start.6
  8.1 4.4 copy-start.7
  12.5 2.4 copy-start.4
  471.7 7.6 %copy-start.3 = (f32[32,32,512]{2,1,0:T(8,128)S(1)}, f32[32,32,512]{2,1,0:T(8,128)}, u32[]{:S(2)}) copy-start(f32[32,32,512]{2,1,0:T(8,128)} %get-tuple-element.38) | copy-start | bytes 6291460
  480.8 1.8 copy-start.5
  480.9 2.7 copy-start.2
  482.6 2.3 copy-start.1

commit v5 on v4

--- a/solution.py
+++ b/solution.py
@@ -48,12 +48,11 @@
 
 
 class Scatter:
-    def __init__(self, ring, count, pick, buffers, sems, out, write):
-        self.ring, self.count, self.pick = ring, count, pick
-        self.load, self.own, self.b1, self.b2, self.b3 = buffers
+    def __init__(self, ring, count, middle, pick, buffers, sems, write):
+        self.ring, self.count, self.middle, self.pick, self.write = ring, count, middle, pick, write
+        self.load, self.own, self.b1, self.tail = buffers
         self.slots = self.load.shape[0]
         self.load_sem, self.send_sem, self.recv_sem = sems
-        self.out, self.write = out, write
         self.p, self.c, self.h = place()
         self.hy, self.hx = self.h // 2, lax.rem(self.h, 2)
         self.core = (1 - self.p, self.c, self.h)
@@ -65,47 +64,43 @@
             src_ref=src, dst_ref=dst, send_sem=self.send_sem.at[stage, i],
             recv_sem=self.recv_sem.at[stage, i], device_id=device, device_id_type=MESH)
 
+    def wait_for(self, ref, sem):
+        pltpu.make_async_copy(ref, ref, sem).wait()
+
+    def near(self, first_y):
+        return self.ypeer if first_y else self.xpeer
+
+    def spot(self, i, first_y, k):
+        return (i, self.hy, k) if first_y else (i, k, self.hx)
+
     def copy0(self, i, src):
         return self.remote(i, 0, src, self.own.at[i], self.core)
 
     def copy1(self, i, first_y):
-        if first_y:
-            return self.remote(i, 1, self.own.at[i, :, 1 - self.hy], self.b1.at[i], self.ypeer)
-        return self.remote(i, 1, self.own.at[i, :, :, 1 - self.hx], self.b1.at[i], self.xpeer)
-
-    def copy2(self, i, first_y):
-        if first_y:
-            return self.remote(i, 2, self.own.at[i, :, self.hy, 1 - self.hx], self.b2.at[i], self.xpeer)
-        return self.remote(i, 2, self.own.at[i, :, 1 - self.hy, self.hx], self.b2.at[i], self.ypeer)
-
-    def copy3(self, i, step):
-        peer = lax.rem(self.c + step, self.ring)
-        return self.remote(i, 3, self.own.at[i, peer, self.hy, self.hx], self.b3.at[i, step - 1], (self.p, peer, self.h))
-
-    def begin(self, i):
+        src = self.own.at[i, :, 1 - self.hy] if first_y else self.own.at[i, :, :, 1 - self.hx]
+        return self.remote(i, 1, src, self.b1.at[i], self.near(first_y))
+
+    def half(self, i, first_y):
+        return self.own.at[i, :, self.hy, 1 - self.hx] if first_y else self.own.at[i, :, 1 - self.hy, self.hx]
+
+    def begin(self, i, first_y, mid):
         def go(mine, other):
             slot = lax.rem(i, self.slots)
             pltpu.make_async_copy(mine, self.load.at[slot], self.load_sem.at[slot]).start()
             self.copy0(i, other).start()
         self.pick(i, self.p, go)
 
-    def mine(self, i, k):
-        return self.load[lax.rem(i, self.slots), k]
-
-    def landed(self, i):
+    def stage1(self, i, first_y, mid):
         slot = lax.rem(i, self.slots)
-        pltpu.make_async_copy(self.load.at[slot], self.load.at[slot], self.load_sem.at[slot]).wait()
-
-    def stage1(self, i, first_y):
-        self.landed(i)
+        self.wait_for(self.load.at[slot], self.load_sem.at[slot])
         self.copy0(i, self.own.at[i]).wait_recv()
         def add(k, carry):
-            self.own[i, k] = self.own[i, k] + self.mine(i, k)
+            self.own[i, k] = self.own[i, k] + self.load[slot, k]
             return carry
         lax.fori_loop(0, self.ring, add, 0)
         self.copy1(i, first_y).start()
 
-    def stage2(self, i, first_y):
+    def stage2(self, i, first_y, mid):
         self.copy1(i, first_y).wait_recv()
         def add(k, carry):
             for m in range(2):
@@ -113,54 +108,77 @@
                 self.own[at] = self.own[at] + self.b1[i, k, m]
             return carry
         lax.fori_loop(0, self.ring, add, 0)
-        self.copy2(i, first_y).start()
-
-    def stage3(self, i, first_y):
-        self.copy2(i, first_y).wait_recv()
+        if not mid:
+            self.remote(i, 2, self.half(i, first_y), self.tail.at[i, pl.ds(0, self.ring)], self.near(not first_y)).start()
+            return
+        for step in range(1, self.ring):
+            peer = lax.rem(self.c + step, self.ring)
+            src = self.own.at[i, peer, self.hy] if first_y else self.own.at[i, peer, :, self.hx]
+            self.remote(i, 2, src, self.tail.at[i, pl.ds(2 * step - 2, 2)], (self.p, peer, self.h)).start()
+
+    def second(self, i, mid):
+        return self.tail.at[i, pl.ds(0, 2 * self.ring - 2 if mid else self.ring)]
+
+    def third(self, i, mid):
+        return self.tail.at[i, pl.ds(2 * self.ring - 2, 1) if mid else pl.ds(self.ring, self.ring - 1)]
+
+    def stage3(self, i, first_y, mid):
+        self.wait_for(self.second(i, mid), self.recv_sem.at[2, i])
+        if mid:
+            for k in range(2):
+                at = (i, self.c, self.hy, k) if first_y else (i, self.c, k, self.hx)
+                total = self.own[at].astype(jnp.float32)
+                for step in range(1, self.ring):
+                    total = total + self.tail[i, 2 * step - 2 + k].astype(jnp.float32)
+                self.own[at] = total.astype(jnp.bfloat16)
+            last = (self.hy, pl.ds(1 - self.hx, 1)) if first_y else (pl.ds(1 - self.hy, 1), self.hx)
+            self.remote(i, 3, self.own.at[(i, self.c) + last], self.third(i, mid), self.near(not first_y)).start()
+            return
         def add(k, carry):
             at = (i, k, self.hy, self.hx)
-            self.own[at] = self.own[at] + self.b2[i, k]
+            self.own[at] = self.own[at] + self.tail[i, k]
             return carry
         lax.fori_loop(0, self.ring, add, 0)
         for step in range(1, self.ring):
-            self.copy3(i, step).start()
-
-    def finish(self, i):
-        pltpu.make_async_copy(self.b3.at[i], self.b3.at[i], self.recv_sem.at[3, i]).wait()
+            peer = lax.rem(self.c + step, self.ring)
+            self.remote(i, 3, self.own.at[i, peer, self.hy, self.hx], self.tail.at[i, self.ring + step - 1], (self.p, peer, self.h)).start()
+
+    def finish(self, i, first_y, mid):
+        self.wait_for(self.third(i, mid), self.recv_sem.at[3, i])
         total = self.own[i, self.c, self.hy, self.hx].astype(jnp.float32)
-        for step in range(1, self.ring):
-            total = total + self.b3[i, step - 1].astype(jnp.float32)
+        for n in range(2 * self.ring - 2 if mid else self.ring, 2 * self.ring - 1):
+            total = total + self.tail[i, n].astype(jnp.float32)
         self.write(i, total)
 
-    def drain(self, i, first_y):
+    def drain(self, i, first_y, mid):
         self.copy0(i, self.own.at[i]).wait_send()
         self.copy1(i, first_y).wait_send()
-        self.copy2(i, first_y).wait_send()
-        pltpu.make_async_copy(self.b3.at[i], self.b3.at[i], self.send_sem.at[3, i]).wait()
-
-    def step(self, t, ahead=3, lags=(0, 2, 4, 6)):
-        pairs = (self.count + 1) // 2
-        def both(pair, act):
-            for first_y in (True, False):
-                i = 2 * pair + (0 if first_y else 1)
-                guard = (pair >= 0) & (i < self.count) & (i >= 0)
-                pl.when(guard)(functools.partial(act, i, first_y))
-        both(t, lambda i, f: self.begin(i))
-        both(t - ahead - lags[0], self.stage1)
-        both(t - ahead - lags[1], self.stage2)
-        both(t - ahead - lags[2], self.stage3)
-        both(t - ahead - lags[3], lambda i, f: self.finish(i))
-
-    def steps(self, ahead=3, lags=(0, 2, 4, 6)):
+        self.wait_for(self.second(i, mid), self.send_sem.at[2, i])
+        self.wait_for(self.third(i, mid), self.send_sem.at[3, i])
+
+    def both(self, pair, act):
+        middle = self.middle(pair)
+        for first_y in (True, False):
+            i = 2 * pair + (0 if first_y else 1)
+            there = (pair >= 0) & (i < self.count)
+            pl.when(there & middle)(functools.partial(act, i, first_y, True))
+            pl.when(there & jnp.logical_not(middle))(functools.partial(act, i, first_y, False))
+
+    def step(self, t, ahead=1, lags=(0, 1, 2, 3)):
+        self.both(t, self.begin)
+        self.both(t - ahead - lags[0], self.stage1)
+        self.both(t - ahead - lags[1], self.stage2)
+        self.both(t - ahead - lags[2], self.stage3)
+        self.both(t - ahead - lags[3], self.finish)
+
+    def steps(self, ahead=1, lags=(0, 1, 2, 3)):
         return (self.count + 1) // 2 + ahead + lags[3]
 
-    def drain_all(self):
+    def drain_all(self, first=0, last=None):
         def one(t, carry):
-            for first_y in (True, False):
-                i = 2 * t + (0 if first_y else 1)
-                pl.when(i < self.count)(functools.partial(self.drain, i, first_y))
+            self.both(t, self.drain)
             return carry
-        lax.fori_loop(0, (self.count + 1) // 2, one, 0)
+        lax.fori_loop(first, (self.count + 1) // 2 if last is None else last, one, 0)
 
 
 def scatter_scratch(ring, count, rows, cols):
@@ -169,8 +187,7 @@
         pltpu.VMEM((4, ring, 2, 2, rows, cols), bf),
         pltpu.VMEM((count, ring, 2, 2, rows, cols), bf),
         pltpu.VMEM((count, ring, 2, rows, cols), bf),
-        pltpu.VMEM((count, ring, rows, cols), bf),
-        pltpu.VMEM((count, ring - 1, rows, cols), bf),
+        pltpu.VMEM((count, 2 * ring - 1, rows, cols), bf),
         pltpu.SemaphoreType.DMA((4,)),
         pltpu.SemaphoreType.DMA((4, count)),
         pltpu.SemaphoreType.DMA((4, count)),
@@ -780,7 +797,9 @@
 
 
 BACK_LAGS = (1, (0, 1, 2, 3))
-BACK_EVERY = 1
+BACK_EVERY = 8
+LATE = 12
+IN_UNPROJECT = 2
 
 
 def down_blocks(value, shape):
@@ -909,7 +928,7 @@
         copy.wait()
 
 
-def score_phase(work, first_step, ring, d_tok, kx_hbm, vx_hbm, kf_ref, qf_ref, qa_hbm, of_hbm, do_loc, rims, back, same, every,
+def score_phase(work, first_step, ring, d_tok, kx_hbm, vx_hbm, kf_ref, qf_ref, qa_hbm, of_hbm, do_loc, rims, back, same, every, between,
                 kx, vx, qa, of, dq_loc, dk_loc, dv_loc, ka, va, kt, dka, dva,
                 load_sem, local_sem, in_send, in_recv, back_send, back_recv, rim_send, rim_recv):
     p, c, h = place()
@@ -990,7 +1009,10 @@
             backward_block(pair, m, qf_ref, qa, do_loc, of, ka, va, kt, dka, dva, dq_loc, same, every)
             return c
         lax.fori_loop(0, blocks // 2, step, 0)
-        pl.when(pair == 1)(lambda: edges_back(0))
+        @pl.when(pair == 1)
+        def _():
+            edges_back(0)
+            between()
         lax.fori_loop(blocks // 2, blocks, step, 0)
         backward_finish(pair, dka, dva, dk_loc, dv_loc)
         for side in range(2):
@@ -1008,8 +1030,7 @@
     def more(t, carry):
         work.step(t, *BACK_LAGS)
         return carry
-    lax.fori_loop(done, max(done, work.steps(*BACK_LAGS)), more, 0)
-    work.drain_all()
+    lax.fori_loop(done, max(done, LATE), more, 0)
 
     part = back.at[:, pl.ds(0, 384)]
     for pair in range(2):
@@ -1027,7 +1048,7 @@
                     rim_copy(ref, side, kind, pair).wait_send()
 
 
-def unproject_phase(work, x_hbm, gain, wide, raw_hbm, cos_ref, sin_ref, hg_ref, dhid_hbm, back, g_qkv, gin_hbm, gattn_ref, ghead_ref,
+def unproject_phase(first, done, work, x_hbm, gain, wide, raw_hbm, cos_ref, sin_ref, hg_ref, dhid_hbm, back, g_qkv, gin_hbm, gattn_ref, ghead_ref,
                     before, x, nrm_t, dnorm, w, raw, stage, dhid, in_sem, w_sem, stage_sem):
     def tile_copies(t, slot):
         copies = [local_copy(wide.at[t], w.at[slot], w_sem.at[slot, 0])]
@@ -1047,7 +1068,6 @@
         nrm_t[:, at] = (u * scale_of(u) * gain).T.astype(BF)
         return carry
     lax.fori_loop(0, 4, normalise, 0)
-    before()
     ghead_ref[...] = jnp.zeros_like(ghead_ref)
     for t in range(6):
         slot = t % 2
@@ -1083,6 +1103,11 @@
         else:
             dnorm[...] += part
         copy.wait()
+        if t < 2:
+            for n in range(IN_UNPROJECT // 2):
+                first.step(done + t * IN_UNPROJECT // 2 + n, *BACK_LAGS)
+        if t == 1:
+            before()
         if t % 2:
             work.step(t // 2, *BACK_LAGS)
     late.wait()
@@ -1110,7 +1135,7 @@
     group, ext = 4 * rows, 4 * rows + 2 * HALF
     r, w = sums.shape[-2:]
     block = (2, ring, 2, 2, r, w)
-    bufs, sems = buffers[:5], buffers[5:]
+    bufs, sems, last_sems = buffers[:4], buffers[4:7], (buffers[4],) + buffers[7:]
     dma = pltpu.SemaphoreType.DMA
     count = 26
 
@@ -1120,8 +1145,8 @@
     def write_last(i, total):
         sums[count + i] = total
 
-    work = Scatter(ring, count, scatter_pick((g_gu, g_go, g_gd), ((16, True), (2, True), (8, False)), w), bufs, sems, sums, write)
-    last = Scatter(ring, 6, scatter_pick((g_qkv,), ((6, True),), w), bufs, sems, sums, write_last)
+    work = Scatter(ring, count, lambda pair: pair < 0, scatter_pick((g_gu, g_go, g_gd), ((16, True), (2, True), (8, False)), w), bufs, sems, write)
+    last = Scatter(ring, 6, lambda pair: pair < 0, scatter_pick((g_qkv,), ((6, True),), w), bufs, last_sems, write_last)
     vm = pltpu.VMEM
     tiles = down.shape[0] // 512
     spots = g_gd.shape[0] * g_gd.shape[1] // tiles
@@ -1130,8 +1155,13 @@
         functools.partial(feed_phase, work, heads, cot, x, gains[1], wide, down, g_gu, g_go, g_gd, out, dhid, d_tok, gffn, back),
         vm((rows, width), F32), vm((rows, width), F32), vm((rows, width), F32), vm((width, rows), BF), vm((2, 2, width, 512), BF), vm((2, 512, width), BF),
         vm((2,) + block, BF), vm((spots,) + g_gd.shape[2:], BF), dma((3,)), dma((2, 3)), dma((3,)), dma((2,)))
+    def between():
+        work.drain_all(0, 3)
+        for peer in peers:
+            pl.semaphore_signal(credit, inc=1, device_id=peer, device_id_type=MESH)
+
     def score(kx_p, vx_p, qa_p, of_p, dq_loc, dk_loc, dv_loc, ka, va, kt, dka, dva, load_sem):
-        score_phase(work, tiles, ring, d_tok, kx, vx, kf, qf, qa, of, do_loc, rims, back, same, every,
+        score_phase(work, tiles, ring, d_tok, kx, vx, kf, qf, qa, of, do_loc, rims, back, same, every, between,
                     kx_p, vx_p, qa_p, of_p, dq_loc, dk_loc, dv_loc, ka, va, kt, dka, dva,
                     load_sem, local_sem, in_send, in_recv, back_send, back_recv, rim_send, rim_recv)
 
@@ -1141,10 +1171,8 @@
         vm((group, 256), BF), vm((ext, 256), BF), vm((ext, 256), BF),
         vm((2, ext, 128), BF), vm((2, ext, 128), BF), vm((2, 128, ext), BF), vm((2, ext, 128), F32), vm((2, ext, 128), F32),
         dma((4,)))
-    for peer in peers:
-        pl.semaphore_signal(credit, inc=1, device_id=peer, device_id_type=MESH)
     pl.run_scoped(
-        functools.partial(unproject_phase, last, x, gains[0], wide, raw, cos_ref, sin_ref, hg_ref, dhid, back, g_qkv, gin, gattn, ghead,
+        functools.partial(unproject_phase, work, max(LATE, tiles + 2 * (group // QB) // BACK_EVERY), last, x, gains[0], wide, raw, cos_ref, sin_ref, hg_ref, dhid, back, g_qkv, gin, gattn, ghead,
                           lambda: pl.semaphore_wait(credit, len(peers))),
         vm((rows, width), BF), vm((width, rows), BF), vm((rows, width), F32), vm((2, width, 512), BF), vm((2, rows, 512), BF),
         vm((2,) + block, BF), vm((rows, width), F32), dma((2,)), dma((2, 2)), dma((2,)))
@@ -1169,7 +1197,9 @@
         return remote(small.at[n], came.at[n], small_send.at[n], small_recv.at[n], hops[n])
 
     hop(0).start()
+    left = max(LATE, tiles + 2 * (group // QB) // BACK_EVERY) + IN_UNPROJECT
     def rest(t, carry):
+        work.step(left + t - 3, *BACK_LAGS)
         last.step(t, *BACK_LAGS)
         for n in range(3):
             @pl.when(t == 3 + n)
@@ -1182,7 +1212,7 @@
                     for step in range(1, ring):
                         remote(small.at[3], far.at[step - 1], small_send.at[3], small_recv.at[3], (p, lax.rem(c + step, ring), h)).start()
         return carry
-    lax.fori_loop(3, last.steps(*BACK_LAGS), rest, 0)
+    lax.fori_loop(3, max(last.steps(*BACK_LAGS), work.steps(*BACK_LAGS) - left + 3), rest, 0)
     local_copy(far, far, small_recv.at[3]).wait()
     total = small[3]
     for step in range(1, ring):
@@ -1191,6 +1221,7 @@
     for n in range(3):
         hop(n).wait_send()
     local_copy(far, far, small_send.at[3]).wait()
+    work.drain_all(3)
     last.drain_all()
 
 
@@ -1216,7 +1247,7 @@
             vm((4, 24, 128), F32), vm((3, 24, 128), F32), vm((ring - 1, 24, 128), F32), dma((4,)), dma((4,)),
             pltpu.SemaphoreType.REGULAR,
             dma((4, 2)), dma((2,)), dma((2,)), dma((3, 2)), dma((3, 2)), dma((2, 2, 2)), dma((2, 2, 2)),
-        ] + scatter_scratch(ring, 26, r, w),
+        ] + scatter_scratch(ring, 26, r, w) + [dma((4, 6)), dma((4, 6))],
         compiler_params=pltpu.CompilerParams(collective_id=collective_id, has_side_effects=True, vmem_limit_bytes=63 * MIB),
         name="train",
     )(x, heads, cot, gains, wide, down, kx, vx, kf, qf, qa, of, raw, cosine, sine, head_gains)

time: 493 us -> 470 us (0.953)
  Pallas kernels: 457 us -> 434 us
    pallas_call x1, Pallas kernels: 258 us -> 235 us  [train(): pl.pallas_call(functools.partial(train_kernel, ring), out_shape=(shape((r...]
where the time goes in v5:
time: 470 us; the launch traced here: 463 us
  Pallas kernels  434 us (92%)
  local copies, waits for them, and re-layouts  18.6 us (4%)
  other arithmetic  8.61 us (2%)
    pallas_call x1, Pallas kernels, train(): pl.pallas_call(functools.partial(train_kernel, ring), out_shape=(shape((r...  235 us
    pallas_call x1, Pallas kernels, attend(): pl.pallas_call(functools.partial(attend_kernel, ring, n_wide, count), out...  199 us

profile of v5, /device:TPU:0, one launch (start us, length us, event | category | flops | bytes accessed | tf_op | source)
XLA Modules:
  0.0 462.8 jit_solution(31279251565308987)
XLA Ops:
  0.7 0.7 pad_maximum_fusion.1
  1.5 0.8 maximum_bitcast_fusion
  2.3 0.6 pad_maximum_fusion.hg_ref
  2.9 0.7 select_select_fusion.hs_ref
  3.5 0.8 dynamic-slice_convert_fusion
  4.3 0.1 dynamic_update_slice.3
  4.4 0.6 reshape.184.gain_src
  5.0 0.9 reshape.179
  5.9 1.2 reshape.178
  7.1 1.0 copy.47
  8.2 1.0 copy.48
  9.2 1.2 reshape.182
  10.4 1.8 fusion.2
  12.5 2.4 select_convert_fusion
  14.9 198.9 %attend.1 = (bf16[512,1024]{1,0:T(8,128)(2,1)}, f32[2048,256]{1,0:T(8,128)}, bf16[4,2048,128]{2,1,0:T(8,128)(2,1)}, bf16[3072,256]{1,0:T(8,128)(2,1)}, bf16[3072...) custom-call(bf16[512,1024]{1,0:T(8,128)(2,1)} %x.1, ...), custom_call_target="tpu_custom_call" | custom-call | tf_op jit(solution)/shard_map/attend/pallas_call | solution.py:771
  213.8 235.3 %train.1 = (bf16[512,1024]{1,0:T(8,128)(2,1)}, f32[512,1024]{1,0:T(8,128)}, f32[32,32,512]{2,1,0:T(8,128)}, f32[24,128]{1,0:T(8,128)}, f32[512,1024]{1,0:T(8,128...) custom-call(bf16[512,1024]{1,0:T(8,128)(2,1)} %x.1, ...), custom_call_target="tpu_custom_call" | custom-call | tf_op jit(solution)/shard_map/train/pallas_call | solution.py:1236
  449.1 0.8 slice_reduce_fusion
  450.0 0.8 slice_add_fusion
  450.8 0.7 slice.56
  451.6 0.5 slice_bitcast_fusion.6
  452.1 0.5 slice_bitcast_fusion.4
  452.7 0.7 copy.42
  453.4 0.9 slice_bitcast_fusion.3
  454.3 0.7 copy.44
  454.9 1.0 slice_bitcast_fusion.2
  456.0 0.8 copy.43
  456.9 0.4 copy.41
  457.3 0.9 copy.49
  458.3 0.8 copy.46
  459.1 0.8 copy.45
  460.0 1.0 copy.61
  461.0 1.3 copy.62
  (39 shorter events, 0.9 us)
Async XLA Ops:
  0.6 0.7 copy-start
  8.1 4.4 copy-start.6
  8.1 4.4 copy-start.7
  12.5 2.4 copy-start.4
  449.1 7.6 %copy-start.3 = (f32[32,32,512]{2,1,0:T(8,128)S(1)}, f32[32,32,512]{2,1,0:T(8,128)}, u32[]{:S(2)}) copy-start(f32[32,32,512]{2,1,0:T(8,128)} %get-tuple-element.38) | copy-start | bytes 6291460
  458.2 1.8 copy-start.5
  458.3 2.7 copy-start.2
  460.0 2.3 copy-start.1

commit v6 on v5

--- a/solution.py
+++ b/solution.py
@@ -238,7 +238,7 @@
             for step in range(1, self.ring):
                 peer = (self.p, lax.rem(self.c + step, self.ring), self.h)
                 self.remote(i, 0, src, mine, peer).start()
-        self.pick(i, go)
+        self.pick(i, go, True)
 
     def near(self, first_x):
         return self.xpeer if first_x else self.ypeer
@@ -257,7 +257,7 @@
     def stage1(self, i, first_x, mid):
         def go(src, out):
             mine = out(self.p, self.c, self.hy, self.hx)
-            pltpu.make_async_copy(src, mine, self.local_sem.at[i]).wait()
+            self.wait_for(mine, self.local_sem.at[i])
             if mid:
                 self.same(i, 0, self.block(out, first_x, False), self.core).wait_recv()
                 both = self.couple(out, first_x, self.c)
@@ -351,17 +351,31 @@
     ]
 
 
-def gather_pick(src, wide, down, n_wide):
-    cols = src.shape[-1]
-    def pick(i, go):
-        @pl.when(i < n_wide)
-        def _():
-            go(src.at[i], lambda p, c, y, x: wide.at[i, p, c, y, x])
+def gather_pick(srcs, wide, down, n_wide, cols):
+    def pick(i, go, source=False):
+        def in_wide(src):
+            go(src, lambda p, c, y, x: wide.at[i, p, c, y, x])
+        def in_down(src):
+            j = i - n_wide
+            at = pl.ds(pl.multiple_of(lax.rem(j, 2) * cols, cols), cols)
+            go(src, lambda p, c, y, x: down.at[p, c, y, x, j // 2, :, at])
+        if len(srcs) == 1 or not source:
+            pl.when(i < n_wide)(lambda: in_wide(srcs[0].at[i] if source else None))
+            pl.when(i >= n_wide)(lambda: in_down(srcs[0].at[i] if source else None))
+            return
+        start = 0
+        for ref in srcs[:-1]:
+            n = ref.shape[1] // cols
+            @pl.when((i >= start) & (i < start + n))
+            def _():
+                in_wide(ref.at[:, pl.ds(pl.multiple_of((i - start) * cols, cols), cols)])
+            start += n
         @pl.when(i >= n_wide)
         def _():
             j = i - n_wide
-            at = pl.ds(pl.multiple_of(lax.rem(j, 2) * cols, cols), cols)
-            go(src.at[i], lambda p, c, y, x: down.at[p, c, y, x, j // 2, :, at])
+            rows = srcs[-1].shape[0] // 4
+            at = pl.ds(pl.multiple_of(j // 2 * rows, rows), rows)
+            in_down(srcs[-1].at[at, pl.ds(pl.multiple_of(lax.rem(j, 2) * cols, cols), cols)])
     return pick
 
 
@@ -594,10 +608,10 @@
     return jnp.concatenate(parts, axis=2).reshape(-1, 512).astype(BF)
 
 
-def attend_kernel(ring, n_wide, count, x_ref, cos_ref, sin_ref, hg_ref, kf_own, qf_ref, hs_ref, src, gain_src,
-                  tok_ref, of_ref, qa_ref, kx, vx, kf_ref, raw_ref, gain_ref, wide, down,
+def attend_kernel(ring, n_wide, count, n_src, x_ref, cos_ref, sin_ref, hg_ref, kf_own, qf_ref, hs_ref, gain_src, *refs):
+    (tok_ref, of_ref, qa_ref, kx, vx, kf_ref, raw_ref, gain_ref, wide, down,
                   rot, nrm, w_tile, gains, q_loc, o_loc, ka, va, tile_sem, local_sem, a2a_send, a2a_recv, rim_send, rim_recv,
-                  kf_send, kf_recv, out_send, out_recv, *sems):
+                  kf_send, kf_recv, out_send, out_recv, *sems) = refs[n_src:]
     p, c, h = place()
     rim = Rim(ring)
     greet(group_peers(ring) + [(p, c, 3 - h)])
@@ -609,8 +623,8 @@
     three = pl.ds(0, 3 * rows)
     sides = ((rim.has_high, rim.high, group, 0), (rim.has_low, rim.low, HALF, HALF + group))
 
-    small = Gather(ring, 1, lambda i, go: go(gain_src, lambda p, c, y, x: gains.at[p, c, y, x]), sems[:3])
-    work = Gather(ring, count, gather_pick(src, wide, down, n_wide), sems[3:])
+    small = Gather(ring, 1, lambda i, go, source=False: go(gain_src, lambda p, c, y, x: gains.at[p, c, y, x]), sems[:3])
+    work = Gather(ring, count, gather_pick(refs[:n_src], wide, down, n_wide, wide.shape[-1]), sems[3:])
 
     def kf_copy(side):
         there, block, first, to = sides[side]
@@ -762,14 +776,14 @@
     work.drain_all()
 
 
-def attend(x, cosine, sine, head_gains, kf, qf, hs, src, gain_src, n_wide, ring, collective_id):
+def attend(x, cosine, sine, head_gains, kf, qf, hs, srcs, gain_src, item, n_wide, count, ring, collective_id):
     rows, width = x.shape
     group = 4 * rows
     ext = group + 2 * HALF
-    count, r, w = src.shape
+    r, w = item
     dma = pltpu.SemaphoreType.DMA
     return pl.pallas_call(
-        functools.partial(attend_kernel, ring, n_wide, count),
+        functools.partial(attend_kernel, ring, n_wide, count, len(srcs)),
         out_shape=(
             jax.ShapeDtypeStruct((rows, width), BF),
             jax.ShapeDtypeStruct((group, 256), F32),
@@ -782,7 +796,7 @@
             jax.ShapeDtypeStruct((n_wide, 2, ring, 2, 2, r, w), BF),
             jax.ShapeDtypeStruct((2, ring, 2, 2, (count - n_wide) // 2, r, 2 * w), BF),
         ),
-        in_specs=[VM] * 7 + [ANY, ANY],
+        in_specs=[VM] * 7 + [ANY] * (1 + len(srcs)),
         out_specs=(VM,) * 8 + (ANY, ANY),
         scratch_shapes=[
             pltpu.VMEM((rows, 3 * width), BF), pltpu.VMEM((rows, width), BF), pltpu.VMEM((2, 2, ring, 2, 2, r, w), BF),
@@ -793,7 +807,7 @@
         ] + gather_sems(1) + gather_sems(count),
         compiler_params=pltpu.CompilerParams(collective_id=collective_id, has_side_effects=True, vmem_limit_bytes=60 * MIB),
         name="attend",
-    )(x, cosine, sine, head_gains, kf, qf, hs, src, gain_src)
+    )(x, cosine, sine, head_gains, kf, qf, hs, gain_src, *srcs)
 
 
 BACK_LAGS = (1, (0, 1, 2, 3))
@@ -870,6 +884,11 @@
         gate = dot(normed, wg)
         up = dot(normed, wu)
         d_product = dot_tb(cot[...], wd)
+        @pl.when(t > 0)
+        def _():
+            for copy in staged(t - 1):
+                copy.wait()
+            work.step(t - 1, *BACK_LAGS)
         sig = jax.nn.sigmoid(gate)
         silu = gate * sig
         product = silu * up
@@ -878,11 +897,6 @@
         d_up = (d_product * silu).astype(BF)
         acc[...] += dot(prod_b, wd)
         dnorm[...] += dot_tb(d_gate, wg) + dot_tb(d_up, wu)
-        @pl.when(t > 0)
-        def _():
-            for copy in staged(t - 1):
-                copy.wait()
-            work.step(t - 1, *BACK_LAGS)
         stage[0] = as_blocks(dot(nrm_t[...], d_gate), stage.shape[1:])
         stage[1] = as_blocks(dot(nrm_t[...], d_up), stage.shape[1:])
         stage_d[...] = down_blocks(dot(product.T.astype(BF), cot[...]), stage_d.shape)
@@ -906,6 +920,7 @@
         cot[at, :] = acc[at, :].astype(BF)
         return carry + terms
     gffn_ref[...] = lax.fori_loop(0, 4, finish, jnp.zeros(gffn_ref.shape, F32))
+    work.step(tiles, *BACK_LAGS)
     last = [local_copy(cot, out_hbm, out_sem.at[0]), local_copy(hidden, dhid_hbm, out_sem.at[1])]
     for copy in last:
         copy.start()
@@ -1145,7 +1160,7 @@
     def write_last(i, total):
         sums[count + i] = total
 
-    work = Scatter(ring, count, lambda pair: pair < 0, scatter_pick((g_gu, g_go, g_gd), ((16, True), (2, True), (8, False)), w), bufs, sems, write)
+    work = Scatter(ring, count, lambda pair: pair < 0, scatter_pick((g_gu, g_gd, g_go), ((16, True), (8, False), (2, True)), w), bufs, sems, write)
     last = Scatter(ring, 6, lambda pair: pair < 0, scatter_pick((g_qkv,), ((6, True),), w), bufs, last_sems, write_last)
     vm = pltpu.VMEM
     tiles = down.shape[0] // 512
@@ -1161,7 +1176,7 @@
             pl.semaphore_signal(credit, inc=1, device_id=peer, device_id_type=MESH)
 
     def score(kx_p, vx_p, qa_p, of_p, dq_loc, dk_loc, dv_loc, ka, va, kt, dka, dva, load_sem):
-        score_phase(work, tiles, ring, d_tok, kx, vx, kf, qf, qa, of, do_loc, rims, back, same, every, between,
+        score_phase(work, tiles + 1, ring, d_tok, kx, vx, kf, qf, qa, of, do_loc, rims, back, same, every, between,
                     kx_p, vx_p, qa_p, of_p, dq_loc, dk_loc, dv_loc, ka, va, kt, dka, dva,
                     load_sem, local_sem, in_send, in_recv, back_send, back_recv, rim_send, rim_recv)
 
@@ -1172,7 +1187,7 @@
         vm((2, ext, 128), BF), vm((2, ext, 128), BF), vm((2, 128, ext), BF), vm((2, ext, 128), F32), vm((2, ext, 128), F32),
         dma((4,)))
     pl.run_scoped(
-        functools.partial(unproject_phase, work, max(LATE, tiles + 2 * (group // QB) // BACK_EVERY), last, x, gains[0], wide, raw, cos_ref, sin_ref, hg_ref, dhid, back, g_qkv, gin, gattn, ghead,
+        functools.partial(unproject_phase, work, max(LATE, tiles + 1 + 2 * (group // QB) // BACK_EVERY), last, x, gains[0], wide, raw, cos_ref, sin_ref, hg_ref, dhid, back, g_qkv, gin, gattn, ghead,
                           lambda: pl.semaphore_wait(credit, len(peers))),
         vm((rows, width), BF), vm((width, rows), BF), vm((rows, width), F32), vm((2, width, 512), BF), vm((2, rows, 512), BF),
         vm((2,) + block, BF), vm((rows, width), F32), dma((2,)), dma((2, 2)), dma((2,)))
@@ -1197,7 +1212,7 @@
         return remote(small.at[n], came.at[n], small_send.at[n], small_recv.at[n], hops[n])
 
     hop(0).start()
-    left = max(LATE, tiles + 2 * (group // QB) // BACK_EVERY) + IN_UNPROJECT
+    left = max(LATE, tiles + 1 + 2 * (group // QB) // BACK_EVERY) + IN_UNPROJECT
     def rest(t, carry):
         work.step(left + t - 3, *BACK_LAGS)
         last.step(t, *BACK_LAGS)
@@ -1274,8 +1289,10 @@
     r, w = item_shape(depth)
 
     me = (lax.axis_index("pack") * ring + lax.axis_index("cp")) * 4 + head
-    down_pieces = w_down.reshape(4, r, 2, w).swapaxes(1, 2).reshape(8, r, w)
-    src = jnp.concatenate([to_blocks(weight, depth, r, w)[:, 0] for weight in (w_qkv, w_out, w_gate, w_up)] + [down_pieces])
+    srcs = (w_qkv, w_out, w_gate, w_up, w_down)
+    if r != depth:
+        down_pieces = w_down.reshape(4, r, 2, w).swapaxes(1, 2).reshape(8, r, w)
+        srcs = (jnp.concatenate([to_blocks(weight, depth, r, w)[:, 0] for weight in srcs[:4]] + [down_pieces]),)
     gain_src = lax.dynamic_update_slice(jnp.zeros((2, width), BF), jnp.stack([gain_attn, gain_ffn]), (0, me * depth))
     gain_src = gain_src.reshape(16, 128)
 
@@ -1291,7 +1308,7 @@
     hs = head_scales(lax.dynamic_slice_in_dim(head_bias, head * 4, 4, 0))
 
     heads_out, of, qa, kx, vx, kf, raw, gains, wide, down = attend(
-        inputs, cosine, sine, head_gains, kf_own, qf, hs, src, gain_src, 24, ring, 1)
+        inputs, cosine, sine, head_gains, kf_own, qf, hs, srcs, gain_src, (r, w), 24, 32, ring, 1)
     wide = from_blocks(wide, depth)
     gains = gains.reshape(2, 1, width)
     layer_out, grad_inputs, items, small, *_ = train(
@@ -1303,11 +1320,11 @@
 
     pairs = items[:16].reshape(8, 2, r, w)
     down_depth = w_down.shape[0] // 4
-    own_down = items[18:26].reshape(4, 2, r // down_depth, down_depth, w).transpose(0, 3, 2, 1, 4).reshape(w_down.shape)
+    own_down = items[16:24].reshape(4, 2, r // down_depth, down_depth, w).transpose(0, 3, 2, 1, 4).reshape(w_down.shape)
     own_gains = lax.dynamic_slice_in_dim(small[:16].reshape(2, width), me * depth, depth, 1)
     own_heads = small[16:18, :HDIM] + small[16:18, HDIM:]
     return (
-        layer_out, grad_inputs, columns(items[26:]), columns(items[16:18]), columns(pairs[:, 0]), columns(pairs[:, 1]),
+        layer_out, grad_inputs, columns(items[26:]), columns(items[24:26]), columns(pairs[:, 0]), columns(pairs[:, 1]),
         own_down, own_gains[0], own_gains[1], own_heads[0], own_heads[1], small[18, :32].reshape(HEADS, 2),
     )
 

time: 470 us -> 462 us (0.983)
  local copies, waits for them, and re-layouts: 18.6 us -> 13.1 us
where the time goes in v6:
time: 462 us; the launch traced here: 455 us
  Pallas kernels  431 us (93%)
  local copies, waits for them, and re-layouts  13.1 us (3%)
  other arithmetic  9.21 us (2%)
    pallas_call x1, Pallas kernels, train(): pl.pallas_call(functools.partial(train_kernel, ring), out_shape=(shape((r...  232 us
    pallas_call x1, Pallas kernels, attend(): pl.pallas_call(functools.partial(attend_kernel, ring, n_wide, count, len(...  199 us

profile of v6, /device:TPU:0, one launch (start us, length us, event | category | flops | bytes accessed | tf_op | source)
XLA Modules:
  0.0 454.9 jit_solution(2449595104979670515)
XLA Ops:
  0.7 0.7 pad_maximum_fusion.1
  1.4 0.1 constant_dynamic-slice_fusion.1
  1.5 0.8 maximum_bitcast_fusion
  2.3 0.6 pad_maximum_fusion.hg_ref
  2.9 0.7 select_select_fusion.hs_ref
  3.5 0.8 dynamic-slice_convert_fusion
  4.3 0.1 dynamic_update_slice.3
  4.4 0.6 reshape.160.gain_src
  5.0 1.8 fusion.2
  6.8 3.0 select_convert_fusion
  9.9 199.0 %attend.1 = (bf16[512,1024]{1,0:T(8,128)(2,1)}, f32[2048,256]{1,0:T(8,128)}, bf16[4,2048,128]{2,1,0:T(8,128)(2,1)}, bf16[3072,256]{1,0:T(8,128)(2,1)}, bf16[3072...) custom-call(bf16[512,1024]{1,0:T(8,128)(2,1)} %x.1, ...), custom_call_target="tpu_custom_call" | custom-call | tf_op jit(solution)/shard_map/attend/pallas_call | solution.py:785
  208.9 232.4 %train.1 = (bf16[512,1024]{1,0:T(8,128)(2,1)}, f32[512,1024]{1,0:T(8,128)}, f32[32,32,512]{2,1,0:T(8,128)}, f32[24,128]{1,0:T(8,128)}, f32[512,1024]{1,0:T(8,128...) custom-call(bf16[512,1024]{1,0:T(8,128)(2,1)} %x.1, ...), custom_call_target="tpu_custom_call" | custom-call | tf_op jit(solution)/shard_map/train/pallas_call | solution.py:1251
  441.4 0.8 slice_reduce_fusion
  442.2 0.8 slice_add_fusion
  443.0 0.7 slice.56
  443.7 0.1 constant_dynamic-slice_fusion
  443.8 0.5 slice_bitcast_fusion.6
  444.3 0.5 slice_bitcast_fusion.4
  444.9 0.1 reshape_squeeze.3
  444.9 0.7 copy.36
  445.6 0.9 slice_bitcast_fusion.3
  446.5 0.7 copy.38
  447.2 1.0 slice_bitcast_fusion.2
  448.2 0.8 copy.37
  449.0 0.1 slice.52
  449.1 0.4 copy.35
  449.5 0.9 copy.41
  450.4 0.1 slice_bitcast_fusion
  450.5 0.8 copy.40
  451.4 0.8 copy.39
  452.2 1.0 copy.45
  453.2 1.3 copy.46
  (22 shorter events, 0.1 us)
Async XLA Ops:
  0.6 0.7 copy-start
  441.3 7.6 %copy-start.3 = (f32[32,32,512]{2,1,0:T(8,128)S(1)}, f32[32,32,512]{2,1,0:T(8,128)}, u32[]{:S(2)}) copy-start(f32[32,32,512]{2,1,0:T(8,128)} %get-tuple-element.38) | copy-start | bytes 6291460
  450.4 1.8 copy-start.4
  450.5 2.7 copy-start.2
  452.2 2.3 copy-start.1
